TPU v7x, 512 devices: a whole 4x4x16 slice. The times are simulated.
512 devices in a mesh: elem: 32 (over z, core), mode: 16 (over y, x).
Axes of the slice: x: 4, y: 4, z: 16, core: 2. Of those that a mesh axis runs over, the one named last changes fastest.
Arguments:
- adjoint: float32 [3, 256, 49, 4096], P(None, 'mode', None, 'elem'), may hold values from -2 to 2
- base_flow: float32 [3, 256, 49, 4096], P(None, 'mode', None, 'elem'), may hold values from -2 to 2
- metric: float32 [4, 49, 4096], P(None, None, 'elem'), may hold values from -1 to 1
- penalty: float32 [4, 7, 4096], P(None, None, 'elem'), may hold values from 0.5 to 4
- send_sides: int32 [32, 4, 32], P('elem'), may hold values from 0 to 512, as said below
- ext_index: int32 [4, 4096], P(None, 'elem'), may hold values from 0 to 640, as said below
Outputs:
- advect: float32 [3, 256, 49, 4096], P(None, 'mode', None, 'elem')
Inputs may be any that keep to these rules, and one draw needn't show every extreme that they name: `send_sides`: entry [p, d, k] is a local side index s * 128 + e of partition p, sent in slot k of block d to partition p + o_d modulo 32 with o = (1, -1, 2, -2); the value 4 * 128 marks an empty slot. No side is sent twice. In every draw some partition fills all 32 slots of some block. `ext_index`: for side s of element e of partition p: a value below 512 is a local side of p; 512 + d * 32 + k is slot k of block d arriving from partition p - o_d; 640 means no neighbour. Pairings are mutual, and every sent side is read by its partner.
All inputs are finite; a program needn't handle non-finite values.
Results may differ from a plain program's by a relative error of at most 0.000098.
Values sent between devices are 32-bit elements; how exact they have to be, the bound alone decides.
No kernel may reach another device: no remote copies, remote signals or barrier semaphores. Data moves between devices by JAX's collectives and lax.ppermute only.
A program may use at most 128 MiB of HBM per device.

v0:
```python
import math

import jax
import jax.numpy as jnp
import numpy as np
from jax import lax
from jax.experimental import pallas as pl
from jax.experimental.pallas import tpu as pltpu
from jax.sharding import PartitionSpec as P

MODES = 256
POINTS = 7
QUAD = 49
GROUPS = 16
NEAR = 8
ROWS = 6 * QUAD
FIELD_TILES = 37
BACK_ROWS = 3 * QUAD
BACK_TILES = 19
SLOTS = 32
OFFSETS = (1, -1, 2, -2)
TRACE_ROWS = 3 * POINTS * GROUPS
TRACE_LANES = 384
VMEM_LIMIT = 56 * 1024 * 1024


def legendre_pair(degree, position):
    previous = 1.0
    current = position
    for order_index in range(2, degree + 1):
        following = (
            (2 * order_index - 1) * position * current - (order_index - 1) * previous
        ) / order_index
        previous = current
        current = following
    return (current, previous)


def lobatto_points(degree):
    node_list = []
    for point_index in range(degree + 1):
        estimate = -math.cos(math.pi * point_index / degree)
        for newton_step in range(60):
            current, previous = legendre_pair(degree, estimate)
            estimate = estimate - (estimate * current - previous) / ((degree + 1) * current)
        node_list.append(estimate)
    node_list[0] = -1.0
    node_list[degree] = 1.0
    return node_list


def lobatto_matrix(degree):
    nodes = lobatto_points(degree)
    at_nodes = [legendre_pair(degree, value)[0] for value in nodes]
    count = degree + 1
    matrix = np.zeros((count, count))
    for row in range(count):
        for col in range(count):
            if row != col:
                matrix[row, col] = at_nodes[row] / (at_nodes[col] * (nodes[row] - nodes[col]))
    matrix[0, 0] = -degree * (degree + 1) / 4.0
    matrix[degree, degree] = degree * (degree + 1) / 4.0
    return matrix


def fourier_tables():
    planes = np.arange(MODES)[:, None]
    slot = np.arange(MODES)[None, :]
    wavenumber = slot // 2
    angles = (wavenumber * planes % MODES) * (2.0 * math.pi / MODES)
    synthesis = np.where(slot % 2 == 1, -np.sin(angles), np.cos(angles))
    synthesis = np.where(slot == 1, np.where(planes % 2 == 0, 1.0, -1.0), synthesis)
    weights = np.where(slot < 2, 1.0, 2.0) / MODES
    analysis = (synthesis * weights).T
    rates = wavenumber * (4.0 / MODES)
    slope = np.zeros((MODES, MODES))
    slope[:, 0::2] = rates[:, 0::2] * synthesis[:, 1::2]
    slope[:, 1::2] = -rates[:, 0::2] * synthesis[:, 0::2]
    return synthesis, analysis, slope


def halves(table):
    table = table.astype(np.float32)
    high = table.astype(jnp.bfloat16)
    low = (table - high.astype(np.float32)).astype(jnp.bfloat16)
    return high, low


def rim_point(side, step):
    last = POINTS - 1
    return (step, POINTS * step + last, POINTS * last + last - step, POINTS * (last - step))[side]


def swap_blocks(tiles, masks):
    turned = [pltpu.roll(tile, 16 * q, 1) if q else tile for q, tile in enumerate(tiles)]
    moved = [turned[-k % 8] for k in range(8)]
    for bit in range(3):
        moved = [jnp.where(masks[bit], moved[(k - (1 << bit)) % 8], moved[k]) for k in range(8)]
    return [pltpu.roll(tile, 128 - 16 * g, 1) if g else tile for g, tile in enumerate(moved)]


def block_masks():
    block = lax.broadcasted_iota(jnp.int32, (8, 128), 1) // 16
    return [(block & (1 << bit)) != 0 for bit in range(3)]


def split_two(value):
    high = value.astype(jnp.bfloat16)
    low = (value - high.astype(jnp.float32)).astype(jnp.bfloat16)
    return high, low


def split_three(value):
    high = value.astype(jnp.bfloat16)
    rest = value - high.astype(jnp.float32)
    middle = rest.astype(jnp.bfloat16)
    low = (rest - middle.astype(jnp.float32)).astype(jnp.bfloat16)
    return high, middle, low


def dot(left, right):
    return jnp.dot(left, right, preferred_element_type=jnp.float32)


def pack_kernel(adjoint_ref, base_ref, out_ref):
    def put(tile, block):
        out_ref[:, tile] = block.reshape(128, 128).T.reshape(GROUPS, NEAR, 128)

    for tile in range(FIELD_TILES):
        first, end = 8 * tile, min(8 * tile + 8, ROWS)
        parts = []
        if first < BACK_ROWS:
            parts.append(adjoint_ref[first : min(end, BACK_ROWS)])
        if end > BACK_ROWS:
            parts.append(base_ref[max(first, BACK_ROWS) - BACK_ROWS : end - BACK_ROWS])
        if 8 * tile + 8 > end:
            parts.append(base_ref[: 8 * tile + 8 - end])
        put(tile, parts[0] if len(parts) == 1 else jnp.concatenate(parts, axis=0))


def derive_line(values, odd_table, even_table, centre):
    sums = [values[k] + values[6 - k] for k in range(3)]
    differences = [values[k] - values[6 - k] for k in range(3)]
    even = [
        sum(float(odd_table[i, j]) * differences[j] for j in range(1, 3))
        + float(odd_table[i, 0]) * differences[0]
        for i in range(4)
    ]
    odd = [
        (float(even_table[i, 0]) * sums[0] + float(even_table[i, 1]) * sums[1])
        + (float(even_table[i, 2]) * sums[2] + float(centre[i]) * values[3])
        for i in range(3)
    ]
    return (
        [even[i] + odd[i] for i in range(3)]
        + [even[3]]
        + [even[i] - odd[i] for i in (2, 1, 0)]
    )


def main_kernel(
    in_ref,
    metric_ref,
    synth_high_ref,
    synth_low_ref,
    back_high_ref,
    back_low_ref,
    out_ref,
    high,
    low,
    plane,
    first,
    second,
    product,
    coefficient,
):
    masks = block_masks()

    @pl.loop(0, FIELD_TILES)
    def _(tile):
        rows = pl.ds(pl.multiple_of(tile * 64, 64), 64)
        for half in range(2):
            swapped = swap_blocks([in_ref[8 * half + k, tile] for k in range(8)], masks)
            upper, lower = split_two(jnp.concatenate(swapped, axis=0))
            high[rows, pl.ds(128 * half, 128)] = upper
            low[rows, pl.ds(128 * half, 128)] = lower

    block = FIELD_TILES * 16

    @pl.loop(0, 4)
    def _(step):
        rows = pl.ds(pl.multiple_of(step * block, 16), block)
        upper = high[rows, :]
        plane[rows, :] = (
            dot(upper, synth_high_ref[...])
            + dot(low[rows, :], synth_high_ref[...])
            + dot(upper, synth_low_ref[...])
        )

    matrix = lobatto_matrix(POINTS - 1)
    mirrored = matrix[:, ::-1]
    odd_table = (matrix - mirrored)[:4, :3] / 2.0
    even_table = (matrix + mirrored)[:3, :3] / 2.0
    centre = matrix[:3, 3]

    @pl.loop(0, 6)
    def _(field):
        def at(point):
            return pl.ds(pl.multiple_of(field * (QUAD * 8) + point * 8, 8), 8)

        for half in range(2):
            lanes = pl.ds(128 * half, 128)
            for line in range(POINTS):
                for stride, base, target in ((1, 7 * line, first), (7, line, second)):
                    values = [plane[at(base + stride * k), lanes] for k in range(POINTS)]
                    for k, slope in enumerate(derive_line(values, odd_table, even_table, centre)):
                        target[at(base + stride * k), lanes] = slope

    @pl.loop(0, QUAD)
    def _(point):
        east_first, north_first, east_second, north_second = (metric_ref[k, point] for k in range(4))

        def at(field):
            return pl.ds(pl.multiple_of(field * (QUAD * 8) + point * 8, 8), 8)

        for half in range(2):
            lanes = pl.ds(128 * half, 128)
            span = pl.ds(MODES + 128 * half, 128)
            speed = [plane[at(k), lanes] for k in range(3)]
            base = [plane[at(3 + k), lanes] for k in range(3)]
            along = sum(speed[k] * first[at(3 + k), lanes] for k in range(3))
            across = sum(speed[k] * second[at(3 + k), lanes] for k in range(3))
            turned = (
                east_first * along + east_second * across,
                north_first * along + north_second * across,
                sum(speed[k] * plane[at(3 + k), span] for k in range(3)),
            )
            flow_first = base[0] * east_first + base[1] * north_first
            flow_second = base[0] * east_second + base[1] * north_second
            for k in range(3):
                carried = (
                    flow_first * first[at(k), lanes]
                    + flow_second * second[at(k), lanes]
                    + base[2] * plane[at(k), span]
                )
                product[at(k), lanes] = turned[k] - carried

    product[BACK_ROWS * 8 :, :] = jnp.zeros((BACK_TILES * 64 - BACK_ROWS * 8, MODES), jnp.float32)
    back_block = BACK_TILES * 32

    @pl.loop(0, 2)
    def _(step):
        rows = pl.ds(pl.multiple_of(step * back_block, 32), back_block)
        upper, lower = split_two(product[rows, :])
        coefficient[rows, :] = (
            dot(upper, back_high_ref[...])
            + dot(lower, back_high_ref[...])
            + dot(upper, back_low_ref[...])
        )

    @pl.loop(0, BACK_TILES)
    def _(tile):
        for half in range(2):
            lanes = pl.ds(128 * half, 128)
            pieces = [
                coefficient[pl.ds(pl.multiple_of(tile * 64 + 8 * k, 8), 8), lanes] for k in range(8)
            ]
            for k, swapped in enumerate(swap_blocks(pieces, masks)):
                out_ref[8 * half + k, tile] = swapped


def traces_of(adjoint_ref):
    return jnp.concatenate(
        [
            jnp.concatenate(
                [adjoint_ref[component * QUAD + rim_point(side, step)] for side in range(4)], axis=1
            )
            for component in range(3)
            for step in range(POINTS)
        ],
        axis=0,
    )


def send_kernel(adjoint_ref, sides_ref, *out_refs):
    traces = traces_of(adjoint_ref)
    chosen = lax.broadcasted_iota(jnp.int32, (512, 4 * SLOTS), 0) == sides_ref[...]
    chosen = jnp.where(chosen, 1.0, 0.0).astype(jnp.bfloat16)
    outgoing = sum(dot(part, chosen) for part in split_three(traces))
    padding = jnp.zeros((TRACE_LANES - TRACE_ROWS, 128), jnp.float32)
    outgoing = jnp.concatenate([outgoing, padding], axis=0).T
    for direction, out_ref in enumerate(out_refs):
        out_ref[...] = outgoing[direction * SLOTS : (direction + 1) * SLOTS]


def metric_kernel(group_ref, metric_ref, out_ref, turned):
    turned[...] = jnp.concatenate(
        [metric_ref[...], jnp.zeros((256 - 4 * QUAD, 128), jnp.float32)], axis=0
    ).T
    own = turned[pl.ds(pl.multiple_of(group_ref[0] * NEAR, NEAR), NEAR), :]
    for index in range(4 * QUAD):
        out_ref[index] = jnp.broadcast_to(own[:, index : index + 1], (NEAR, 128))


def jump_kernel(adjoint_ref, index_ref, penalty_ref, *refs):
    received_refs, out_ref = refs[:4], refs[4]
    traces = traces_of(adjoint_ref)
    received = jnp.concatenate([ref[...] for ref in received_refs], axis=0).T[:TRACE_ROWS]
    index = index_ref[...]
    where_local = lax.broadcasted_iota(jnp.int32, (512, 128), 0)
    where_far = lax.broadcasted_iota(jnp.int32, (128, 128), 0) + 512
    local_parts = split_three(traces)
    far_parts = split_three(received)
    for side in range(4):
        wanted = index[side : side + 1]
        near = jnp.where(where_local == wanted, 1.0, 0.0).astype(jnp.bfloat16)
        far = jnp.where(where_far == wanted, 1.0, 0.0).astype(jnp.bfloat16)
        outer = sum(dot(part, near) for part in local_parts) + sum(
            dot(part, far) for part in far_parts
        )
        for component in range(3):
            for step in range(POINTS):
                row = (component * POINTS + step) * GROUPS
                far_row = (component * POINTS + 6 - step) * GROUPS
                weight = penalty_ref[side * POINTS + step : side * POINTS + step + 1]
                inner = adjoint_ref[component * QUAD + rim_point(side, step)]
                jump = outer[far_row : far_row + GROUPS] - inner
                out_ref[(component * POINTS + step) * 4 + side] = weight * jump


def unpack_kernel(in_ref, jump_ref, out_ref):
    sides_at = {}
    for side in range(4):
        for step in range(POINTS):
            sides_at.setdefault(rim_point(side, step), []).append((side, step))
    for tile in range(BACK_TILES):
        block = in_ref[:, tile].reshape(128, 128).T
        for k in range(8):
            row = 8 * tile + k
            if row >= BACK_ROWS:
                break
            component, point = divmod(row, QUAD)
            value = block[16 * k : 16 * k + 16]
            for side, step in sides_at.get(point, ()):
                value = value + jump_ref[(component * POINTS + step) * 4 + side]
            out_ref[row] = value


def call(kernel, shapes, *args, scratch=(), scalars=0, flops=0):
    vmem = pl.BlockSpec(memory_space=pltpu.VMEM)
    smem = pl.BlockSpec(memory_space=pltpu.SMEM)
    many = isinstance(shapes, list)
    outs = [jax.ShapeDtypeStruct(s, jnp.float32) for s in (shapes if many else [shapes])]
    moved = sum(int(np.prod(a.shape)) * a.dtype.itemsize for a in args)
    moved += sum(int(np.prod(o.shape)) * 4 for o in outs)
    return pl.pallas_call(
        kernel,
        out_shape=outs if many else outs[0],
        in_specs=[smem] * scalars + [vmem] * (len(args) - scalars),
        out_specs=[vmem] * len(outs) if many else vmem,
        scratch_shapes=list(scratch),
        compiler_params=pltpu.CompilerParams(vmem_limit_bytes=VMEM_LIMIT),
        cost_estimate=pl.CostEstimate(flops=flops, bytes_accessed=moved, transcendentals=0),
    )(*args)


def passed_along(block, axis, distance):
    count = lax.axis_size(axis)
    return lax.ppermute(block, axis, [((i - distance) % count, i) for i in range(count)])


def shards(adjoint, base_flow, metric, penalty, send_sides, ext_index):
    synthesis, analysis, slope = fourier_tables()
    synth_high, synth_low = halves(np.concatenate([synthesis, slope], axis=0).T)
    back_high, back_low = halves(analysis.T)
    natural = jnp.transpose(adjoint, (0, 2, 1, 3)).reshape(BACK_ROWS, GROUPS, 128)
    base = jnp.transpose(base_flow, (0, 2, 1, 3)).reshape(BACK_ROWS, GROUPS, 128)
    group = lax.axis_index("mode").reshape(1)

    packed = call(pack_kernel, (GROUPS, FIELD_TILES, NEAR, 128), natural, base)
    arrived = lax.all_to_all(packed, "mode", split_axis=0, concat_axis=0, tiled=True)

    outgoing = call(
        send_kernel, [(SLOTS, TRACE_LANES)] * 4, natural, send_sides.reshape(1, 4 * SLOTS)
    )
    received = [passed_along(block, "elem", o) for block, o in zip(outgoing, OFFSETS)]
    own_metric = call(
        metric_kernel,
        (4 * QUAD, NEAR, 128),
        group,
        metric.reshape(4 * QUAD, 128),
        scratch=[pltpu.VMEM((128, 256), jnp.float32)],
        scalars=1,
    ).reshape(4, QUAD, NEAR, 128)

    field_rows, back_rows = FIELD_TILES * 64, BACK_TILES * 64
    coefficients = call(
        main_kernel,
        (GROUPS, BACK_TILES, NEAR, 128),
        arrived,
        own_metric,
        jnp.asarray(synth_high),
        jnp.asarray(synth_low),
        jnp.asarray(back_high),
        jnp.asarray(back_low),
        scratch=[
            pltpu.VMEM((field_rows, MODES), jnp.bfloat16),
            pltpu.VMEM((field_rows, MODES), jnp.bfloat16),
            pltpu.VMEM((field_rows, 2 * MODES), jnp.float32),
            pltpu.VMEM((ROWS * 8, MODES), jnp.float32),
            pltpu.VMEM((ROWS * 8, MODES), jnp.float32),
            pltpu.VMEM((back_rows, MODES), jnp.float32),
            pltpu.VMEM((back_rows, MODES), jnp.float32),
        ],
    )
    returned = lax.all_to_all(coefficients, "mode", split_axis=0, concat_axis=0, tiled=True)
    jumps = call(
        jump_kernel,
        (84, GROUPS, 128),
        natural,
        ext_index,
        penalty.reshape(4 * POINTS, 128),
        *received,
    )
    out = call(unpack_kernel, (BACK_ROWS, GROUPS, 128), returned, jumps)
    return jnp.transpose(out.reshape(3, QUAD, GROUPS, 128), (0, 2, 1, 3))


def solution(mesh):
    placed = (
        P(None, "mode", None, "elem"),
        P(None, "mode", None, "elem"),
        P(None, None, "elem"),
        P(None, None, "elem"),
        P("elem", None, None),
        P(None, "elem"),
    )
    return jax.shard_map(
        shards, mesh=mesh, in_specs=placed, out_specs=P(None, "mode", None, "elem"), check_vma=False
    )
```

profile of v0, /device:TPU:2, one launch (start us, length us, event | category | flops | bytes accessed | tf_op | source)
XLA Modules:
  0.0 100.3 jit_solution(7284306480225159025)
XLA Ops:
  0.0 3.8 %shard_map.100 = f32[16,37,8,128]{3,2,1,0:T(8,128)} custom-call(f32[147,16,128]{2,1,0:T(8,128)} %bitcast.11, f32[147,16,128]{2,1,0:T(8,128)} %bitcast.15), custom_call_target="tpu_custom_call" | custom-call | bytes 4833280 | tf_op jit(solution)/shard_map/pallas_call | solution.py:356
  3.8 9.6 %all-to-all-start = ((f32[16,37,8,128]{3,2,1,0:T(8,128)}), f32[16,37,8,128]{3,2,1,0:T(8,128)S(1)}, u32[]{:S(2)}, u32[]{:S(2)}) async-start(f32[16,37,8,128]{3,2,1,0:T(8,128)} %shard_map.100), calls=%async_computation | async-start | bytes 4849664 | tf_op jit(solution)/shard_map/all_to_all | solution.py:381
  13.4 0.7 reshape.27.metric_ref
  14.0 2.3 %shard_map.101 = f32[196,8,128]{2,1,0:T(8,128)} custom-call(s32[1]{0:T(128)} %bitcast.4.group_ref, f32[196,128]{1,0:T(8,128)} %reshape.27.metric_ref), custom_call_target="tpu_custom_call" | custom-call | bytes 903172 | tf_op jit(solution)/shard_map/pallas_call | solution.py:356
  16.3 25.7 %all-to-all-done.in_ref = f32[16,37,8,128]{3,2,1,0:T(8,128)S(1)} async-done(((f32[16,37,8,128]{3,2,1,0:T(8,128)}), f32[16,37,8,128]{3,2,1,0:T(8,128)S(1)}, u32[]{:S(2)}, u32[]{:S(2)}) %all-to-all-start) | async-done | bytes 2424864 | tf_op jit(solution)/shard_map/all_to_all | solution.py:381
  42.1 1.5 %copy-done = f32[16,37,8,128]{3,2,1,0:T(8,128)} copy-done((f32[16,37,8,128]{3,2,1,0:T(8,128)}, f32[16,37,8,128]{3,2,1,0:T(8,128)S(1)}, u32[]{:S(2)}) %copy-start) | copy-done | bytes 2424856
  43.5 18.3 %shard_map.102 = f32[16,19,8,128]{3,2,1,0:T(8,128)} custom-call(f32[16,37,8,128]{3,2,1,0:T(8,128)} %copy-done, f32[4,49,8,128]{3,2,1,0:T(8,128)} %bitcast.14, bf16[256,512]{1,0:T(8,128)(2,1)} %constant.12.clone.synth_high_ref, bf16[256,512]{1,0:T(8,128)(2,1)} %constant.13.clone.synth_low_ref, bf16[256,256]{1,0:T(8,128)(2,1)} %constant.14.clone.back_high_ref, ...), custom_call_target="tpu_custom_call" | custom-call | bytes 5259264 | tf_op jit(solution)/shard_map/pallas_call | solution.py:356
  61.8 7.4 %all-to-all-start.1 = ((f32[16,19,8,128]{3,2,1,0:T(8,128)}), f32[16,19,8,128]{3,2,1,0:T(8,128)S(1)}, u32[]{:S(2)}, u32[]{:S(2)}) async-start(f32[16,19,8,128]{3,2,1,0:T(8,128)} %shard_map.102), calls=%async_computation.1 | async-start | bytes 2490368 | tf_op jit(solution)/shard_map/all_to_all | solution.py:416
  69.2 0.6 reshape.30.sides_ref
  69.8 2.4 %shard_map.103 = (f32[32,384]{1,0:T(8,128)}, f32[32,384]{1,0:T(8,128)}, f32[32,384]{1,0:T(8,128)}, f32[32,384]{1,0:T(8,128)}) custom-call(f32[147,16,128]{2,1,0:T(8,128)} %bitcast.12, s32[1,128]{1,0:T(1,128)} %reshape.30.sides_ref), custom_call_target="tpu_custom_call" | custom-call | bytes 1401344 | tf_op jit(solution)/shard_map/pallas_call | solution.py:356
  72.2 0.0 collective-permute-start
  72.2 9.8 %collective-permute-start.1 = (f32[32,384]{1,0:T(8,128)}, f32[32,384]{1,0:T(8,128)S(1)}, u32[]{:S(2)}, u32[]{:S(2)}) collective-permute-start(f32[32,384]{1,0:T(8,128)} %get-tuple-element.10), channel_id=1, source_target_pairs={{16,0},{32,16},{48,32},{64,48},{80,64},{96,80},{112,96},{128,112},... | collective-permute-start | bytes 147464 | tf_op jit(solution)/shard_map/ppermute | solution.py:369
  82.0 1.9 %collective-permute-start.2 = (f32[32,384]{1,0:T(8,128)}, f32[32,384]{1,0:T(8,128)S(1)}, u32[]{:S(2)}, u32[]{:S(2)}) collective-permute-start(f32[32,384]{1,0:T(8,128)} %get-tuple-element.11), channel_id=1, source_target_pairs={{480,0},{496,16},{0,32},{16,48},{32,64},{48,80},{64,96},{80,112},{... | collective-permute-start | bytes 147464 | tf_op jit(solution)/shard_map/ppermute | solution.py:369
  84.0 5.8 %collective-permute-start.3 = (f32[32,384]{1,0:T(8,128)}, f32[32,384]{1,0:T(8,128)S(1)}, u32[]{:S(2)}, u32[]{:S(2)}) collective-permute-start(f32[32,384]{1,0:T(8,128)} %get-tuple-element.12), channel_id=1, source_target_pairs={{32,0},{48,16},{64,32},{80,48},{96,64},{112,80},{128,96},{144,112}... | collective-permute-start | bytes 147464 | tf_op jit(solution)/shard_map/ppermute | solution.py:369
  89.7 0.6 reshape.29.penalty_ref
  90.3 0.0 collective-permute-done.refs_0_
  90.3 0.0 collective-permute-done.1.refs_1_
  90.4 0.0 collective-permute-done.2.refs_2_
  90.4 1.4 %collective-permute-done.3.refs_3_ = f32[32,384]{1,0:T(8,128)S(1)} collective-permute-done((f32[32,384]{1,0:T(8,128)}, f32[32,384]{1,0:T(8,128)S(1)}, u32[]{:S(2)}, u32[]{:S(2)}) %collective-permute-start.3) | collective-permute-done | bytes 49184 | tf_op jit(solution)/shard_map/ppermute | solution.py:369
  91.8 0.6 copy-done.6
  92.4 4.0 %shard_map.104.jump_ref = f32[84,16,128]{2,1,0:T(8,128)} custom-call(f32[147,16,128]{2,1,0:T(8,128)} %bitcast.13, s32[4,128]{1,0:T(4,128)} %index_ref.1, f32[28,128]{1,0:T(8,128)} %reshape.29.penalty_ref, f32[32,384]{1,0:T(8,128)} %copy-done.3, f32[32,384]{1,0:T(8,128)} %copy-done.4, f32[32,384]{1,0:T(8,128)} %copy-done.5, f32[32,384]{1,0:T(8,128)} %copy-done.6), custom_call_target="tpu_custom_call" | custom-call | bytes 2105344 | tf_op jit(solution)/shard_map/pallas_call | solution.py:356
  96.4 0.0 all-to-all-done.1.in_ref
  96.4 1.1 %copy-done.1 = f32[16,19,8,128]{3,2,1,0:T(8,128)} copy-done((f32[16,19,8,128]{3,2,1,0:T(8,128)}, f32[16,19,8,128]{3,2,1,0:T(8,128)S(1)}, u32[]{:S(2)}) %copy-start.1) | copy-done | bytes 1245208
  97.5 2.9 %shard_map.105 = f32[147,16,128]{2,1,0:T(8,128)} custom-call(f32[16,19,8,128]{3,2,1,0:T(8,128)} %copy-done.1, f32[84,16,128]{2,1,0:T(8,128)} %shard_map.104.jump_ref), custom_call_target="tpu_custom_call" | custom-call | bytes 3137536 | tf_op jit(solution)/shard_map/pallas_call | solution.py:356
  (17 shorter events, 0.0 us)
Async XLA Ops:
  3.8 9.6 %copy-start.2 = (f32[4,49,128]{2,0,1:T(4,128)S(1)}, f32[4,49,128]{2,0,1:T(4,128)}, u32[]{:S(2)}) copy-start(f32[4,49,128]{2,0,1:T(4,128)} %param.12) | copy-start | bytes 301060
  3.8 38.3 %all-to-all-start = ((f32[16,37,8,128]{3,2,1,0:T(8,128)}), f32[16,37,8,128]{3,2,1,0:T(8,128)S(1)}, u32[]{:S(2)}, u32[]{:S(2)}) async-start(f32[16,37,8,128]{3,2,1,0:T(8,128)} %shard_map.100), calls=%async_computation | async-start | bytes 4849664 | tf_op jit(solution)/shard_map/all_to_all | solution.py:381
  42.1 1.5 %copy-start = (f32[16,37,8,128]{3,2,1,0:T(8,128)}, f32[16,37,8,128]{3,2,1,0:T(8,128)S(1)}, u32[]{:S(2)}) copy-start(f32[16,37,8,128]{3,2,1,0:T(8,128)S(1)} %all-to-all-done.in_ref) | copy-start | bytes 7274500
  61.8 7.4 %copy-start.8 = (s32[1,4,32]{2,1,0:T(4,128)S(1)}, s32[1,4,32]{2,1,0:T(4,128)}, u32[]{:S(2)}) copy-start(s32[1,4,32]{2,1,0:T(4,128)} %param.14) | copy-start | bytes 1540
  61.8 27.9 %copy-start.7 = (f32[4,7,128]{2,0,1:T(4,128)S(1)}, f32[4,7,128]{2,0,1:T(4,128)}, u32[]{:S(2)}) copy-start(f32[4,7,128]{2,0,1:T(4,128)} %param.13) | copy-start | bytes 43012
  61.8 34.6 %all-to-all-start.1 = ((f32[16,19,8,128]{3,2,1,0:T(8,128)}), f32[16,19,8,128]{3,2,1,0:T(8,128)S(1)}, u32[]{:S(2)}, u32[]{:S(2)}) async-start(f32[16,19,8,128]{3,2,1,0:T(8,128)} %shard_map.102), calls=%async_computation.1 | async-start | bytes 2490368 | tf_op jit(solution)/shard_map/all_to_all | solution.py:416
  72.2 18.1 %collective-permute-start = (f32[32,384]{1,0:T(8,128)}, f32[32,384]{1,0:T(8,128)S(1)}, u32[]{:S(2)}, u32[]{:S(2)}) collective-permute-start(f32[32,384]{1,0:T(8,128)} %get-tuple-element.9), channel_id=1, source_target_pairs={{496,0},{0,16},{16,32},{32,48},{48,64},{64,80},{80,96},{96,112},{1... | collective-permute-start | bytes 147464 | tf_op jit(solution)/shard_map/ppermute | solution.py:369
  72.2 18.1 %collective-permute-start.1 = (f32[32,384]{1,0:T(8,128)}, f32[32,384]{1,0:T(8,128)S(1)}, u32[]{:S(2)}, u32[]{:S(2)}) collective-permute-start(f32[32,384]{1,0:T(8,128)} %get-tuple-element.10), channel_id=1, source_target_pairs={{16,0},{32,16},{48,32},{64,48},{80,64},{96,80},{112,96},{128,112},... | collective-permute-start | bytes 147464 | tf_op jit(solution)/shard_map/ppermute | solution.py:369
  82.0 8.3 %collective-permute-start.2 = (f32[32,384]{1,0:T(8,128)}, f32[32,384]{1,0:T(8,128)S(1)}, u32[]{:S(2)}, u32[]{:S(2)}) collective-permute-start(f32[32,384]{1,0:T(8,128)} %get-tuple-element.11), channel_id=1, source_target_pairs={{480,0},{496,16},{0,32},{16,48},{32,64},{48,80},{64,96},{80,112},{... | collective-permute-start | bytes 147464 | tf_op jit(solution)/shard_map/ppermute | solution.py:369
  84.0 7.8 %collective-permute-start.3 = (f32[32,384]{1,0:T(8,128)}, f32[32,384]{1,0:T(8,128)S(1)}, u32[]{:S(2)}, u32[]{:S(2)}) collective-permute-start(f32[32,384]{1,0:T(8,128)} %get-tuple-element.12), channel_id=1, source_target_pairs={{32,0},{48,16},{64,32},{80,48},{96,64},{112,80},{128,96},{144,112}... | collective-permute-start | bytes 147464 | tf_op jit(solution)/shard_map/ppermute | solution.py:369
  90.3 1.4 %copy-start.3 = (f32[32,384]{1,0:T(8,128)}, f32[32,384]{1,0:T(8,128)S(1)}, u32[]{:S(2)}) copy-start(f32[32,384]{1,0:T(8,128)S(1)} %collective-permute-done.refs_0_) | copy-start | bytes 147460
  90.3 1.4 %copy-start.4 = (f32[32,384]{1,0:T(8,128)}, f32[32,384]{1,0:T(8,128)S(1)}, u32[]{:S(2)}) copy-start(f32[32,384]{1,0:T(8,128)S(1)} %collective-permute-done.1.refs_1_) | copy-start | bytes 147460
  90.4 1.4 %copy-start.5 = (f32[32,384]{1,0:T(8,128)}, f32[32,384]{1,0:T(8,128)S(1)}, u32[]{:S(2)}) copy-start(f32[32,384]{1,0:T(8,128)S(1)} %collective-permute-done.2.refs_2_) | copy-start | bytes 147460
  91.8 0.6 copy-start.6
  96.4 1.1 %copy-start.1 = (f32[16,19,8,128]{3,2,1,0:T(8,128)}, f32[16,19,8,128]{3,2,1,0:T(8,128)S(1)}, u32[]{:S(2)}) copy-start(f32[16,19,8,128]{3,2,1,0:T(8,128)S(1)} %all-to-all-done.1.in_ref) | copy-start | bytes 3735556
where the time goes:
time: 101 us; the launch traced here: 100 us
  starting transfers between devices  34.4 us (34%)
  Pallas kernels  33.7 us (33%)
  waiting for transfers between devices  27.1 us (27%)
  local copies, waits for them, and re-layouts  5.03 us (5%)
    pallas_call x6, Pallas kernels, call(): pl.pallas_call(kernel, out_shape=outs if many else outs[0], in_specs=[sme...  33.7 us
    all_to_all x1, waiting for transfers between devices, shards(): lax.all_to_all(packed, 'mode', split_axis=0, concat_axis=0, tiled=True)  25.7 us
    ppermute x4, starting transfers between devices, passed_along(): lax.ppermute(block, axis, [((i - distance) % count, i) for i in range(cou...  17.5 us
    all_to_all x1, starting transfers between devices, shards(): lax.all_to_all(packed, 'mode', split_axis=0, concat_axis=0, tiled=True)  9.55 us
    all_to_all x1, starting transfers between devices, shards(): lax.all_to_all(coefficients, 'mode', split_axis=0, concat_axis=0, tiled=T...  7.36 us
    unnamed x20, local copies, waits for them, and re-layouts  3.17 us
  transfers between devices with their start and end apart: 6, of which 2 were waited for; matrix products, arithmetic and copies ran while one was open for 2% of the time, Pallas kernels for 9%

commit v1 on v0

--- a/solution.py
+++ b/solution.py
@@ -21,7 +21,7 @@
 OFFSETS = (1, -1, 2, -2)
 TRACE_ROWS = 3 * POINTS * GROUPS
 TRACE_LANES = 384
-VMEM_LIMIT = 56 * 1024 * 1024
+MEBI = 1024 * 1024
 
 
 def legendre_pair(degree, position):
@@ -79,11 +79,11 @@
     return synthesis, analysis, slope
 
 
-def halves(table):
+def stacked(table):
     table = table.astype(np.float32)
     high = table.astype(jnp.bfloat16)
     low = (table - high.astype(np.float32)).astype(jnp.bfloat16)
-    return high, low
+    return np.concatenate([high, high, low], axis=0)
 
 
 def rim_point(side, step):
@@ -91,12 +91,22 @@
     return (step, POINTS * step + last, POINTS * last + last - step, POINTS * (last - step))[side]
 
 
-def swap_blocks(tiles, masks):
-    turned = [pltpu.roll(tile, 16 * q, 1) if q else tile for q, tile in enumerate(tiles)]
+def barrel(turned, masks):
     moved = [turned[-k % 8] for k in range(8)]
     for bit in range(3):
         moved = [jnp.where(masks[bit], moved[(k - (1 << bit)) % 8], moved[k]) for k in range(8)]
-    return [pltpu.roll(tile, 128 - 16 * g, 1) if g else tile for g, tile in enumerate(moved)]
+    return moved
+
+
+def gather_blocks(turned, masks):
+    return [
+        pltpu.roll(tile, 128 - 16 * g, 1) if g else tile
+        for g, tile in enumerate(barrel(turned, masks))
+    ]
+
+
+def scatter_blocks(tiles, masks):
+    return barrel([pltpu.roll(tile, 16 * q, 1) if q else tile for q, tile in enumerate(tiles)], masks)
 
 
 def block_masks():
@@ -122,20 +132,30 @@
     return jnp.dot(left, right, preferred_element_type=jnp.float32)
 
 
-def pack_kernel(adjoint_ref, base_ref, out_ref):
-    def put(tile, block):
-        out_ref[:, tile] = block.reshape(128, 128).T.reshape(GROUPS, NEAR, 128)
-
-    for tile in range(FIELD_TILES):
-        first, end = 8 * tile, min(8 * tile + 8, ROWS)
-        parts = []
-        if first < BACK_ROWS:
-            parts.append(adjoint_ref[first : min(end, BACK_ROWS)])
-        if end > BACK_ROWS:
-            parts.append(base_ref[max(first, BACK_ROWS) - BACK_ROWS : end - BACK_ROWS])
-        if 8 * tile + 8 > end:
-            parts.append(base_ref[: 8 * tile + 8 - end])
-        put(tile, parts[0] if len(parts) == 1 else jnp.concatenate(parts, axis=0))
+def pack_kernel(group_ref, adjoint_ref, base_ref, out_ref):
+    turn = group_ref[0] % 8
+    order = [lax.rem(k - turn + 8, 8) for k in range(8)]
+
+    def put(tile, source, first):
+        block = jnp.concatenate([source[first + k] for k in order], axis=0)
+        out_ref[:, tile] = block.T.reshape(GROUPS, NEAR, 128)
+
+    @pl.loop(0, 18, unroll=3)
+    def _(tile):
+        put(tile, adjoint_ref, 8 * tile)
+
+    @pl.loop(0, 17)
+    def _(tile):
+        put(19 + tile, base_ref, 8 * tile + 5)
+
+    for tile, first in ((18, 144), (36, 288)):
+        rows = []
+        for k in order:
+            row = jnp.minimum(first + k, ROWS - 1)
+            inside = adjoint_ref[jnp.minimum(row, BACK_ROWS - 1)]
+            outside = base_ref[jnp.maximum(row - BACK_ROWS, 0)]
+            rows.append(jnp.where(row < BACK_ROWS, inside, outside))
+        out_ref[:, tile] = jnp.concatenate(rows, axis=0).T.reshape(GROUPS, NEAR, 128)
 
 
 def derive_line(values, odd_table, even_table, centre):
@@ -161,10 +181,9 @@
 def main_kernel(
     in_ref,
     metric_ref,
-    synth_high_ref,
-    synth_low_ref,
-    back_high_ref,
-    back_low_ref,
+    synth_ref,
+    back_ref,
+    jump_ref,
     out_ref,
     high,
     low,
@@ -176,14 +195,16 @@
 ):
     masks = block_masks()
 
-    @pl.loop(0, FIELD_TILES)
-    def _(tile):
+    def gather(tile):
         rows = pl.ds(pl.multiple_of(tile * 64, 64), 64)
         for half in range(2):
-            swapped = swap_blocks([in_ref[8 * half + k, tile] for k in range(8)], masks)
+            swapped = gather_blocks([in_ref[8 * half + k, tile] for k in range(8)], masks)
             upper, lower = split_two(jnp.concatenate(swapped, axis=0))
             high[rows, pl.ds(128 * half, 128)] = upper
             low[rows, pl.ds(128 * half, 128)] = lower
+
+    pl.loop(0, FIELD_TILES - 1, unroll=4)(gather)
+    gather(FIELD_TILES - 1)
 
     block = FIELD_TILES * 16
 
@@ -191,11 +212,8 @@
     def _(step):
         rows = pl.ds(pl.multiple_of(step * block, 16), block)
         upper = high[rows, :]
-        plane[rows, :] = (
-            dot(upper, synth_high_ref[...])
-            + dot(low[rows, :], synth_high_ref[...])
-            + dot(upper, synth_low_ref[...])
-        )
+        parts = jnp.concatenate([upper, low[rows, :], upper], axis=1)
+        plane[rows, :] = dot(parts, synth_ref[...])
 
     matrix = lobatto_matrix(POINTS - 1)
     mirrored = matrix[:, ::-1]
@@ -252,21 +270,20 @@
     def _(step):
         rows = pl.ds(pl.multiple_of(step * back_block, 32), back_block)
         upper, lower = split_two(product[rows, :])
-        coefficient[rows, :] = (
-            dot(upper, back_high_ref[...])
-            + dot(lower, back_high_ref[...])
-            + dot(upper, back_low_ref[...])
-        )
-
-    @pl.loop(0, BACK_TILES)
-    def _(tile):
+        parts = jnp.concatenate([upper, lower, upper], axis=1)
+        coefficient[rows, :] = dot(parts, back_ref[...])
+
+    def scatter(tile):
         for half in range(2):
             lanes = pl.ds(128 * half, 128)
             pieces = [
                 coefficient[pl.ds(pl.multiple_of(tile * 64 + 8 * k, 8), 8), lanes] for k in range(8)
             ]
-            for k, swapped in enumerate(swap_blocks(pieces, masks)):
+            for k, swapped in enumerate(scatter_blocks(pieces, masks)):
                 out_ref[8 * half + k, tile] = swapped
+
+    pl.loop(0, BACK_TILES - 1, unroll=3)(scatter)
+    scatter(BACK_TILES - 1)
 
 
 def traces_of(adjoint_ref):
@@ -328,27 +345,42 @@
                 out_ref[(component * POINTS + step) * 4 + side] = weight * jump
 
 
-def unpack_kernel(in_ref, jump_ref, out_ref):
+def unpack_kernel(group_ref, in_ref, jump_ref, out_ref):
+    turn = group_ref[0] % 8
+
+    def place(tile, count):
+        block = in_ref[:, tile].reshape(128, 128).T
+        for k in range(8):
+            row = 8 * tile + lax.rem(k - turn + 8, 8)
+
+            def store(row=row, k=k):
+                out_ref[row] = block[16 * k : 16 * k + 16]
+
+            if count == 8:
+                store()
+            else:
+                pl.when(row < BACK_ROWS)(store)
+
+    pl.loop(0, BACK_TILES - 1, unroll=3)(lambda tile: place(tile, 8))
+    place(BACK_TILES - 1, BACK_ROWS % 8)
     sides_at = {}
     for side in range(4):
         for step in range(POINTS):
             sides_at.setdefault(rim_point(side, step), []).append((side, step))
-    for tile in range(BACK_TILES):
-        block = in_ref[:, tile].reshape(128, 128).T
-        for k in range(8):
-            row = 8 * tile + k
-            if row >= BACK_ROWS:
-                break
-            component, point = divmod(row, QUAD)
-            value = block[16 * k : 16 * k + 16]
-            for side, step in sides_at.get(point, ()):
-                value = value + jump_ref[(component * POINTS + step) * 4 + side]
-            out_ref[row] = value
-
-
-def call(kernel, shapes, *args, scratch=(), scalars=0, flops=0):
+
+    @pl.loop(0, 3)
+    def _(component):
+        for point, sides in sides_at.items():
+            value = out_ref[component * QUAD + point]
+            for side, step in sides:
+                value = value + jump_ref[component * 4 * POINTS + step * 4 + side]
+            out_ref[component * QUAD + point] = value
+
+
+def call(kernel, shapes, *args, scratch=(), scalars=0, unread=0, grant=12):
     vmem = pl.BlockSpec(memory_space=pltpu.VMEM)
     smem = pl.BlockSpec(memory_space=pltpu.SMEM)
+    anywhere = pl.BlockSpec(memory_space=pl.ANY)
     many = isinstance(shapes, list)
     outs = [jax.ShapeDtypeStruct(s, jnp.float32) for s in (shapes if many else [shapes])]
     moved = sum(int(np.prod(a.shape)) * a.dtype.itemsize for a in args)
@@ -356,11 +388,11 @@
     return pl.pallas_call(
         kernel,
         out_shape=outs if many else outs[0],
-        in_specs=[smem] * scalars + [vmem] * (len(args) - scalars),
+        in_specs=[smem] * scalars + [vmem] * (len(args) - scalars - unread) + [anywhere] * unread,
         out_specs=[vmem] * len(outs) if many else vmem,
         scratch_shapes=list(scratch),
-        compiler_params=pltpu.CompilerParams(vmem_limit_bytes=VMEM_LIMIT),
-        cost_estimate=pl.CostEstimate(flops=flops, bytes_accessed=moved, transcendentals=0),
+        compiler_params=pltpu.CompilerParams(vmem_limit_bytes=grant * MEBI),
+        cost_estimate=pl.CostEstimate(flops=0, bytes_accessed=moved, transcendentals=0),
     )(*args)
 
 
@@ -371,13 +403,13 @@
 
 def shards(adjoint, base_flow, metric, penalty, send_sides, ext_index):
     synthesis, analysis, slope = fourier_tables()
-    synth_high, synth_low = halves(np.concatenate([synthesis, slope], axis=0).T)
-    back_high, back_low = halves(analysis.T)
+    synth = stacked(np.concatenate([synthesis, slope], axis=0).T)
+    back = stacked(analysis.T)
     natural = jnp.transpose(adjoint, (0, 2, 1, 3)).reshape(BACK_ROWS, GROUPS, 128)
     base = jnp.transpose(base_flow, (0, 2, 1, 3)).reshape(BACK_ROWS, GROUPS, 128)
     group = lax.axis_index("mode").reshape(1)
 
-    packed = call(pack_kernel, (GROUPS, FIELD_TILES, NEAR, 128), natural, base)
+    packed = call(pack_kernel, (GROUPS, FIELD_TILES, NEAR, 128), group, natural, base, scalars=1)
     arrived = lax.all_to_all(packed, "mode", split_axis=0, concat_axis=0, tiled=True)
 
     outgoing = call(
@@ -392,6 +424,14 @@
         scratch=[pltpu.VMEM((128, 256), jnp.float32)],
         scalars=1,
     ).reshape(4, QUAD, NEAR, 128)
+    jumps = call(
+        jump_kernel,
+        (84, GROUPS, 128),
+        natural,
+        ext_index,
+        penalty.reshape(4 * POINTS, 128),
+        *received,
+    )
 
     field_rows, back_rows = FIELD_TILES * 64, BACK_TILES * 64
     coefficients = call(
@@ -399,10 +439,9 @@
         (GROUPS, BACK_TILES, NEAR, 128),
         arrived,
         own_metric,
-        jnp.asarray(synth_high),
-        jnp.asarray(synth_low),
-        jnp.asarray(back_high),
-        jnp.asarray(back_low),
+        jnp.asarray(synth),
+        jnp.asarray(back),
+        jumps,
         scratch=[
             pltpu.VMEM((field_rows, MODES), jnp.bfloat16),
             pltpu.VMEM((field_rows, MODES), jnp.bfloat16),
@@ -412,17 +451,11 @@
             pltpu.VMEM((back_rows, MODES), jnp.float32),
             pltpu.VMEM((back_rows, MODES), jnp.float32),
         ],
+        unread=1,
+        grant=28,
     )
     returned = lax.all_to_all(coefficients, "mode", split_axis=0, concat_axis=0, tiled=True)
-    jumps = call(
-        jump_kernel,
-        (84, GROUPS, 128),
-        natural,
-        ext_index,
-        penalty.reshape(4 * POINTS, 128),
-        *received,
-    )
-    out = call(unpack_kernel, (BACK_ROWS, GROUPS, 128), returned, jumps)
+    out = call(unpack_kernel, (BACK_ROWS, GROUPS, 128), group, returned, jumps, scalars=1)
     return jnp.transpose(out.reshape(3, QUAD, GROUPS, 128), (0, 2, 1, 3))
 
 

time: 101 us -> 85.9 us (0.85)
  the two profiles are of different devices: /device:TPU:2 before, /device:TPU:480 now
where the time goes in v1:
time: 85.9 us; the launch traced here: 85.3 us
  blocking collectives  21.9 us (25%)
  waiting for transfers between devices  21.7 us (25%)
  Pallas kernels  17.4 us (20%)
  starting transfers between devices  14.8 us (17%)
  local copies, waits for them, and re-layouts  9.4 us (11%)
    all_to_all x1, blocking collectives, shards(): lax.all_to_all(coefficients, 'mode', split_axis=0, concat_axis=0, tiled=T...  21.9 us
    all_to_all x1, waiting for transfers between devices, shards(): lax.all_to_all(packed, 'mode', split_axis=0, concat_axis=0, tiled=True)  19.6 us
    pallas_call x6, Pallas kernels, call(): pl.pallas_call(kernel, out_shape=outs if many else outs[0], in_specs=[sme...  17.4 us
    unnamed x34, local copies, waits for them, and re-layouts  9.31 us
    ppermute x4, starting transfers between devices, passed_along(): lax.ppermute(block, axis, [((i - distance) % count, i) for i in range(cou...  7.58 us
    all_to_all x1, starting transfers between devices, shards(): lax.all_to_all(packed, 'mode', split_axis=0, concat_axis=0, tiled=True)  7.21 us
    ppermute x4, waiting for transfers between devices, passed_along(): lax.ppermute(block, axis, [((i - distance) % count, i) for i in range(cou...  2.08 us
  transfers between devices with their start and end apart: 5, of which 2 were waited for; matrix products, arithmetic and copies ran while one was open for 0% of the time, Pallas kernels for 3%

profile of v1, /device:TPU:480, one launch (start us, length us, event | category | flops | bytes accessed | tf_op | source)
XLA Modules:
  0.0 85.3 jit_solution(3091741880875154256)
XLA Ops:
  0.0 1.3 %copy-done = f32[3,16,49,128]{3,1,2,0:T(8,128)S(1)} copy-done((f32[3,16,49,128]{3,1,2,0:T(8,128)S(1)}, f32[3,16,49,128]{3,1,2,0:T(8,128)}, u32[]{:S(2)}) %copy-start) | copy-done | bytes 1204248
  1.3 1.3 %copy-done.3 = f32[3,16,49,128]{3,1,2,0:T(8,128)S(1)} copy-done((f32[3,16,49,128]{3,1,2,0:T(8,128)S(1)}, f32[3,16,49,128]{3,1,2,0:T(8,128)}, u32[]{:S(2)}) %copy-start.3) | copy-done | bytes 1204248
  2.6 2.6 %shard_map.82 = f32[16,37,8,128]{3,2,1,0:T(8,128)S(1)} custom-call(s32[1]{0:T(128)} %bitcast.group_ref, f32[147,16,128]{2,1,0:T(8,128)S(1)} %bitcast.11, f32[147,16,128]{2,1,0:T(8,128)S(1)} %bitcast.15), custom_call_target="tpu_custom_call" | custom-call | bytes 4833284 | tf_op jit(solution)/shard_map/pallas_call | solution.py:388
  5.2 1.5 %copy-done.2 = f32[16,37,8,128]{3,2,1,0:T(8,128)} copy-done((f32[16,37,8,128]{3,2,1,0:T(8,128)}, f32[16,37,8,128]{3,2,1,0:T(8,128)S(1)}, u32[]{:S(2)}) %copy-start.2) | copy-done | bytes 2424856
  6.7 7.2 %all-to-all-start = ((f32[16,37,8,128]{3,2,1,0:T(8,128)}), f32[16,37,8,128]{3,2,1,0:T(8,128)}, u32[]{:S(2)}, u32[]{:S(2)}) async-start(f32[16,37,8,128]{3,2,1,0:T(8,128)} %copy-done.2), calls=%async_computation | async-start | bytes 4849664 | tf_op jit(solution)/shard_map/all_to_all | solution.py:413
  13.9 0.1 reshape.30.sides_ref
  14.0 0.5 shard_map.84
  14.5 1.7 %collective-permute-start.1 = (f32[32,384]{1,0:T(8,128)S(1)}, f32[32,384]{1,0:T(8,128)S(1)}, u32[]{:S(2)}, u32[]{:S(2)}) collective-permute-start(f32[32,384]{1,0:T(8,128)S(1)} %get-tuple-element.10), channel_id=1, source_target_pairs={{16,0},{32,16},{48,32},{64,48},{80,64},{96,80},{112,96},{128,112},... | collective-permute-start | bytes 147464 | tf_op jit(solution)/shard_map/ppermute | solution.py:401
  16.3 2.6 %collective-permute-start.2 = (f32[32,384]{1,0:T(8,128)S(1)}, f32[32,384]{1,0:T(8,128)S(1)}, u32[]{:S(2)}, u32[]{:S(2)}) collective-permute-start(f32[32,384]{1,0:T(8,128)S(1)} %get-tuple-element.11), channel_id=1, source_target_pairs={{480,0},{496,16},{0,32},{16,48},{32,64},{48,80},{64,96},{80,112},{... | collective-permute-start | bytes 147464 | tf_op jit(solution)/shard_map/ppermute | solution.py:401
  18.8 3.3 %collective-permute-start.3 = (f32[32,384]{1,0:T(8,128)S(1)}, f32[32,384]{1,0:T(8,128)S(1)}, u32[]{:S(2)}, u32[]{:S(2)}) collective-permute-start(f32[32,384]{1,0:T(8,128)S(1)} %get-tuple-element.12), channel_id=1, source_target_pairs={{32,0},{48,16},{64,32},{80,48},{96,64},{112,80},{128,96},{144,112}... | collective-permute-start | bytes 147464 | tf_op jit(solution)/shard_map/ppermute | solution.py:401
  22.2 0.5 shard_map.83
  22.7 0.6 copy-done.6
  23.4 0.6 copy-done.8
  24.0 2.1 %collective-permute-done.3.refs_3_ = f32[32,384]{1,0:T(8,128)S(1)} collective-permute-done((f32[32,384]{1,0:T(8,128)S(1)}, f32[32,384]{1,0:T(8,128)S(1)}, u32[]{:S(2)}, u32[]{:S(2)}) %collective-permute-start.3) | collective-permute-done | bytes 49184 | tf_op jit(solution)/shard_map/ppermute | solution.py:401
  26.0 0.6 copy-done.10
  26.7 0.8 copy-done.7
  27.5 0.8 copy-done.9
  28.3 0.8 copy-done.11
  29.1 1.8 %shard_map.85.jump_ref = f32[84,16,128]{2,1,0:T(8,128)S(1)} custom-call(f32[147,16,128]{2,1,0:T(8,128)S(1)} %bitcast.13, s32[4,128]{1,0:T(4,128)S(1)} %copy-done.12, f32[28,128]{1,0:T(8,128)S(1)} %reshape.29.penalty_ref, f32[32,384]{1,0:T(8,128)S(1)} %collective-permute-done.refs_0_, f32[32,384]{1,0:T(8,128)S(1)} %copy-done.7, f32[32,384]{1,0:T(8,128)S(1)} %copy-done.9, ...), custom_call_target="tpu_custom_call" | custom-call | bytes 2105344 | tf_op jit(solution)/shard_map/pallas_call | solution.py:388
  30.9 19.6 %all-to-all-done.in_ref = f32[16,37,8,128]{3,2,1,0:T(8,128)} async-done(((f32[16,37,8,128]{3,2,1,0:T(8,128)}), f32[16,37,8,128]{3,2,1,0:T(8,128)}, u32[]{:S(2)}, u32[]{:S(2)}) %all-to-all-start) | async-done | bytes 2424864 | tf_op jit(solution)/shard_map/all_to_all | solution.py:413
  50.5 1.0 %copy-done.5 = bf16[768,256]{1,0:T(8,128)(2,1)S(1)} copy-done((bf16[768,256]{1,0:T(8,128)(2,1)S(1)}, bf16[768,256]{1,0:T(8,128)(2,1)}, u32[]{:S(2)}) %copy-start.5) | copy-done | bytes 393240
  51.5 10.0 %shard_map.86 = f32[16,19,8,128]{3,2,1,0:T(8,128)S(1)} custom-call(f32[16,37,8,128]{3,2,1,0:T(8,128)} %all-to-all-done.in_ref, f32[4,49,8,128]{3,2,1,0:T(8,128)S(1)} %bitcast.14, bf16[768,512]{1,0:T(8,128)(2,1)S(1)} %copy-done.4, bf16[768,256]{1,0:T(8,128)(2,1)S(1)} %copy-done.5, f32[84,16,128]{2,1,0:T(8,128)S(1)} %shard_map.85.jump_ref), custom_call_target="tpu_custom_call" | custom-call | bytes 6340608 | tf_op jit(solution)/shard_map/pallas_call | solution.py:388
  61.5 21.9 %all_to_all.10.in_ref = f32[16,19,8,128]{3,2,1,0:T(8,128)S(1)} all-to-all(f32[16,19,8,128]{3,2,1,0:T(8,128)S(1)} %shard_map.86), channel_id=1, replica_groups=mesh['elem'=32,'mode'=16] {'mode'}, dimensions={0} | all-to-all | bytes 2490368 | tf_op jit(solution)/shard_map/all_to_all | solution.py:457
  83.4 1.9 %shard_map.87 = f32[147,16,128]{2,1,0:T(8,128)} custom-call(s32[1]{0:T(128)} %bitcast.group_ref, f32[16,19,8,128]{3,2,1,0:T(8,128)S(1)} %all_to_all.10.in_ref, f32[84,16,128]{2,1,0:T(8,128)S(1)} %shard_map.85.jump_ref), custom_call_target="tpu_custom_call" | custom-call | bytes 3137540 | tf_op jit(solution)/shard_map/pallas_call | solution.py:388
  (30 shorter events, 0.1 us)
Async XLA Ops:
  0.0 1.3 %copy-start = (f32[3,16,49,128]{3,1,2,0:T(8,128)S(1)}, f32[3,16,49,128]{3,1,2,0:T(8,128)}, u32[]{:S(2)}) copy-start(f32[3,16,49,128]{3,1,2,0:T(8,128)} %param.8) | copy-start | bytes 3612676
  1.3 1.3 %copy-start.3 = (f32[3,16,49,128]{3,1,2,0:T(8,128)S(1)}, f32[3,16,49,128]{3,1,2,0:T(8,128)}, u32[]{:S(2)}) copy-start(f32[3,16,49,128]{3,1,2,0:T(8,128)} %param.9) | copy-start | bytes 3612676
  5.2 1.5 %copy-start.2 = (f32[16,37,8,128]{3,2,1,0:T(8,128)}, f32[16,37,8,128]{3,2,1,0:T(8,128)S(1)}, u32[]{:S(2)}) copy-start(f32[16,37,8,128]{3,2,1,0:T(8,128)S(1)} %shard_map.82) | copy-start | bytes 7274500
  6.6 7.2 %copy-start.15 = (s32[1,4,32]{2,1,0:T(4,128)S(1)}, s32[1,4,32]{2,1,0:T(4,128)}, u32[]{:S(2)}) copy-start(s32[1,4,32]{2,1,0:T(4,128)} %param.12) | copy-start | bytes 1540
  6.6 7.3 %copy-start.1 = (f32[3,16,49,128]{3,1,2,0:T(8,128)S(1)}, f32[3,16,49,128]{3,1,2,0:T(8,128)}, u32[]{:S(2)}) copy-start(f32[3,16,49,128]{3,1,2,0:T(8,128)} %param.8) | copy-start | bytes 3612676
  6.7 43.9 %all-to-all-start = ((f32[16,37,8,128]{3,2,1,0:T(8,128)}), f32[16,37,8,128]{3,2,1,0:T(8,128)}, u32[]{:S(2)}, u32[]{:S(2)}) async-start(f32[16,37,8,128]{3,2,1,0:T(8,128)} %copy-done.2), calls=%async_computation | async-start | bytes 4849664 | tf_op jit(solution)/shard_map/all_to_all | solution.py:413
  13.9 8.2 %copy-start.13 = (f32[4,49,128]{2,0,1:T(4,128)S(1)}, f32[4,49,128]{2,0,1:T(4,128)}, u32[]{:S(2)}) copy-start(f32[4,49,128]{2,0,1:T(4,128)} %param.10) | copy-start | bytes 301060
  14.0 8.7 %copy-start.14 = (f32[4,7,128]{2,0,1:T(4,128)S(1)}, f32[4,7,128]{2,0,1:T(4,128)}, u32[]{:S(2)}) copy-start(f32[4,7,128]{2,0,1:T(4,128)} %param.11) | copy-start | bytes 43012
  14.0 12.7 %copy-start.12 = (s32[4,128]{1,0:T(4,128)S(1)}, s32[4,128]{1,0:T(4,128)}, u32[]{:S(2)}) copy-start(s32[4,128]{1,0:T(4,128)} %index_ref.1) | copy-start | bytes 6148
  14.5 8.2 %collective-permute-start = (f32[32,384]{1,0:T(8,128)S(1)}, f32[32,384]{1,0:T(8,128)S(1)}, u32[]{:S(2)}, u32[]{:S(2)}) collective-permute-start(f32[32,384]{1,0:T(8,128)S(1)} %get-tuple-element.9), channel_id=1, source_target_pairs={{496,0},{0,16},{16,32},{32,48},{48,64},{64,80},{80,96},{96,112},{1... | collective-permute-start | bytes 147464 | tf_op jit(solution)/shard_map/ppermute | solution.py:401
  14.5 8.2 %collective-permute-start.1 = (f32[32,384]{1,0:T(8,128)S(1)}, f32[32,384]{1,0:T(8,128)S(1)}, u32[]{:S(2)}, u32[]{:S(2)}) collective-permute-start(f32[32,384]{1,0:T(8,128)S(1)} %get-tuple-element.10), channel_id=1, source_target_pairs={{16,0},{32,16},{48,32},{64,48},{80,64},{96,80},{112,96},{128,112},... | collective-permute-start | bytes 147464 | tf_op jit(solution)/shard_map/ppermute | solution.py:401
  16.3 7.1 %collective-permute-start.2 = (f32[32,384]{1,0:T(8,128)S(1)}, f32[32,384]{1,0:T(8,128)S(1)}, u32[]{:S(2)}, u32[]{:S(2)}) collective-permute-start(f32[32,384]{1,0:T(8,128)S(1)} %get-tuple-element.11), channel_id=1, source_target_pairs={{480,0},{496,16},{0,32},{16,48},{32,64},{48,80},{64,96},{80,112},{... | collective-permute-start | bytes 147464 | tf_op jit(solution)/shard_map/ppermute | solution.py:401
  18.8 7.2 %collective-permute-start.3 = (f32[32,384]{1,0:T(8,128)S(1)}, f32[32,384]{1,0:T(8,128)S(1)}, u32[]{:S(2)}, u32[]{:S(2)}) collective-permute-start(f32[32,384]{1,0:T(8,128)S(1)} %get-tuple-element.12), channel_id=1, source_target_pairs={{32,0},{48,16},{64,32},{80,48},{96,64},{112,80},{128,96},{144,112}... | collective-permute-start | bytes 147464 | tf_op jit(solution)/shard_map/ppermute | solution.py:401
  22.7 27.8 %copy-start.4 = (bf16[768,512]{1,0:T(8,128)(2,1)S(1)}, bf16[768,512]{1,0:T(8,128)(2,1)}, u32[]{:S(2)}) copy-start(bf16[768,512]{1,0:T(8,128)(2,1)} %constant.8.clone.synth_ref) | copy-start | bytes 2359300
  22.7 0.6 copy-start.6
  23.4 0.6 copy-start.8
  26.0 0.6 copy-start.10
  26.7 0.8 copy-start.7
  27.5 0.8 copy-start.9
  28.3 0.8 copy-start.11
  50.5 1.0 %copy-start.5 = (bf16[768,256]{1,0:T(8,128)(2,1)S(1)}, bf16[768,256]{1,0:T(8,128)(2,1)}, u32[]{:S(2)}) copy-start(bf16[768,256]{1,0:T(8,128)(2,1)} %constant.9.clone.back_ref) | copy-start | bytes 1179652

commit v2 on v1

--- a/solution.py
+++ b/solution.py
@@ -83,7 +83,7 @@
     table = table.astype(np.float32)
     high = table.astype(jnp.bfloat16)
     low = (table - high.astype(np.float32)).astype(jnp.bfloat16)
-    return np.concatenate([high, high, low], axis=0)
+    return np.concatenate([high, low], axis=0)
 
 
 def rim_point(side, step):
@@ -132,30 +132,41 @@
     return jnp.dot(left, right, preferred_element_type=jnp.float32)
 
 
-def pack_kernel(group_ref, adjoint_ref, base_ref, out_ref):
+FIELD_CUTS = (0, 48, 96, BACK_ROWS)
+PACK_GROUPS = (0, 6, 12, 18, 24, 30, FIELD_TILES)
+
+
+def pack_kernel(group_ref, adjoint_ref, base_ref, out_ref, fields, packed, in_sems, out_sems):
+    arrivals = []
+    for source, offset in ((adjoint_ref, 0), (base_ref, BACK_ROWS)):
+        for first, end in zip(FIELD_CUTS, FIELD_CUTS[1:]):
+            arrivals.append(
+                pltpu.make_async_copy(
+                    source.at[pl.ds(first, end - first)],
+                    fields.at[pl.ds(offset + first, end - first)],
+                    in_sems.at[len(arrivals)],
+                )
+            )
+            arrivals[-1].start()
+    fields[ROWS:] = jnp.zeros((8 * FIELD_TILES - ROWS, GROUPS, 128), jnp.float32)
     turn = group_ref[0] % 8
     order = [lax.rem(k - turn + 8, 8) for k in range(8)]
-
-    def put(tile, source, first):
-        block = jnp.concatenate([source[first + k] for k in order], axis=0)
-        out_ref[:, tile] = block.T.reshape(GROUPS, NEAR, 128)
-
-    @pl.loop(0, 18, unroll=3)
-    def _(tile):
-        put(tile, adjoint_ref, 8 * tile)
-
-    @pl.loop(0, 17)
-    def _(tile):
-        put(19 + tile, base_ref, 8 * tile + 5)
-
-    for tile, first in ((18, 144), (36, 288)):
-        rows = []
-        for k in order:
-            row = jnp.minimum(first + k, ROWS - 1)
-            inside = adjoint_ref[jnp.minimum(row, BACK_ROWS - 1)]
-            outside = base_ref[jnp.maximum(row - BACK_ROWS, 0)]
-            rows.append(jnp.where(row < BACK_ROWS, inside, outside))
-        out_ref[:, tile] = jnp.concatenate(rows, axis=0).T.reshape(GROUPS, NEAR, 128)
+    departures = []
+    for number, (first, end) in enumerate(zip(PACK_GROUPS, PACK_GROUPS[1:])):
+        arrivals[number].wait()
+        for tile in range(first, end):
+            block = jnp.concatenate([fields[8 * tile + k] for k in order], axis=0)
+            packed[:, tile] = block.T.reshape(GROUPS, NEAR, 128)
+        departures.append(
+            pltpu.make_async_copy(
+                packed.at[:, pl.ds(first, end - first)],
+                out_ref.at[:, pl.ds(first, end - first)],
+                out_sems.at[number],
+            )
+        )
+        departures[-1].start()
+    for departure in departures:
+        departure.wait()
 
 
 def derive_line(values, odd_table, even_table, centre):
@@ -185,6 +196,9 @@
     back_ref,
     jump_ref,
     out_ref,
+    synth,
+    back,
+    table_sems,
     high,
     low,
     plane,
@@ -194,6 +208,17 @@
     coefficient,
 ):
     masks = block_masks()
+    tables = []
+    for source, target in ((synth_ref, synth), (back_ref, back)):
+        for place, part in enumerate((0, 0, 1)):
+            tables.append(
+                pltpu.make_async_copy(
+                    source.at[pl.ds(MODES * part, MODES)],
+                    target.at[pl.ds(MODES * place, MODES)],
+                    table_sems.at[len(tables)],
+                )
+            )
+            tables[-1].start()
 
     def gather(tile):
         rows = pl.ds(pl.multiple_of(tile * 64, 64), 64)
@@ -203,17 +228,19 @@
             high[rows, pl.ds(128 * half, 128)] = upper
             low[rows, pl.ds(128 * half, 128)] = lower
 
-    pl.loop(0, FIELD_TILES - 1, unroll=4)(gather)
+    pl.loop(0, FIELD_TILES - 1, unroll=6)(gather)
     gather(FIELD_TILES - 1)
-
-    block = FIELD_TILES * 16
-
-    @pl.loop(0, 4)
+    for table in tables:
+        table.wait()
+
+    block = FIELD_TILES * 32
+
+    @pl.loop(0, 2)
     def _(step):
         rows = pl.ds(pl.multiple_of(step * block, 16), block)
         upper = high[rows, :]
         parts = jnp.concatenate([upper, low[rows, :], upper], axis=1)
-        plane[rows, :] = dot(parts, synth_ref[...])
+        plane[rows, :] = dot(parts, synth[...])
 
     matrix = lobatto_matrix(POINTS - 1)
     mirrored = matrix[:, ::-1]
@@ -264,14 +291,9 @@
                 product[at(k), lanes] = turned[k] - carried
 
     product[BACK_ROWS * 8 :, :] = jnp.zeros((BACK_TILES * 64 - BACK_ROWS * 8, MODES), jnp.float32)
-    back_block = BACK_TILES * 32
-
-    @pl.loop(0, 2)
-    def _(step):
-        rows = pl.ds(pl.multiple_of(step * back_block, 32), back_block)
-        upper, lower = split_two(product[rows, :])
-        parts = jnp.concatenate([upper, lower, upper], axis=1)
-        coefficient[rows, :] = dot(parts, back_ref[...])
+    upper, lower = split_two(product[...])
+    parts = jnp.concatenate([upper, lower, upper], axis=1)
+    coefficient[...] = dot(parts, back[...])
 
     def scatter(tile):
         for half in range(2):
@@ -345,51 +367,58 @@
                 out_ref[(component * POINTS + step) * 4 + side] = weight * jump
 
 
-def unpack_kernel(group_ref, in_ref, jump_ref, out_ref):
+BACK_GROUPS = (0, 7, 13, BACK_TILES)
+
+
+def unpack_kernel(group_ref, in_ref, jump_ref, out_ref, advect, sems):
     turn = group_ref[0] % 8
-
-    def place(tile, count):
-        block = in_ref[:, tile].reshape(128, 128).T
-        for k in range(8):
-            row = 8 * tile + lax.rem(k - turn + 8, 8)
-
-            def store(row=row, k=k):
-                out_ref[row] = block[16 * k : 16 * k + 16]
-
-            if count == 8:
-                store()
-            else:
-                pl.when(row < BACK_ROWS)(store)
-
-    pl.loop(0, BACK_TILES - 1, unroll=3)(lambda tile: place(tile, 8))
-    place(BACK_TILES - 1, BACK_ROWS % 8)
     sides_at = {}
     for side in range(4):
         for step in range(POINTS):
             sides_at.setdefault(rim_point(side, step), []).append((side, step))
-
-    @pl.loop(0, 3)
-    def _(component):
+    departures = []
+    for component in range(3):
+        for tile in range(BACK_GROUPS[component], BACK_GROUPS[component + 1]):
+            block = in_ref[:, tile].reshape(128, 128).T
+            for k in range(8):
+                row = 8 * tile + lax.rem(k - turn + 8, 8)
+                advect[row] = block[16 * k : 16 * k + 16]
+        first = component * QUAD
         for point, sides in sides_at.items():
-            value = out_ref[component * QUAD + point]
+            value = advect[first + point]
             for side, step in sides:
-                value = value + jump_ref[component * 4 * POINTS + step * 4 + side]
-            out_ref[component * QUAD + point] = value
-
-
-def call(kernel, shapes, *args, scratch=(), scalars=0, unread=0, grant=12):
-    vmem = pl.BlockSpec(memory_space=pltpu.VMEM)
-    smem = pl.BlockSpec(memory_space=pltpu.SMEM)
-    anywhere = pl.BlockSpec(memory_space=pl.ANY)
+                value = value + jump_ref[(component * POINTS + step) * 4 + side]
+            advect[first + point] = value
+        departures.append(
+            pltpu.make_async_copy(
+                advect.at[pl.ds(first, QUAD)], out_ref.at[pl.ds(first, QUAD)], sems.at[component]
+            )
+        )
+        departures[-1].start()
+    for departure in departures:
+        departure.wait()
+
+
+def call(kernel, shapes, *args, places=None, into=pltpu.VMEM, scratch=(), grant=12):
+    spaces = {"v": pltpu.VMEM, "h": pltpu.HBM, "s": pltpu.SMEM, "a": pl.ANY}
+    places = places or "v" * len(args)
     many = isinstance(shapes, list)
-    outs = [jax.ShapeDtypeStruct(s, jnp.float32) for s in (shapes if many else [shapes])]
+    if into is pltpu.HBM:
+        outs = [pltpu.HBM(s, jnp.float32) for s in (shapes if many else [shapes])]
+    else:
+        outs = [jax.ShapeDtypeStruct(s, jnp.float32) for s in (shapes if many else [shapes])]
     moved = sum(int(np.prod(a.shape)) * a.dtype.itemsize for a in args)
     moved += sum(int(np.prod(o.shape)) * 4 for o in outs)
+    args = [
+        pltpu.with_memory_space_constraint(a, pltpu.HBM) if p == "h" else a
+        for a, p in zip(args, places)
+    ]
+    out_spec = pl.BlockSpec(memory_space=into)
     return pl.pallas_call(
         kernel,
         out_shape=outs if many else outs[0],
-        in_specs=[smem] * scalars + [vmem] * (len(args) - scalars - unread) + [anywhere] * unread,
-        out_specs=[vmem] * len(outs) if many else vmem,
+        in_specs=[pl.BlockSpec(memory_space=spaces[p]) for p in places],
+        out_specs=[out_spec] * len(outs) if many else out_spec,
         scratch_shapes=list(scratch),
         compiler_params=pltpu.CompilerParams(vmem_limit_bytes=grant * MEBI),
         cost_estimate=pl.CostEstimate(flops=0, bytes_accessed=moved, transcendentals=0),
@@ -409,7 +438,21 @@
     base = jnp.transpose(base_flow, (0, 2, 1, 3)).reshape(BACK_ROWS, GROUPS, 128)
     group = lax.axis_index("mode").reshape(1)
 
-    packed = call(pack_kernel, (GROUPS, FIELD_TILES, NEAR, 128), group, natural, base, scalars=1)
+    packed = call(
+        pack_kernel,
+        (GROUPS, FIELD_TILES, NEAR, 128),
+        group,
+        natural,
+        base,
+        places="shh",
+        into=pltpu.HBM,
+        scratch=[
+            pltpu.VMEM((8 * FIELD_TILES, GROUPS, 128), jnp.float32),
+            pltpu.VMEM((GROUPS, FIELD_TILES, NEAR, 128), jnp.float32),
+            pltpu.SemaphoreType.DMA((6,)),
+            pltpu.SemaphoreType.DMA((6,)),
+        ],
+    )
     arrived = lax.all_to_all(packed, "mode", split_axis=0, concat_axis=0, tiled=True)
 
     outgoing = call(
@@ -421,8 +464,8 @@
         (4 * QUAD, NEAR, 128),
         group,
         metric.reshape(4 * QUAD, 128),
+        places="sv",
         scratch=[pltpu.VMEM((128, 256), jnp.float32)],
-        scalars=1,
     ).reshape(4, QUAD, NEAR, 128)
     jumps = call(
         jump_kernel,
@@ -442,7 +485,11 @@
         jnp.asarray(synth),
         jnp.asarray(back),
         jumps,
+        places="vvhha",
         scratch=[
+            pltpu.VMEM((3 * MODES, 2 * MODES), jnp.bfloat16),
+            pltpu.VMEM((3 * MODES, MODES), jnp.bfloat16),
+            pltpu.SemaphoreType.DMA((6,)),
             pltpu.VMEM((field_rows, MODES), jnp.bfloat16),
             pltpu.VMEM((field_rows, MODES), jnp.bfloat16),
             pltpu.VMEM((field_rows, 2 * MODES), jnp.float32),
@@ -451,11 +498,22 @@
             pltpu.VMEM((back_rows, MODES), jnp.float32),
             pltpu.VMEM((back_rows, MODES), jnp.float32),
         ],
-        unread=1,
         grant=28,
     )
     returned = lax.all_to_all(coefficients, "mode", split_axis=0, concat_axis=0, tiled=True)
-    out = call(unpack_kernel, (BACK_ROWS, GROUPS, 128), group, returned, jumps, scalars=1)
+    out = call(
+        unpack_kernel,
+        (BACK_ROWS, GROUPS, 128),
+        group,
+        returned,
+        jumps,
+        places="svv",
+        into=pltpu.HBM,
+        scratch=[
+            pltpu.VMEM((8 * BACK_TILES, GROUPS, 128), jnp.float32),
+            pltpu.SemaphoreType.DMA((3,)),
+        ],
+    )
     return jnp.transpose(out.reshape(3, QUAD, GROUPS, 128), (0, 2, 1, 3))
 
 

time: 85.9 us -> 79.8 us (0.929)
  local copies, waits for them, and re-layouts: 9.4 us -> 0.14 us
  waiting for transfers between devices: 21.7 us -> 26 us
  Pallas kernels: 17.4 us -> 16.5 us
    unnamed x34 -> x12, local copies, waits for them, and re-layouts: 9.31 us -> 0.04 us
    all_to_all x1, waiting for transfers between devices: 19.6 us -> 22.7 us  [shards(): lax.all_to_all(packed, 'mode', split_axis=0, concat_axis=0, tiled=True)]
    ppermute x4, waiting for transfers between devices: 2.08 us -> 3.32 us  [passed_along(): lax.ppermute(block, axis, [((i - distance) % count, i) for i in range(cou...]
  transfers between devices with their start and end apart: 5 -> 5, of which waited for: 2 -> 2; matrix products, arithmetic and copies ran while one was open for 0% -> 0% of each run, Pallas kernels for 3% -> 4%
where the time goes in v2:
time: 79.8 us; the launch traced here: 79.4 us
  waiting for transfers between devices  26 us (33%)
  blocking collectives  21.9 us (27%)
  Pallas kernels  16.5 us (21%)
  starting transfers between devices  14.8 us (19%)
    all_to_all x1, waiting for transfers between devices, shards(): lax.all_to_all(packed, 'mode', split_axis=0, concat_axis=0, tiled=True)  22.7 us
    all_to_all x1, blocking collectives, shards(): lax.all_to_all(coefficients, 'mode', split_axis=0, concat_axis=0, tiled=T...  21.9 us
    pallas_call x6, Pallas kernels, call(): pl.pallas_call(kernel, out_shape=outs if many else outs[0], in_specs=[pl....  16.5 us
    ppermute x4, starting transfers between devices, passed_along(): lax.ppermute(block, axis, [((i - distance) % count, i) for i in range(cou...  7.58 us
    all_to_all x1, starting transfers between devices, shards(): lax.all_to_all(packed, 'mode', split_axis=0, concat_axis=0, tiled=True)  7.22 us
    ppermute x4, waiting for transfers between devices, passed_along(): lax.ppermute(block, axis, [((i - distance) % count, i) for i in range(cou...  3.32 us
  transfers between devices with their start and end apart: 5, of which 2 were waited for; matrix products, arithmetic and copies ran while one was open for 0% of the time, Pallas kernels for 4%

profile of v2, /device:TPU:480, one launch (start us, length us, event | category | flops | bytes accessed | tf_op | source)
XLA Modules:
  0.0 79.4 jit_solution(4107266029926559676)
XLA Ops:
  0.0 3.0 %shard_map.82 = f32[16,37,8,128]{3,2,1,0:T(8,128)} custom-call(s32[1]{0:T(128)} %bitcast.group_ref, f32[147,16,128]{2,1,0:T(8,128)} %bitcast.11, f32[147,16,128]{2,1,0:T(8,128)} %bitcast.15), custom_call_target="tpu_custom_call" | custom-call | bytes 4833284 | tf_op jit(solution)/shard_map/pallas_call | solution.py:417
  3.0 0.0 copy-start.4
  3.0 0.0 copy-start
  3.0 7.2 %all-to-all-start = ((f32[16,37,8,128]{3,2,1,0:T(8,128)}), f32[16,37,8,128]{3,2,1,0:T(8,128)}, u32[]{:S(2)}, u32[]{:S(2)}) async-start(f32[16,37,8,128]{3,2,1,0:T(8,128)} %shard_map.82), calls=%async_computation | async-start | bytes 4849664 | tf_op jit(solution)/shard_map/all_to_all | solution.py:456
  10.2 0.0 copy-done.4
  10.2 0.0 copy-start.2
  10.2 0.1 reshape.30.sides_ref
  10.3 0.0 copy-done
  10.3 0.5 shard_map.84
  10.8 0.0 collective-permute-start
  10.9 1.7 %collective-permute-start.1 = (f32[32,384]{1,0:T(8,128)S(1)}, f32[32,384]{1,0:T(8,128)S(1)}, u32[]{:S(2)}, u32[]{:S(2)}) collective-permute-start(f32[32,384]{1,0:T(8,128)S(1)} %get-tuple-element.10), channel_id=1, source_target_pairs={{16,0},{32,16},{48,32},{64,48},{80,64},{96,80},{112,96},{128,112},... | collective-permute-start | bytes 147464 | tf_op jit(solution)/shard_map/ppermute | solution.py:430
  12.6 2.6 %collective-permute-start.2 = (f32[32,384]{1,0:T(8,128)S(1)}, f32[32,384]{1,0:T(8,128)S(1)}, u32[]{:S(2)}, u32[]{:S(2)}) collective-permute-start(f32[32,384]{1,0:T(8,128)S(1)} %get-tuple-element.11), channel_id=1, source_target_pairs={{480,0},{496,16},{0,32},{16,48},{32,64},{48,80},{64,96},{80,112},{... | collective-permute-start | bytes 147464 | tf_op jit(solution)/shard_map/ppermute | solution.py:430
  15.2 3.3 %collective-permute-start.3 = (f32[32,384]{1,0:T(8,128)S(1)}, f32[32,384]{1,0:T(8,128)S(1)}, u32[]{:S(2)}, u32[]{:S(2)}) collective-permute-start(f32[32,384]{1,0:T(8,128)S(1)} %get-tuple-element.12), channel_id=1, source_target_pairs={{32,0},{48,16},{64,32},{80,48},{96,64},{112,80},{128,96},{144,112}... | collective-permute-start | bytes 147464 | tf_op jit(solution)/shard_map/ppermute | solution.py:430
  18.5 0.0 copy-done.2
  18.5 0.5 shard_map.83
  19.0 0.0 collective-permute-done.refs_0_
  19.0 0.0 collective-permute-done.1.refs_1_
  19.1 0.0 collective-permute-done.2.refs_2_
  19.1 3.3 %collective-permute-done.3.refs_3_ = f32[32,384]{1,0:T(8,128)S(1)} collective-permute-done((f32[32,384]{1,0:T(8,128)S(1)}, f32[32,384]{1,0:T(8,128)S(1)}, u32[]{:S(2)}, u32[]{:S(2)}) %collective-permute-start.3) | collective-permute-done | bytes 49184 | tf_op jit(solution)/shard_map/ppermute | solution.py:430
  22.4 1.8 %shard_map.85.jump_ref = f32[84,16,128]{2,1,0:T(8,128)S(1)} custom-call(f32[147,16,128]{2,1,0:T(8,128)S(1)} %bitcast.13, s32[4,128]{1,0:T(4,128)S(1)} %copy-done.1, f32[28,128]{1,0:T(8,128)S(1)} %reshape.29.penalty_ref, f32[32,384]{1,0:T(8,128)S(1)} %collective-permute-done.refs_0_, f32[32,384]{1,0:T(8,128)S(1)} %collective-permute-done.1.refs_1_, ...), custom_call_target="tpu_custom_call" | custom-call | bytes 2105344 | tf_op jit(solution)/shard_map/pallas_call | solution.py:417
  24.2 22.7 %all-to-all-done.in_ref = f32[16,37,8,128]{3,2,1,0:T(8,128)} async-done(((f32[16,37,8,128]{3,2,1,0:T(8,128)}), f32[16,37,8,128]{3,2,1,0:T(8,128)}, u32[]{:S(2)}, u32[]{:S(2)}) %all-to-all-start) | async-done | bytes 2424864 | tf_op jit(solution)/shard_map/all_to_all | solution.py:456
  46.8 9.5 %shard_map.86 = f32[16,19,8,128]{3,2,1,0:T(8,128)S(1)} custom-call(f32[16,37,8,128]{3,2,1,0:T(8,128)} %all-to-all-done.in_ref, f32[4,49,8,128]{3,2,1,0:T(8,128)S(1)} %bitcast.14, bf16[512,512]{1,0:T(8,128)(2,1)} %constant.8.clone.synth_ref, bf16[512,256]{1,0:T(8,128)(2,1)} %constant.9.clone.back_ref, f32[84,16,128]{2,1,0:T(8,128)S(1)} %shard_map.85.jump_ref), custom_call_target="tpu_custom_call" | custom-call | bytes 5947392 | tf_op jit(solution)/shard_map/pallas_call | solution.py:417
  56.3 21.9 %all_to_all.10.in_ref = f32[16,19,8,128]{3,2,1,0:T(8,128)S(1)} all-to-all(f32[16,19,8,128]{3,2,1,0:T(8,128)S(1)} %shard_map.86), channel_id=1, replica_groups=mesh['elem'=32,'mode'=16] {'mode'}, dimensions={0} | all-to-all | bytes 2490368 | tf_op jit(solution)/shard_map/all_to_all | solution.py:503
  78.2 1.3 %shard_map.87 = f32[147,16,128]{2,1,0:T(8,128)} custom-call(s32[1]{0:T(128)} %bitcast.group_ref, f32[16,19,8,128]{3,2,1,0:T(8,128)S(1)} %all_to_all.10.in_ref, f32[84,16,128]{2,1,0:T(8,128)S(1)} %shard_map.85.jump_ref), custom_call_target="tpu_custom_call" | custom-call | bytes 3137540 | tf_op jit(solution)/shard_map/pallas_call | solution.py:417
  (8 shorter events, 0.0 us)
Async XLA Ops:
  3.0 7.3 %copy-start.4 = (s32[1,4,32]{2,1,0:T(4,128)S(1)}, s32[1,4,32]{2,1,0:T(4,128)}, u32[]{:S(2)}) copy-start(s32[1,4,32]{2,1,0:T(4,128)} %param.12) | copy-start | bytes 1540
  3.0 7.4 %copy-start = (f32[3,16,49,128]{3,1,2,0:T(8,128)S(1)}, f32[3,16,49,128]{3,1,2,0:T(8,128)}, u32[]{:S(2)}) copy-start(f32[3,16,49,128]{3,1,2,0:T(8,128)} %param.8) | copy-start | bytes 3612676
  3.0 43.9 %all-to-all-start = ((f32[16,37,8,128]{3,2,1,0:T(8,128)}), f32[16,37,8,128]{3,2,1,0:T(8,128)}, u32[]{:S(2)}, u32[]{:S(2)}) async-start(f32[16,37,8,128]{3,2,1,0:T(8,128)} %shard_map.82), calls=%async_computation | async-start | bytes 4849664 | tf_op jit(solution)/shard_map/all_to_all | solution.py:456
  10.2 8.2 %copy-start.2 = (f32[4,49,128]{2,0,1:T(4,128)S(1)}, f32[4,49,128]{2,0,1:T(4,128)}, u32[]{:S(2)}) copy-start(f32[4,49,128]{2,0,1:T(4,128)} %param.10) | copy-start | bytes 301060
  10.3 8.7 %copy-start.3 = (f32[4,7,128]{2,0,1:T(4,128)S(1)}, f32[4,7,128]{2,0,1:T(4,128)}, u32[]{:S(2)}) copy-start(f32[4,7,128]{2,0,1:T(4,128)} %param.11) | copy-start | bytes 43012
  10.3 12.1 %copy-start.1 = (s32[4,128]{1,0:T(4,128)S(1)}, s32[4,128]{1,0:T(4,128)}, u32[]{:S(2)}) copy-start(s32[4,128]{1,0:T(4,128)} %index_ref.1) | copy-start | bytes 6148
  10.8 8.2 %collective-permute-start = (f32[32,384]{1,0:T(8,128)S(1)}, f32[32,384]{1,0:T(8,128)S(1)}, u32[]{:S(2)}, u32[]{:S(2)}) collective-permute-start(f32[32,384]{1,0:T(8,128)S(1)} %get-tuple-element.9), channel_id=1, source_target_pairs={{496,0},{0,16},{16,32},{32,48},{48,64},{64,80},{80,96},{96,112},{1... | collective-permute-start | bytes 147464 | tf_op jit(solution)/shard_map/ppermute | solution.py:430
  10.9 8.2 %collective-permute-start.1 = (f32[32,384]{1,0:T(8,128)S(1)}, f32[32,384]{1,0:T(8,128)S(1)}, u32[]{:S(2)}, u32[]{:S(2)}) collective-permute-start(f32[32,384]{1,0:T(8,128)S(1)} %get-tuple-element.10), channel_id=1, source_target_pairs={{16,0},{32,16},{48,32},{64,48},{80,64},{96,80},{112,96},{128,112},... | collective-permute-start | bytes 147464 | tf_op jit(solution)/shard_map/ppermute | solution.py:430
  12.6 6.5 %collective-permute-start.2 = (f32[32,384]{1,0:T(8,128)S(1)}, f32[32,384]{1,0:T(8,128)S(1)}, u32[]{:S(2)}, u32[]{:S(2)}) collective-permute-start(f32[32,384]{1,0:T(8,128)S(1)} %get-tuple-element.11), channel_id=1, source_target_pairs={{480,0},{496,16},{0,32},{16,48},{32,64},{48,80},{64,96},{80,112},{... | collective-permute-start | bytes 147464 | tf_op jit(solution)/shard_map/ppermute | solution.py:430
  15.2 7.2 %collective-permute-start.3 = (f32[32,384]{1,0:T(8,128)S(1)}, f32[32,384]{1,0:T(8,128)S(1)}, u32[]{:S(2)}, u32[]{:S(2)}) collective-permute-start(f32[32,384]{1,0:T(8,128)S(1)} %get-tuple-element.12), channel_id=1, source_target_pairs={{32,0},{48,16},{64,32},{80,48},{96,64},{112,80},{128,96},{144,112}... | collective-permute-start | bytes 147464 | tf_op jit(solution)/shard_map/ppermute | solution.py:430

commit v3 on v2

--- a/solution.py
+++ b/solution.py
@@ -189,123 +189,119 @@
     )
 
 
+CHUNKS = (0, 7, 13, 19, 25, 31, FIELD_TILES)
+BACK_CHUNKS = (0, 5, 10, 15, BACK_TILES)
+
+
 def main_kernel(
-    in_ref,
-    metric_ref,
-    synth_ref,
-    back_ref,
-    jump_ref,
-    out_ref,
-    synth,
-    back,
-    table_sems,
-    high,
-    low,
-    plane,
-    first,
-    second,
-    product,
-    coefficient,
+    in_ref, metric_ref, synth_ref, back_ref, jump_ref, out_ref, plane, first, second, product, *parts
 ):
     masks = block_masks()
-    tables = []
-    for source, target in ((synth_ref, synth), (back_ref, back)):
-        for place, part in enumerate((0, 0, 1)):
-            tables.append(
-                pltpu.make_async_copy(
-                    source.at[pl.ds(MODES * part, MODES)],
-                    target.at[pl.ds(MODES * place, MODES)],
-                    table_sems.at[len(tables)],
-                )
-            )
-            tables[-1].start()
-
-    def gather(tile):
-        rows = pl.ds(pl.multiple_of(tile * 64, 64), 64)
-        for half in range(2):
-            swapped = gather_blocks([in_ref[8 * half + k, tile] for k in range(8)], masks)
-            upper, lower = split_two(jnp.concatenate(swapped, axis=0))
-            high[rows, pl.ds(128 * half, 128)] = upper
-            low[rows, pl.ds(128 * half, 128)] = lower
-
-    pl.loop(0, FIELD_TILES - 1, unroll=6)(gather)
-    gather(FIELD_TILES - 1)
-    for table in tables:
-        table.wait()
-
-    block = FIELD_TILES * 32
-
-    @pl.loop(0, 2)
-    def _(step):
-        rows = pl.ds(pl.multiple_of(step * block, 16), block)
-        upper = high[rows, :]
-        parts = jnp.concatenate([upper, low[rows, :], upper], axis=1)
-        plane[rows, :] = dot(parts, synth[...])
-
     matrix = lobatto_matrix(POINTS - 1)
     mirrored = matrix[:, ::-1]
     odd_table = (matrix - mirrored)[:4, :3] / 2.0
     even_table = (matrix + mirrored)[:3, :3] / 2.0
     centre = matrix[:3, 3]
 
-    @pl.loop(0, 6)
-    def _(field):
+    def gather(chunk):
+        for place, tile in enumerate(range(CHUNKS[chunk], CHUNKS[chunk + 1])):
+            rows = slice(64 * place, 64 * place + 64)
+            for half in range(2):
+                swapped = gather_blocks([in_ref[8 * half + k, tile] for k in range(8)], masks)
+                upper, lower = split_two(jnp.concatenate(swapped, axis=0))
+                parts[chunk][rows, 128 * half : 128 * half + 128] = upper
+                parts[chunk][rows, MODES + 128 * half : MODES + 128 * half + 128] = lower
+
+    def synthesize(half, chunk):
+        both = parts[chunk][...]
+        deep = jnp.concatenate([both, both[:, :MODES]], axis=1)
+        rows = slice(64 * CHUNKS[chunk], 64 * CHUNKS[chunk + 1])
+        lanes = slice(MODES * half, MODES * half + MODES)
+        plane[rows, lanes] = dot(deep, synth_ref[:, lanes])
+
+    def derive(half, field):
+        source = slice(MODES * half, MODES * half + 128)
+        lanes = slice(128 * half, 128 * half + 128)
+
         def at(point):
-            return pl.ds(pl.multiple_of(field * (QUAD * 8) + point * 8, 8), 8)
-
-        for half in range(2):
-            lanes = pl.ds(128 * half, 128)
-            for line in range(POINTS):
-                for stride, base, target in ((1, 7 * line, first), (7, line, second)):
-                    values = [plane[at(base + stride * k), lanes] for k in range(POINTS)]
-                    for k, slope in enumerate(derive_line(values, odd_table, even_table, centre)):
-                        target[at(base + stride * k), lanes] = slope
-
-    @pl.loop(0, QUAD)
+            row = (field * QUAD + point) * 8
+            return slice(row, row + 8)
+
+        for line in range(POINTS):
+            for stride, base, target in ((1, 7 * line, first), (7, line, second)):
+                values = [plane[at(base + stride * k), source] for k in range(POINTS)]
+                for k, slope in enumerate(derive_line(values, odd_table, even_table, centre)):
+                    target[at(base + stride * k), lanes] = slope
+
+    def combine(half, point):
+        east_first, north_first, east_second, north_second = (metric_ref[k, point] for k in range(4))
+        source = slice(MODES * half, MODES * half + 128)
+        span = slice(MODES * half + 128, MODES * half + MODES)
+        lanes = slice(128 * half, 128 * half + 128)
+
+        def at(field):
+            return pl.ds(pl.multiple_of((field * QUAD + point) * 8, 8), 8)
+
+        speed = [plane[at(k), source] for k in range(3)]
+        base = [plane[at(3 + k), source] for k in range(3)]
+        along = sum(speed[k] * first[at(3 + k), lanes] for k in range(3))
+        across = sum(speed[k] * second[at(3 + k), lanes] for k in range(3))
+        turned = (
+            east_first * along + east_second * across,
+            north_first * along + north_second * across,
+            sum(speed[k] * plane[at(3 + k), span] for k in range(3)),
+        )
+        flow_first = base[0] * east_first + base[1] * north_first
+        flow_second = base[0] * east_second + base[1] * north_second
+        for k in range(3):
+            carried = (
+                flow_first * first[at(k), lanes]
+                + flow_second * second[at(k), lanes]
+                + base[2] * plane[at(k), span]
+            )
+            product[at(k), lanes] = turned[k] - carried
+
+    def analyse(chunk):
+        rows = slice(64 * BACK_CHUNKS[chunk], 64 * BACK_CHUNKS[chunk + 1])
+        upper, lower = split_two(product[rows, :])
+        return dot(jnp.concatenate([upper, lower, upper], axis=1), back_ref[...])
+
+    def scatter(chunk, coefficient):
+        for place, tile in enumerate(range(BACK_CHUNKS[chunk], BACK_CHUNKS[chunk + 1])):
+            for half in range(2):
+                pieces = [
+                    coefficient[64 * place + 8 * k : 64 * place + 8 * k + 8, 128 * half : 128 * half + 128]
+                    for k in range(8)
+                ]
+                for k, swapped in enumerate(scatter_blocks(pieces, masks)):
+                    out_ref[8 * half + k, tile] = swapped
+
+
+    product[BACK_ROWS * 8 :, :] = jnp.zeros((BACK_TILES * 64 - BACK_ROWS * 8, MODES), jnp.float32)
+    gather(0)
+    for chunk in range(6):
+        synthesize(0, chunk)
+        if chunk < 5:
+            gather(chunk + 1)
+        if chunk:
+            derive(0, chunk - 1)
+    for chunk in range(6):
+        synthesize(1, chunk)
+        if chunk == 0:
+            derive(0, 5)
+        else:
+            derive(1, chunk - 1)
+    derive(1, 5)
+
+    @pl.loop(0, QUAD, unroll=4)
     def _(point):
-        east_first, north_first, east_second, north_second = (metric_ref[k, point] for k in range(4))
-
-        def at(field):
-            return pl.ds(pl.multiple_of(field * (QUAD * 8) + point * 8, 8), 8)
-
-        for half in range(2):
-            lanes = pl.ds(128 * half, 128)
-            span = pl.ds(MODES + 128 * half, 128)
-            speed = [plane[at(k), lanes] for k in range(3)]
-            base = [plane[at(3 + k), lanes] for k in range(3)]
-            along = sum(speed[k] * first[at(3 + k), lanes] for k in range(3))
-            across = sum(speed[k] * second[at(3 + k), lanes] for k in range(3))
-            turned = (
-                east_first * along + east_second * across,
-                north_first * along + north_second * across,
-                sum(speed[k] * plane[at(3 + k), span] for k in range(3)),
-            )
-            flow_first = base[0] * east_first + base[1] * north_first
-            flow_second = base[0] * east_second + base[1] * north_second
-            for k in range(3):
-                carried = (
-                    flow_first * first[at(k), lanes]
-                    + flow_second * second[at(k), lanes]
-                    + base[2] * plane[at(k), span]
-                )
-                product[at(k), lanes] = turned[k] - carried
-
-    product[BACK_ROWS * 8 :, :] = jnp.zeros((BACK_TILES * 64 - BACK_ROWS * 8, MODES), jnp.float32)
-    upper, lower = split_two(product[...])
-    parts = jnp.concatenate([upper, lower, upper], axis=1)
-    coefficient[...] = dot(parts, back[...])
-
-    def scatter(tile):
-        for half in range(2):
-            lanes = pl.ds(128 * half, 128)
-            pieces = [
-                coefficient[pl.ds(pl.multiple_of(tile * 64 + 8 * k, 8), 8), lanes] for k in range(8)
-            ]
-            for k, swapped in enumerate(scatter_blocks(pieces, masks)):
-                out_ref[8 * half + k, tile] = swapped
-
-    pl.loop(0, BACK_TILES - 1, unroll=3)(scatter)
-    scatter(BACK_TILES - 1)
+        combine(0, point)
+        combine(1, point)
+    held = analyse(0)
+    for chunk in range(4):
+        following = analyse(chunk + 1) if chunk < 3 else None
+        scatter(chunk, held)
+        held = following
 
 
 def traces_of(adjoint_ref):
@@ -332,13 +328,28 @@
         out_ref[...] = outgoing[direction * SLOTS : (direction + 1) * SLOTS]
 
 
-def metric_kernel(group_ref, metric_ref, out_ref, turned):
+def ready_kernel(
+    group_ref, metric_ref, synth_ref, back_ref, out_ref, synth_out, back_out, turned, sems
+):
+    copies = []
+    for source, target in ((synth_ref, synth_out), (back_ref, back_out)):
+        for place, part in enumerate((0, 0, 1)):
+            copies.append(
+                pltpu.make_async_copy(
+                    source.at[pl.ds(MODES * part, MODES)],
+                    target.at[pl.ds(MODES * place, MODES)],
+                    sems.at[len(copies)],
+                )
+            )
+            copies[-1].start()
     turned[...] = jnp.concatenate(
         [metric_ref[...], jnp.zeros((256 - 4 * QUAD, 128), jnp.float32)], axis=0
     ).T
     own = turned[pl.ds(pl.multiple_of(group_ref[0] * NEAR, NEAR), NEAR), :]
     for index in range(4 * QUAD):
         out_ref[index] = jnp.broadcast_to(own[:, index : index + 1], (NEAR, 128))
+    for copy in copies:
+        copy.wait()
 
 
 def jump_kernel(adjoint_ref, index_ref, penalty_ref, *refs):
@@ -399,26 +410,27 @@
         departure.wait()
 
 
-def call(kernel, shapes, *args, places=None, into=pltpu.VMEM, scratch=(), grant=12):
+def call(kernel, outs, *args, places=None, scratch=(), grant=12):
     spaces = {"v": pltpu.VMEM, "h": pltpu.HBM, "s": pltpu.SMEM, "a": pl.ANY}
     places = places or "v" * len(args)
-    many = isinstance(shapes, list)
-    if into is pltpu.HBM:
-        outs = [pltpu.HBM(s, jnp.float32) for s in (shapes if many else [shapes])]
-    else:
-        outs = [jax.ShapeDtypeStruct(s, jnp.float32) for s in (shapes if many else [shapes])]
-    moved = sum(int(np.prod(a.shape)) * a.dtype.itemsize for a in args)
-    moved += sum(int(np.prod(o.shape)) * 4 for o in outs)
+    many = isinstance(outs, list)
+    outs = [
+        jax.ShapeDtypeStruct(o, jnp.float32) if isinstance(o, tuple) else o
+        for o in (outs if many else [outs])
+    ]
+    out_specs = [
+        pl.BlockSpec(memory_space=getattr(o, "memory_space", None) or pltpu.VMEM) for o in outs
+    ]
+    moved = sum(int(np.prod(a.shape)) * a.dtype.itemsize for a in (*args, *outs))
     args = [
         pltpu.with_memory_space_constraint(a, pltpu.HBM) if p == "h" else a
         for a, p in zip(args, places)
     ]
-    out_spec = pl.BlockSpec(memory_space=into)
     return pl.pallas_call(
         kernel,
         out_shape=outs if many else outs[0],
         in_specs=[pl.BlockSpec(memory_space=spaces[p]) for p in places],
-        out_specs=[out_spec] * len(outs) if many else out_spec,
+        out_specs=out_specs if many else out_specs[0],
         scratch_shapes=list(scratch),
         compiler_params=pltpu.CompilerParams(vmem_limit_bytes=grant * MEBI),
         cost_estimate=pl.CostEstimate(flops=0, bytes_accessed=moved, transcendentals=0),
@@ -432,7 +444,8 @@
 
 def shards(adjoint, base_flow, metric, penalty, send_sides, ext_index):
     synthesis, analysis, slope = fourier_tables()
-    synth = stacked(np.concatenate([synthesis, slope], axis=0).T)
+    by_half = np.arange(2 * MODES).reshape(2, 2, 128).transpose(1, 0, 2).reshape(-1)
+    synth = stacked(np.concatenate([synthesis, slope], axis=0)[by_half].T)
     back = stacked(analysis.T)
     natural = jnp.transpose(adjoint, (0, 2, 1, 3)).reshape(BACK_ROWS, GROUPS, 128)
     base = jnp.transpose(base_flow, (0, 2, 1, 3)).reshape(BACK_ROWS, GROUPS, 128)
@@ -440,12 +453,11 @@
 
     packed = call(
         pack_kernel,
-        (GROUPS, FIELD_TILES, NEAR, 128),
+        pltpu.HBM((GROUPS, FIELD_TILES, NEAR, 128), jnp.float32),
         group,
         natural,
         base,
         places="shh",
-        into=pltpu.HBM,
         scratch=[
             pltpu.VMEM((8 * FIELD_TILES, GROUPS, 128), jnp.float32),
             pltpu.VMEM((GROUPS, FIELD_TILES, NEAR, 128), jnp.float32),
@@ -459,14 +471,20 @@
         send_kernel, [(SLOTS, TRACE_LANES)] * 4, natural, send_sides.reshape(1, 4 * SLOTS)
     )
     received = [passed_along(block, "elem", o) for block, o in zip(outgoing, OFFSETS)]
-    own_metric = call(
-        metric_kernel,
-        (4 * QUAD, NEAR, 128),
+    own_metric, synth, back = call(
+        ready_kernel,
+        [
+            pltpu.VMEM((4 * QUAD, NEAR, 128), jnp.float32),
+            pltpu.VMEM((3 * MODES, 2 * MODES), jnp.bfloat16),
+            pltpu.VMEM((3 * MODES, MODES), jnp.bfloat16),
+        ],
         group,
         metric.reshape(4 * QUAD, 128),
-        places="sv",
-        scratch=[pltpu.VMEM((128, 256), jnp.float32)],
-    ).reshape(4, QUAD, NEAR, 128)
+        jnp.asarray(synth),
+        jnp.asarray(back),
+        places="svhh",
+        scratch=[pltpu.VMEM((128, 256), jnp.float32), pltpu.SemaphoreType.DMA((6,))],
+    )
     jumps = call(
         jump_kernel,
         (84, GROUPS, 128),
@@ -476,39 +494,35 @@
         *received,
     )
 
-    field_rows, back_rows = FIELD_TILES * 64, BACK_TILES * 64
     coefficients = call(
         main_kernel,
         (GROUPS, BACK_TILES, NEAR, 128),
         arrived,
-        own_metric,
-        jnp.asarray(synth),
-        jnp.asarray(back),
+        own_metric.reshape(4, QUAD, NEAR, 128),
+        synth,
+        back,
         jumps,
-        places="vvhha",
+        places="vvvva",
         scratch=[
-            pltpu.VMEM((3 * MODES, 2 * MODES), jnp.bfloat16),
-            pltpu.VMEM((3 * MODES, MODES), jnp.bfloat16),
-            pltpu.SemaphoreType.DMA((6,)),
-            pltpu.VMEM((field_rows, MODES), jnp.bfloat16),
-            pltpu.VMEM((field_rows, MODES), jnp.bfloat16),
-            pltpu.VMEM((field_rows, 2 * MODES), jnp.float32),
-            pltpu.VMEM((ROWS * 8, MODES), jnp.float32),
-            pltpu.VMEM((ROWS * 8, MODES), jnp.float32),
-            pltpu.VMEM((back_rows, MODES), jnp.float32),
-            pltpu.VMEM((back_rows, MODES), jnp.float32),
+            pltpu.VMEM((64 * FIELD_TILES, 2 * MODES), jnp.float32),
+            pltpu.VMEM((8 * ROWS, MODES), jnp.float32),
+            pltpu.VMEM((8 * ROWS, MODES), jnp.float32),
+            pltpu.VMEM((64 * BACK_TILES, MODES), jnp.float32),
+        ]
+        + [
+            pltpu.VMEM((64 * (end - first), 2 * MODES), jnp.bfloat16)
+            for first, end in zip(CHUNKS, CHUNKS[1:])
         ],
         grant=28,
     )
     returned = lax.all_to_all(coefficients, "mode", split_axis=0, concat_axis=0, tiled=True)
     out = call(
         unpack_kernel,
-        (BACK_ROWS, GROUPS, 128),
+        pltpu.HBM((BACK_ROWS, GROUPS, 128), jnp.float32),
         group,
         returned,
         jumps,
         places="svv",
-        into=pltpu.HBM,
         scratch=[
             pltpu.VMEM((8 * BACK_TILES, GROUPS, 128), jnp.float32),
             pltpu.SemaphoreType.DMA((3,)),

time: 79.8 us -> 77.8 us (0.975)
  waiting for transfers between devices: 26 us -> 19.4 us
  local copies, waits for them, and re-layouts: 0.14 us -> 6.12 us
  Pallas kernels: 16.5 us -> 14.9 us
    unnamed x12 -> x28, local copies, waits for them, and re-layouts: 0.04 us -> 6.02 us
    all_to_all x1, waiting for transfers between devices: 22.7 us -> 18.8 us  [shards(): lax.all_to_all(packed, 'mode', split_axis=0, concat_axis=0, tiled=True)]
    ppermute x4, waiting for transfers between devices: 3.32 us -> 0.57 us  [passed_along(): lax.ppermute(block, axis, [((i - distance) % count, i) for i in range(cou...]
    pallas_call x6, Pallas kernels: 16.5 us -> 14.9 us  [call(): pl.pallas_call(kernel, out_shape=outs if many else outs[0], in_specs=[pl....]
  transfers between devices with their start and end apart: 5 -> 5, of which waited for: 2 -> 2; matrix products, arithmetic and copies ran while one was open for 0% -> 0% of each run, Pallas kernels for 4% -> 6%
where the time goes in v3:
time: 77.8 us; the launch traced here: 77.2 us
  blocking collectives  21.9 us (28%)
  waiting for transfers between devices  19.4 us (25%)
  Pallas kernels  14.9 us (19%)
  starting transfers between devices  14.8 us (19%)
  local copies, waits for them, and re-layouts  6.12 us (8%)
    all_to_all x1, blocking collectives, shards(): lax.all_to_all(coefficients, 'mode', split_axis=0, concat_axis=0, tiled=T...  21.9 us
    all_to_all x1, waiting for transfers between devices, shards(): lax.all_to_all(packed, 'mode', split_axis=0, concat_axis=0, tiled=True)  18.8 us
    pallas_call x6, Pallas kernels, call(): pl.pallas_call(kernel, out_shape=outs if many else outs[0], in_specs=[pl....  14.9 us
    ppermute x4, starting transfers between devices, passed_along(): lax.ppermute(block, axis, [((i - distance) % count, i) for i in range(cou...  7.58 us
    all_to_all x1, starting transfers between devices, shards(): lax.all_to_all(packed, 'mode', split_axis=0, concat_axis=0, tiled=True)  7.22 us
    unnamed x28, local copies, waits for them, and re-layouts  6.02 us
  transfers between devices with their start and end apart: 5, of which 2 were waited for; matrix products, arithmetic and copies ran while one was open for 0% of the time, Pallas kernels for 6%

profile of v3, /device:TPU:480, one launch (start us, length us, event | category | flops | bytes accessed | tf_op | source)
XLA Modules:
  0.0 77.2 jit_solution(15619861996971033365)
XLA Ops:
  0.0 2.9 %shard_map.82 = f32[16,37,8,128]{3,2,1,0:T(8,128)} custom-call(s32[1]{0:T(128)} %bitcast.group_ref, f32[147,16,128]{2,1,0:T(8,128)} %bitcast.11, f32[147,16,128]{2,1,0:T(8,128)} %bitcast.15), custom_call_target="tpu_custom_call" | custom-call | bytes 4833284 | tf_op jit(solution)/shard_map/pallas_call | solution.py:429
  2.9 0.0 copy-start.12
  3.0 0.0 copy-start
  3.0 7.2 %all-to-all-start = ((f32[16,37,8,128]{3,2,1,0:T(8,128)}), f32[16,37,8,128]{3,2,1,0:T(8,128)}, u32[]{:S(2)}, u32[]{:S(2)}) async-start(f32[16,37,8,128]{3,2,1,0:T(8,128)} %shard_map.82), calls=%async_computation | async-start | bytes 4849664 | tf_op jit(solution)/shard_map/all_to_all | solution.py:468
  10.2 0.1 reshape.30.sides_ref
  10.3 1.2 %shard_map.84 = (f32[32,384]{1,0:T(8,128)}, f32[32,384]{1,0:T(8,128)}, f32[32,384]{1,0:T(8,128)}, f32[32,384]{1,0:T(8,128)}) custom-call(f32[147,16,128]{2,1,0:T(8,128)S(1)} %bitcast.12, s32[1,128]{1,0:T(1,128)S(1)} %reshape.30.sides_ref), custom_call_target="tpu_custom_call" | custom-call | bytes 1401344 | tf_op jit(solution)/shard_map/pallas_call | solution.py:429
  11.5 1.7 %collective-permute-start.1 = (f32[32,384]{1,0:T(8,128)}, f32[32,384]{1,0:T(8,128)S(1)}, u32[]{:S(2)}, u32[]{:S(2)}) collective-permute-start(f32[32,384]{1,0:T(8,128)} %get-tuple-element.16), channel_id=1, source_target_pairs={{16,0},{32,16},{48,32},{64,48},{80,64},{96,80},{112,96},{128,112},... | collective-permute-start | bytes 147464 | tf_op jit(solution)/shard_map/ppermute | solution.py:442
  13.3 2.5 %collective-permute-start.2 = (f32[32,384]{1,0:T(8,128)}, f32[32,384]{1,0:T(8,128)S(1)}, u32[]{:S(2)}, u32[]{:S(2)}) collective-permute-start(f32[32,384]{1,0:T(8,128)} %get-tuple-element.17), channel_id=1, source_target_pairs={{480,0},{496,16},{0,32},{16,48},{32,64},{48,80},{64,96},{80,112},{... | collective-permute-start | bytes 147464 | tf_op jit(solution)/shard_map/ppermute | solution.py:442
  15.8 3.3 %collective-permute-start.3 = (f32[32,384]{1,0:T(8,128)}, f32[32,384]{1,0:T(8,128)S(1)}, u32[]{:S(2)}, u32[]{:S(2)}) collective-permute-start(f32[32,384]{1,0:T(8,128)} %get-tuple-element.18), channel_id=1, source_target_pairs={{32,0},{48,16},{64,32},{80,48},{96,64},{112,80},{128,96},{144,112}... | collective-permute-start | bytes 147464 | tf_op jit(solution)/shard_map/ppermute | solution.py:442
  19.2 1.5 %shard_map.83 = (f32[196,8,128]{2,1,0:T(8,128)S(1)}, bf16[768,512]{1,0:T(8,128)(2,1)S(1)}, bf16[768,256]{1,0:T(8,128)(2,1)S(1)}) custom-call(s32[1]{0:T(128)} %bitcast.group_ref, f32[196,128]{1,0:T(8,128)S(1)} %reshape.27.metric_ref, bf16[512,512]{1,0:T(8,128)(2,1)} %constant.8.clone.synth_ref, bf16[512,256]{1,0:T(8,128)(2,1)} %constant.9.clone.back_ref), custom_call_target="tpu_custom_call" | custom-call | bytes 2869252 | tf_op jit(solution)/shard_map/pallas_call | solution.py:429
  20.7 0.7 copy-done.1
  21.4 0.6 copy-done.3
  22.0 0.6 copy-done.5
  22.7 0.6 collective-permute-done.3.refs_3_
  23.2 0.6 copy-done.7
  23.8 0.8 %copy-done.4 = f32[32,384]{1,0:T(8,128)S(1)} copy-done((f32[32,384]{1,0:T(8,128)S(1)}, f32[32,384]{1,0:T(8,128)}, u32[]{:S(2)}) %copy-start.4) | copy-done | bytes 49176
  24.6 0.8 %copy-done.6 = f32[32,384]{1,0:T(8,128)S(1)} copy-done((f32[32,384]{1,0:T(8,128)S(1)}, f32[32,384]{1,0:T(8,128)}, u32[]{:S(2)}) %copy-start.6) | copy-done | bytes 49176
  25.4 0.8 %copy-done.8 = f32[32,384]{1,0:T(8,128)S(1)} copy-done((f32[32,384]{1,0:T(8,128)S(1)}, f32[32,384]{1,0:T(8,128)}, u32[]{:S(2)}) %copy-start.8) | copy-done | bytes 49176
  26.2 1.8 %shard_map.85.jump_ref = f32[84,16,128]{2,1,0:T(8,128)S(1)} custom-call(f32[147,16,128]{2,1,0:T(8,128)S(1)} %bitcast.13, s32[4,128]{1,0:T(4,128)S(1)} %copy-done.9, f32[28,128]{1,0:T(8,128)S(1)} %reshape.29.penalty_ref, f32[32,384]{1,0:T(8,128)S(1)} %collective-permute-done.refs_0_, f32[32,384]{1,0:T(8,128)S(1)} %copy-done.4, f32[32,384]{1,0:T(8,128)S(1)} %copy-done.6, ...), custom_call_target="tpu_custom_call" | custom-call | bytes 2105344 | tf_op jit(solution)/shard_map/pallas_call | solution.py:429
  28.0 18.8 %all-to-all-done.in_ref = f32[16,37,8,128]{3,2,1,0:T(8,128)} async-done(((f32[16,37,8,128]{3,2,1,0:T(8,128)}), f32[16,37,8,128]{3,2,1,0:T(8,128)}, u32[]{:S(2)}, u32[]{:S(2)}) %all-to-all-start) | async-done | bytes 2424864 | tf_op jit(solution)/shard_map/all_to_all | solution.py:468
  46.9 1.0 %copy-done.2 = bf16[768,256]{1,0:T(8,128)(2,1)S(1)} copy-done((bf16[768,256]{1,0:T(8,128)(2,1)S(1)}, bf16[768,256]{1,0:T(8,128)(2,1)}, u32[]{:S(2)}) %copy-start.2) | copy-done | bytes 393240
  47.8 6.2 %shard_map.86 = f32[16,19,8,128]{3,2,1,0:T(8,128)S(1)} custom-call(f32[16,37,8,128]{3,2,1,0:T(8,128)} %all-to-all-done.in_ref, f32[4,49,8,128]{3,2,1,0:T(8,128)S(1)} %bitcast.14, bf16[768,512]{1,0:T(8,128)(2,1)S(1)} %get-tuple-element.13.synth_ref, bf16[768,256]{1,0:T(8,128)(2,1)S(1)} %copy-done.2, f32[84,16,128]{2,1,0:T(8,128)S(1)} %shard_map.85.jump_ref), custom_call_target="tpu_custom_call" | custom-call | bytes 6340608 | tf_op jit(solution)/shard_map/pallas_call | solution.py:429
  54.1 21.9 %all_to_all.10.in_ref = f32[16,19,8,128]{3,2,1,0:T(8,128)S(1)} all-to-all(f32[16,19,8,128]{3,2,1,0:T(8,128)S(1)} %shard_map.86), channel_id=1, replica_groups=mesh['elem'=32,'mode'=16] {'mode'}, dimensions={0} | all-to-all | bytes 2490368 | tf_op jit(solution)/shard_map/all_to_all | solution.py:518
  75.9 1.3 %shard_map.87 = f32[147,16,128]{2,1,0:T(8,128)} custom-call(s32[1]{0:T(128)} %bitcast.group_ref, f32[16,19,8,128]{3,2,1,0:T(8,128)S(1)} %all_to_all.10.in_ref, f32[84,16,128]{2,1,0:T(8,128)S(1)} %shard_map.85.jump_ref), custom_call_target="tpu_custom_call" | custom-call | bytes 3137540 | tf_op jit(solution)/shard_map/pallas_call | solution.py:429
  (24 shorter events, 0.1 us)
Async XLA Ops:
  2.9 7.3 %copy-start.12 = (s32[1,4,32]{2,1,0:T(4,128)S(1)}, s32[1,4,32]{2,1,0:T(4,128)}, u32[]{:S(2)}) copy-start(s32[1,4,32]{2,1,0:T(4,128)} %param.12) | copy-start | bytes 1540
  3.0 7.4 %copy-start = (f32[3,16,49,128]{3,1,2,0:T(8,128)S(1)}, f32[3,16,49,128]{3,1,2,0:T(8,128)}, u32[]{:S(2)}) copy-start(f32[3,16,49,128]{3,1,2,0:T(8,128)} %param.8) | copy-start | bytes 3612676
  3.0 16.1 %copy-start.11 = (f32[4,7,128]{2,0,1:T(4,128)S(1)}, f32[4,7,128]{2,0,1:T(4,128)}, u32[]{:S(2)}) copy-start(f32[4,7,128]{2,0,1:T(4,128)} %param.11) | copy-start | bytes 43012
  3.0 43.9 %all-to-all-start = ((f32[16,37,8,128]{3,2,1,0:T(8,128)}), f32[16,37,8,128]{3,2,1,0:T(8,128)}, u32[]{:S(2)}, u32[]{:S(2)}) async-start(f32[16,37,8,128]{3,2,1,0:T(8,128)} %shard_map.82), calls=%async_computation | async-start | bytes 4849664 | tf_op jit(solution)/shard_map/all_to_all | solution.py:468
  10.2 8.9 %copy-start.10 = (f32[4,49,128]{2,0,1:T(4,128)S(1)}, f32[4,49,128]{2,0,1:T(4,128)}, u32[]{:S(2)}) copy-start(f32[4,49,128]{2,0,1:T(4,128)} %param.10) | copy-start | bytes 301060
  10.3 13.5 %copy-start.9 = (s32[4,128]{1,0:T(4,128)S(1)}, s32[4,128]{1,0:T(4,128)}, u32[]{:S(2)}) copy-start(s32[4,128]{1,0:T(4,128)} %index_ref.1) | copy-start | bytes 6148
  11.5 9.9 %collective-permute-start = (f32[32,384]{1,0:T(8,128)}, f32[32,384]{1,0:T(8,128)S(1)}, u32[]{:S(2)}, u32[]{:S(2)}) collective-permute-start(f32[32,384]{1,0:T(8,128)} %get-tuple-element.15), channel_id=1, source_target_pairs={{496,0},{0,16},{16,32},{32,48},{48,64},{64,80},{80,96},{96,112},{1... | collective-permute-start | bytes 147464 | tf_op jit(solution)/shard_map/ppermute | solution.py:442
  11.5 9.9 %collective-permute-start.1 = (f32[32,384]{1,0:T(8,128)}, f32[32,384]{1,0:T(8,128)S(1)}, u32[]{:S(2)}, u32[]{:S(2)}) collective-permute-start(f32[32,384]{1,0:T(8,128)} %get-tuple-element.16), channel_id=1, source_target_pairs={{16,0},{32,16},{48,32},{64,48},{80,64},{96,80},{112,96},{128,112},... | collective-permute-start | bytes 147464 | tf_op jit(solution)/shard_map/ppermute | solution.py:442
  13.3 8.8 %collective-permute-start.2 = (f32[32,384]{1,0:T(8,128)}, f32[32,384]{1,0:T(8,128)S(1)}, u32[]{:S(2)}, u32[]{:S(2)}) collective-permute-start(f32[32,384]{1,0:T(8,128)} %get-tuple-element.17), channel_id=1, source_target_pairs={{480,0},{496,16},{0,32},{16,48},{32,64},{48,80},{64,96},{80,112},{... | collective-permute-start | bytes 147464 | tf_op jit(solution)/shard_map/ppermute | solution.py:442
  15.8 7.4 %collective-permute-start.3 = (f32[32,384]{1,0:T(8,128)}, f32[32,384]{1,0:T(8,128)S(1)}, u32[]{:S(2)}, u32[]{:S(2)}) collective-permute-start(f32[32,384]{1,0:T(8,128)} %get-tuple-element.18), channel_id=1, source_target_pairs={{32,0},{48,16},{64,32},{80,48},{96,64},{112,80},{128,96},{144,112}... | collective-permute-start | bytes 147464 | tf_op jit(solution)/shard_map/ppermute | solution.py:442
  20.7 0.7 copy-start.1
  21.4 0.6 copy-start.3
  22.0 0.6 copy-start.5
  23.2 0.6 copy-start.7
  23.8 0.8 %copy-start.4 = (f32[32,384]{1,0:T(8,128)S(1)}, f32[32,384]{1,0:T(8,128)}, u32[]{:S(2)}) copy-start(f32[32,384]{1,0:T(8,128)} %copy-done.3) | copy-start | bytes 147460
  24.6 0.8 %copy-start.6 = (f32[32,384]{1,0:T(8,128)S(1)}, f32[32,384]{1,0:T(8,128)}, u32[]{:S(2)}) copy-start(f32[32,384]{1,0:T(8,128)} %copy-done.5) | copy-start | bytes 147460
  25.4 0.8 %copy-start.8 = (f32[32,384]{1,0:T(8,128)S(1)}, f32[32,384]{1,0:T(8,128)}, u32[]{:S(2)}) copy-start(f32[32,384]{1,0:T(8,128)} %copy-done.7) | copy-start | bytes 147460
  46.9 1.0 %copy-start.2 = (bf16[768,256]{1,0:T(8,128)(2,1)S(1)}, bf16[768,256]{1,0:T(8,128)(2,1)}, u32[]{:S(2)}) copy-start(bf16[768,256]{1,0:T(8,128)(2,1)} %copy-done.1) | copy-start | bytes 1179652

commit v4 on v3

--- a/solution.py
+++ b/solution.py
@@ -132,14 +132,16 @@
     return jnp.dot(left, right, preferred_element_type=jnp.float32)
 
 
-FIELD_CUTS = (0, 48, 96, BACK_ROWS)
-PACK_GROUPS = (0, 6, 12, 18, 24, 30, FIELD_TILES)
+ADJOINT_CUTS = (0, 48, 96, BACK_ROWS)
+BASE_CUTS = (0, 48, 96, 128, BACK_ROWS)
+PACK_GROUPS = (0, 6, 12, 18, 24, 30, 34, FIELD_TILES)
 
 
 def pack_kernel(group_ref, adjoint_ref, base_ref, out_ref, fields, packed, in_sems, out_sems):
     arrivals = []
-    for source, offset in ((adjoint_ref, 0), (base_ref, BACK_ROWS)):
-        for first, end in zip(FIELD_CUTS, FIELD_CUTS[1:]):
+    sources = ((adjoint_ref, 0, ADJOINT_CUTS), (base_ref, BACK_ROWS, BASE_CUTS))
+    for source, offset, cuts in sources:
+        for first, end in zip(cuts, cuts[1:]):
             arrivals.append(
                 pltpu.make_async_copy(
                     source.at[pl.ds(first, end - first)],
@@ -194,8 +196,24 @@
 
 
 def main_kernel(
-    in_ref, metric_ref, synth_ref, back_ref, jump_ref, out_ref, plane, first, second, product, *parts
+    in_ref,
+    metric_hbm,
+    synth_ref,
+    back_hbm,
+    jump_ref,
+    out_ref,
+    metric_ref,
+    back_ref,
+    sems,
+    plane,
+    first,
+    second,
+    product,
+    *parts,
 ):
+    metric_copy = pltpu.make_async_copy(metric_hbm, metric_ref, sems.at[3])
+    metric_copy.start()
+    back_copies = stack_table(back_hbm, back_ref, sems)
     masks = block_masks()
     matrix = lobatto_matrix(POINTS - 1)
     mirrored = matrix[:, ::-1]
@@ -234,7 +252,9 @@
                     target[at(base + stride * k), lanes] = slope
 
     def combine(half, point):
-        east_first, north_first, east_second, north_second = (metric_ref[k, point] for k in range(4))
+        east_first, north_first, east_second, north_second = (
+            metric_ref[k * QUAD + point] for k in range(4)
+        )
         source = slice(MODES * half, MODES * half + 128)
         span = slice(MODES * half + 128, MODES * half + MODES)
         lanes = slice(128 * half, 128 * half + 128)
@@ -292,6 +312,9 @@
         else:
             derive(1, chunk - 1)
     derive(1, 5)
+    metric_copy.wait()
+    for copy in back_copies:
+        copy.wait()
 
     @pl.loop(0, QUAD, unroll=4)
     def _(point):
@@ -317,7 +340,15 @@
     )
 
 
-def send_kernel(adjoint_ref, sides_ref, *out_refs):
+def fetch(source, target, sem):
+    copy = pltpu.make_async_copy(source, target, sem)
+    copy.start()
+    copy.wait()
+
+
+def send_kernel(adjoint_hbm, sides_ref, *refs):
+    out_refs, (adjoint_ref, sem) = refs[:4], refs[4:]
+    fetch(adjoint_hbm, adjoint_ref, sem)
     traces = traces_of(adjoint_ref)
     chosen = lax.broadcasted_iota(jnp.int32, (512, 4 * SLOTS), 0) == sides_ref[...]
     chosen = jnp.where(chosen, 1.0, 0.0).astype(jnp.bfloat16)
@@ -328,32 +359,37 @@
         out_ref[...] = outgoing[direction * SLOTS : (direction + 1) * SLOTS]
 
 
-def ready_kernel(
-    group_ref, metric_ref, synth_ref, back_ref, out_ref, synth_out, back_out, turned, sems
-):
-    copies = []
-    for source, target in ((synth_ref, synth_out), (back_ref, back_out)):
-        for place, part in enumerate((0, 0, 1)):
-            copies.append(
-                pltpu.make_async_copy(
-                    source.at[pl.ds(MODES * part, MODES)],
-                    target.at[pl.ds(MODES * place, MODES)],
-                    sems.at[len(copies)],
-                )
-            )
-            copies[-1].start()
+def stack_table(source, target, sems):
+    copies = [
+        pltpu.make_async_copy(
+            source.at[pl.ds(MODES * part, MODES)],
+            target.at[pl.ds(MODES * place, MODES)],
+            sems.at[place],
+        )
+        for place, part in enumerate((0, 0, 1))
+    ]
+    for copy in copies:
+        copy.start()
+    return copies
+
+
+def ready_kernel(group_ref, metric_ref, synth_ref, out_ref, synth_out, turned, spread, sems):
+    copies = stack_table(synth_ref, synth_out, sems)
     turned[...] = jnp.concatenate(
         [metric_ref[...], jnp.zeros((256 - 4 * QUAD, 128), jnp.float32)], axis=0
     ).T
     own = turned[pl.ds(pl.multiple_of(group_ref[0] * NEAR, NEAR), NEAR), :]
     for index in range(4 * QUAD):
-        out_ref[index] = jnp.broadcast_to(own[:, index : index + 1], (NEAR, 128))
+        spread[index] = jnp.broadcast_to(own[:, index : index + 1], (NEAR, 128))
+    copies.append(pltpu.make_async_copy(spread, out_ref, sems.at[3]))
+    copies[-1].start()
     for copy in copies:
         copy.wait()
 
 
-def jump_kernel(adjoint_ref, index_ref, penalty_ref, *refs):
-    received_refs, out_ref = refs[:4], refs[4]
+def jump_kernel(adjoint_hbm, index_ref, penalty_ref, *refs):
+    received_refs, (out_ref, adjoint_ref, held, sem) = refs[:4], refs[4:]
+    fetch(adjoint_hbm, adjoint_ref, sem)
     traces = traces_of(adjoint_ref)
     received = jnp.concatenate([ref[...] for ref in received_refs], axis=0).T[:TRACE_ROWS]
     index = index_ref[...]
@@ -375,13 +411,24 @@
                 weight = penalty_ref[side * POINTS + step : side * POINTS + step + 1]
                 inner = adjoint_ref[component * QUAD + rim_point(side, step)]
                 jump = outer[far_row : far_row + GROUPS] - inner
-                out_ref[(component * POINTS + step) * 4 + side] = weight * jump
+                held[(component * POINTS + step) * 4 + side] = weight * jump
+    fetch(held, out_ref, sem)
 
 
 BACK_GROUPS = (0, 7, 13, BACK_TILES)
 
 
-def unpack_kernel(group_ref, in_ref, jump_ref, out_ref, advect, sems):
+def unpack_kernel(group_ref, in_ref, jump_hbm, out_ref, advect, jump_ref, sems):
+    arrivals = [
+        pltpu.make_async_copy(
+            jump_hbm.at[pl.ds(28 * component, 28)],
+            jump_ref.at[pl.ds(28 * component, 28)],
+            sems.at[3 + component],
+        )
+        for component in range(3)
+    ]
+    for arrival in arrivals:
+        arrival.start()
     turn = group_ref[0] % 8
     sides_at = {}
     for side in range(4):
@@ -395,6 +442,7 @@
                 row = 8 * tile + lax.rem(k - turn + 8, 8)
                 advect[row] = block[16 * k : 16 * k + 16]
         first = component * QUAD
+        arrivals[component].wait()
         for point, sides in sides_at.items():
             value = advect[first + point]
             for side, step in sides:
@@ -411,7 +459,7 @@
 
 
 def call(kernel, outs, *args, places=None, scratch=(), grant=12):
-    spaces = {"v": pltpu.VMEM, "h": pltpu.HBM, "s": pltpu.SMEM, "a": pl.ANY}
+    spaces = {"v": pltpu.VMEM, "V": pltpu.VMEM, "h": pltpu.HBM, "s": pltpu.SMEM}
     places = places or "v" * len(args)
     many = isinstance(outs, list)
     outs = [
@@ -423,7 +471,7 @@
     ]
     moved = sum(int(np.prod(a.shape)) * a.dtype.itemsize for a in (*args, *outs))
     args = [
-        pltpu.with_memory_space_constraint(a, pltpu.HBM) if p == "h" else a
+        pltpu.with_memory_space_constraint(a, spaces[p]) if p in "hV" else a
         for a, p in zip(args, places)
     ]
     return pl.pallas_call(
@@ -461,49 +509,68 @@
         scratch=[
             pltpu.VMEM((8 * FIELD_TILES, GROUPS, 128), jnp.float32),
             pltpu.VMEM((GROUPS, FIELD_TILES, NEAR, 128), jnp.float32),
-            pltpu.SemaphoreType.DMA((6,)),
-            pltpu.SemaphoreType.DMA((6,)),
+            pltpu.SemaphoreType.DMA((7,)),
+            pltpu.SemaphoreType.DMA((7,)),
         ],
     )
     arrived = lax.all_to_all(packed, "mode", split_axis=0, concat_axis=0, tiled=True)
 
     outgoing = call(
-        send_kernel, [(SLOTS, TRACE_LANES)] * 4, natural, send_sides.reshape(1, 4 * SLOTS)
+        send_kernel,
+        [(SLOTS, TRACE_LANES)] * 4,
+        natural,
+        send_sides.reshape(1, 4 * SLOTS),
+        places="hv",
+        scratch=[
+            pltpu.VMEM((BACK_ROWS, GROUPS, 128), jnp.float32),
+            pltpu.SemaphoreType.DMA(()),
+        ],
     )
     received = [passed_along(block, "elem", o) for block, o in zip(outgoing, OFFSETS)]
-    own_metric, synth, back = call(
+    own_metric, synth = call(
         ready_kernel,
         [
-            pltpu.VMEM((4 * QUAD, NEAR, 128), jnp.float32),
+            pltpu.HBM((4 * QUAD, NEAR, 128), jnp.float32),
             pltpu.VMEM((3 * MODES, 2 * MODES), jnp.bfloat16),
-            pltpu.VMEM((3 * MODES, MODES), jnp.bfloat16),
         ],
         group,
         metric.reshape(4 * QUAD, 128),
         jnp.asarray(synth),
-        jnp.asarray(back),
-        places="svhh",
-        scratch=[pltpu.VMEM((128, 256), jnp.float32), pltpu.SemaphoreType.DMA((6,))],
+        places="svh",
+        scratch=[
+            pltpu.VMEM((128, 256), jnp.float32),
+            pltpu.VMEM((4 * QUAD, NEAR, 128), jnp.float32),
+            pltpu.SemaphoreType.DMA((4,)),
+        ],
     )
     jumps = call(
         jump_kernel,
-        (84, GROUPS, 128),
+        pltpu.HBM((84, GROUPS, 128), jnp.float32),
         natural,
         ext_index,
         penalty.reshape(4 * POINTS, 128),
         *received,
+        places="hvvvvvv",
+        scratch=[
+            pltpu.VMEM((BACK_ROWS, GROUPS, 128), jnp.float32),
+            pltpu.VMEM((84, GROUPS, 128), jnp.float32),
+            pltpu.SemaphoreType.DMA(()),
+        ],
     )
 
     coefficients = call(
         main_kernel,
         (GROUPS, BACK_TILES, NEAR, 128),
         arrived,
-        own_metric.reshape(4, QUAD, NEAR, 128),
+        own_metric,
         synth,
-        back,
+        jnp.asarray(back),
         jumps,
-        places="vvvva",
+        places="Vhvhh",
         scratch=[
+            pltpu.VMEM((4 * QUAD, NEAR, 128), jnp.float32),
+            pltpu.VMEM((3 * MODES, MODES), jnp.bfloat16),
+            pltpu.SemaphoreType.DMA((4,)),
             pltpu.VMEM((64 * FIELD_TILES, 2 * MODES), jnp.float32),
             pltpu.VMEM((8 * ROWS, MODES), jnp.float32),
             pltpu.VMEM((8 * ROWS, MODES), jnp.float32),
@@ -522,10 +589,11 @@
         group,
         returned,
         jumps,
-        places="svv",
+        places="svh",
         scratch=[
             pltpu.VMEM((8 * BACK_TILES, GROUPS, 128), jnp.float32),
-            pltpu.SemaphoreType.DMA((3,)),
+            pltpu.VMEM((84, GROUPS, 128), jnp.float32),
+            pltpu.SemaphoreType.DMA((6,)),
         ],
     )
     return jnp.transpose(out.reshape(3, QUAD, GROUPS, 128), (0, 2, 1, 3))

time: 77.8 us -> 76.4 us (0.982)
  local copies, waits for them, and re-layouts: 6.12 us -> 0.13 us
  Pallas kernels: 14.9 us -> 18.3 us
  waiting for transfers between devices: 19.4 us -> 20.9 us
    unnamed x28 -> x10, local copies, waits for them, and re-layouts: 6.02 us -> 0.04 us
    pallas_call x6, Pallas kernels: 14.9 us -> 18.3 us  [call(): pl.pallas_call(kernel, out_shape=outs if many else outs[0], in_specs=[pl....]
    ppermute x4, waiting for transfers between devices: 0.57 us -> 2.6 us  [passed_along(): lax.ppermute(block, axis, [((i - distance) % count, i) for i in range(cou...]
  transfers between devices with their start and end apart: 5 -> 5, of which waited for: 2 -> 2; matrix products, arithmetic and copies ran while one was open for 0% -> 0% of each run, Pallas kernels for 6% -> 10%
where the time goes in v4:
time: 76.4 us; the launch traced here: 76 us
  blocking collectives  21.9 us (29%)
  waiting for transfers between devices  20.9 us (27%)
  Pallas kernels  18.3 us (24%)
  starting transfers between devices  14.6 us (19%)
    all_to_all x1, blocking collectives, shards(): lax.all_to_all(coefficients, 'mode', split_axis=0, concat_axis=0, tiled=T...  21.9 us
    all_to_all x1, waiting for transfers between devices, shards(): lax.all_to_all(packed, 'mode', split_axis=0, concat_axis=0, tiled=True)  18.3 us
    pallas_call x6, Pallas kernels, call(): pl.pallas_call(kernel, out_shape=outs if many else outs[0], in_specs=[pl....  18.3 us
    ppermute x4, starting transfers between devices, passed_along(): lax.ppermute(block, axis, [((i - distance) % count, i) for i in range(cou...  7.58 us
    all_to_all x1, starting transfers between devices, shards(): lax.all_to_all(packed, 'mode', split_axis=0, concat_axis=0, tiled=True)  7.05 us
    ppermute x4, waiting for transfers between devices, passed_along(): lax.ppermute(block, axis, [((i - distance) % count, i) for i in range(cou...  2.6 us
  transfers between devices with their start and end apart: 5, of which 2 were waited for; matrix products, arithmetic and copies ran while one was open for 0% of the time, Pallas kernels for 10%

profile of v4, /device:TPU:480, one launch (start us, length us, event | category | flops | bytes accessed | tf_op | source)
XLA Modules:
  0.0 76.0 jit_solution(7920402698446124130)
XLA Ops:
  0.0 2.9 %shard_map.82 = f32[16,37,8,128]{3,2,1,0:T(8,128)} custom-call(s32[1]{0:T(128)} %bitcast.group_ref, f32[147,16,128]{2,1,0:T(8,128)} %bitcast.10, f32[147,16,128]{2,1,0:T(8,128)} %bitcast.13), custom_call_target="tpu_custom_call" | custom-call | bytes 4833284 | tf_op jit(solution)/shard_map/pallas_call | solution.py:477
  3.0 0.0 copy-start.3
  3.0 0.0 copy-start.2
  3.0 7.0 %all-to-all-start = ((f32[16,37,8,128]{3,2,1,0:T(8,128)}), f32[16,37,8,128]{3,2,1,0:T(8,128)S(1)}, u32[]{:S(2)}, u32[]{:S(2)}) async-start(f32[16,37,8,128]{3,2,1,0:T(8,128)} %shard_map.82), calls=%async_computation | async-start | bytes 4849664 | tf_op jit(solution)/shard_map/all_to_all | solution.py:516
  10.0 0.0 copy-start.1
  10.1 0.0 copy-start
  10.1 0.1 reshape.26.sides_ref
  10.1 2.5 %shard_map.84 = (f32[32,384]{1,0:T(8,128)}, f32[32,384]{1,0:T(8,128)}, f32[32,384]{1,0:T(8,128)}, f32[32,384]{1,0:T(8,128)}) custom-call(f32[147,16,128]{2,1,0:T(8,128)} %bitcast.11, s32[1,128]{1,0:T(1,128)S(1)} %reshape.26.sides_ref), custom_call_target="tpu_custom_call" | custom-call | bytes 1401344 | tf_op jit(solution)/shard_map/pallas_call | solution.py:477
  12.6 0.0 collective-permute-start
  12.6 1.7 %collective-permute-start.1 = (f32[32,384]{1,0:T(8,128)}, f32[32,384]{1,0:T(8,128)S(1)}, u32[]{:S(2)}, u32[]{:S(2)}) collective-permute-start(f32[32,384]{1,0:T(8,128)} %get-tuple-element.14), channel_id=1, source_target_pairs={{16,0},{32,16},{48,32},{64,48},{80,64},{96,80},{112,96},{128,112},... | collective-permute-start | bytes 147464 | tf_op jit(solution)/shard_map/ppermute | solution.py:490
  14.4 2.6 %collective-permute-start.2 = (f32[32,384]{1,0:T(8,128)}, f32[32,384]{1,0:T(8,128)S(1)}, u32[]{:S(2)}, u32[]{:S(2)}) collective-permute-start(f32[32,384]{1,0:T(8,128)} %get-tuple-element.15), channel_id=1, source_target_pairs={{480,0},{496,16},{0,32},{16,48},{32,64},{48,80},{64,96},{80,112},{... | collective-permute-start | bytes 147464 | tf_op jit(solution)/shard_map/ppermute | solution.py:490
  17.0 3.3 %collective-permute-start.3 = (f32[32,384]{1,0:T(8,128)}, f32[32,384]{1,0:T(8,128)S(1)}, u32[]{:S(2)}, u32[]{:S(2)}) collective-permute-start(f32[32,384]{1,0:T(8,128)} %get-tuple-element.16), channel_id=1, source_target_pairs={{32,0},{48,16},{64,32},{80,48},{96,64},{112,80},{128,96},{144,112}... | collective-permute-start | bytes 147464 | tf_op jit(solution)/shard_map/ppermute | solution.py:490
  20.2 0.0 copy-done.2
  20.3 1.4 %shard_map.83 = (f32[196,8,128]{2,1,0:T(8,128)}, bf16[768,512]{1,0:T(8,128)(2,1)S(1)}) custom-call(s32[1]{0:T(128)} %bitcast.group_ref, f32[196,128]{1,0:T(8,128)S(1)} %reshape.24.metric_ref, bf16[512,512]{1,0:T(8,128)(2,1)} %constant.8.clone.synth_ref), custom_call_target="tpu_custom_call" | custom-call | bytes 2213892 | tf_op jit(solution)/shard_map/pallas_call | solution.py:477
  21.7 0.0 collective-permute-done.refs_0_
  21.7 0.0 collective-permute-done.1.refs_1_
  21.8 0.0 collective-permute-done.2.refs_2_
  21.8 2.6 %collective-permute-done.3.refs_3_ = f32[32,384]{1,0:T(8,128)S(1)} collective-permute-done((f32[32,384]{1,0:T(8,128)}, f32[32,384]{1,0:T(8,128)S(1)}, u32[]{:S(2)}, u32[]{:S(2)}) %collective-permute-start.3) | collective-permute-done | bytes 49184 | tf_op jit(solution)/shard_map/ppermute | solution.py:490
  24.4 0.0 copy-done
  24.4 3.9 %shard_map.85.jump_ref.jump_hbm = f32[84,16,128]{2,1,0:T(8,128)} custom-call(f32[147,16,128]{2,1,0:T(8,128)} %bitcast.12, s32[4,128]{1,0:T(4,128)S(1)} %copy-done, f32[28,128]{1,0:T(8,128)S(1)} %reshape.25.penalty_ref, f32[32,384]{1,0:T(8,128)S(1)} %collective-permute-done.refs_0_, f32[32,384]{1,0:T(8,128)S(1)} %collective-permute-done.1.refs_1_, ...), custom_call_target="tpu_custom_call" | custom-call | bytes 2105344 | tf_op jit(solution)/shard_map/pallas_call | solution.py:477
  28.3 18.3 %all-to-all-done.in_ref = f32[16,37,8,128]{3,2,1,0:T(8,128)S(1)} async-done(((f32[16,37,8,128]{3,2,1,0:T(8,128)}), f32[16,37,8,128]{3,2,1,0:T(8,128)S(1)}, u32[]{:S(2)}, u32[]{:S(2)}) %all-to-all-start) | async-done | bytes 2424864 | tf_op jit(solution)/shard_map/all_to_all | solution.py:516
  46.6 5.4 %shard_map.86 = f32[16,19,8,128]{3,2,1,0:T(8,128)S(1)} custom-call(f32[16,37,8,128]{3,2,1,0:T(8,128)S(1)} %all-to-all-done.in_ref, f32[196,8,128]{2,1,0:T(8,128)} %get-tuple-element.11.metric_hbm, bf16[768,512]{1,0:T(8,128)(2,1)S(1)} %get-tuple-element.12.synth_ref, bf16[512,256]{1,0:T(8,128)(2,1)} %constant.9.clone.back_hbm, ...), custom_call_target="tpu_custom_call" | custom-call | bytes 6209536 | tf_op jit(solution)/shard_map/pallas_call | solution.py:477
  52.0 21.9 %all_to_all.10.in_ref = f32[16,19,8,128]{3,2,1,0:T(8,128)S(1)} all-to-all(f32[16,19,8,128]{3,2,1,0:T(8,128)S(1)} %shard_map.86), channel_id=1, replica_groups=mesh['elem'=32,'mode'=16] {'mode'}, dimensions={0} | all-to-all | bytes 2490368 | tf_op jit(solution)/shard_map/all_to_all | solution.py:585
  73.9 2.1 %shard_map.87 = f32[147,16,128]{2,1,0:T(8,128)} custom-call(s32[1]{0:T(128)} %bitcast.group_ref, f32[16,19,8,128]{3,2,1,0:T(8,128)S(1)} %all_to_all.10.in_ref, f32[84,16,128]{2,1,0:T(8,128)} %shard_map.85.jump_ref.jump_hbm), custom_call_target="tpu_custom_call" | custom-call | bytes 3137540 | tf_op jit(solution)/shard_map/pallas_call | solution.py:477
  (6 shorter events, 0.0 us)
Async XLA Ops:
  3.0 7.1 %copy-start.3 = (s32[1,4,32]{2,1,0:T(4,128)S(1)}, s32[1,4,32]{2,1,0:T(4,128)}, u32[]{:S(2)}) copy-start(s32[1,4,32]{2,1,0:T(4,128)} %param.12) | copy-start | bytes 1540
  3.0 17.3 %copy-start.2 = (f32[4,7,128]{2,0,1:T(4,128)S(1)}, f32[4,7,128]{2,0,1:T(4,128)}, u32[]{:S(2)}) copy-start(f32[4,7,128]{2,0,1:T(4,128)} %param.11) | copy-start | bytes 43012
  3.0 43.6 %all-to-all-start = ((f32[16,37,8,128]{3,2,1,0:T(8,128)}), f32[16,37,8,128]{3,2,1,0:T(8,128)S(1)}, u32[]{:S(2)}, u32[]{:S(2)}) async-start(f32[16,37,8,128]{3,2,1,0:T(8,128)} %shard_map.82), calls=%async_computation | async-start | bytes 4849664 | tf_op jit(solution)/shard_map/all_to_all | solution.py:516
  10.0 10.2 %copy-start.1 = (f32[4,49,128]{2,0,1:T(4,128)S(1)}, f32[4,49,128]{2,0,1:T(4,128)}, u32[]{:S(2)}) copy-start(f32[4,49,128]{2,0,1:T(4,128)} %param.10) | copy-start | bytes 301060
  10.1 14.3 %copy-start = (s32[4,128]{1,0:T(4,128)S(1)}, s32[4,128]{1,0:T(4,128)}, u32[]{:S(2)}) copy-start(s32[4,128]{1,0:T(4,128)} %index_ref.1) | copy-start | bytes 6148
  12.6 9.1 %collective-permute-start = (f32[32,384]{1,0:T(8,128)}, f32[32,384]{1,0:T(8,128)S(1)}, u32[]{:S(2)}, u32[]{:S(2)}) collective-permute-start(f32[32,384]{1,0:T(8,128)} %get-tuple-element.13), channel_id=1, source_target_pairs={{496,0},{0,16},{16,32},{32,48},{48,64},{64,80},{80,96},{96,112},{1... | collective-permute-start | bytes 147464 | tf_op jit(solution)/shard_map/ppermute | solution.py:490
  12.6 9.1 %collective-permute-start.1 = (f32[32,384]{1,0:T(8,128)}, f32[32,384]{1,0:T(8,128)S(1)}, u32[]{:S(2)}, u32[]{:S(2)}) collective-permute-start(f32[32,384]{1,0:T(8,128)} %get-tuple-element.14), channel_id=1, source_target_pairs={{16,0},{32,16},{48,32},{64,48},{80,64},{96,80},{112,96},{128,112},... | collective-permute-start | bytes 147464 | tf_op jit(solution)/shard_map/ppermute | solution.py:490
  14.4 7.4 %collective-permute-start.2 = (f32[32,384]{1,0:T(8,128)}, f32[32,384]{1,0:T(8,128)S(1)}, u32[]{:S(2)}, u32[]{:S(2)}) collective-permute-start(f32[32,384]{1,0:T(8,128)} %get-tuple-element.15), channel_id=1, source_target_pairs={{480,0},{496,16},{0,32},{16,48},{32,64},{48,80},{64,96},{80,112},{... | collective-permute-start | bytes 147464 | tf_op jit(solution)/shard_map/ppermute | solution.py:490
  17.0 7.4 %collective-permute-start.3 = (f32[32,384]{1,0:T(8,128)}, f32[32,384]{1,0:T(8,128)S(1)}, u32[]{:S(2)}, u32[]{:S(2)}) collective-permute-start(f32[32,384]{1,0:T(8,128)} %get-tuple-element.16), channel_id=1, source_target_pairs={{32,0},{48,16},{64,32},{80,48},{96,64},{112,80},{128,96},{144,112}... | collective-permute-start | bytes 147464 | tf_op jit(solution)/shard_map/ppermute | solution.py:490

commit v5 on v4

--- a/solution.py
+++ b/solution.py
@@ -200,8 +200,9 @@
     metric_hbm,
     synth_ref,
     back_hbm,
-    jump_ref,
+    jump_hbm,
     out_ref,
+    jump_out,
     metric_ref,
     back_ref,
     sems,
@@ -214,6 +215,8 @@
     metric_copy = pltpu.make_async_copy(metric_hbm, metric_ref, sems.at[3])
     metric_copy.start()
     back_copies = stack_table(back_hbm, back_ref, sems)
+    jump_copy = pltpu.make_async_copy(jump_hbm, jump_out, sems.at[4])
+    jump_copy.start()
     masks = block_masks()
     matrix = lobatto_matrix(POINTS - 1)
     mirrored = matrix[:, ::-1]
@@ -325,6 +328,7 @@
         following = analyse(chunk + 1) if chunk < 3 else None
         scatter(chunk, held)
         held = following
+    jump_copy.wait()
 
 
 def traces_of(adjoint_ref):
@@ -418,17 +422,7 @@
 BACK_GROUPS = (0, 7, 13, BACK_TILES)
 
 
-def unpack_kernel(group_ref, in_ref, jump_hbm, out_ref, advect, jump_ref, sems):
-    arrivals = [
-        pltpu.make_async_copy(
-            jump_hbm.at[pl.ds(28 * component, 28)],
-            jump_ref.at[pl.ds(28 * component, 28)],
-            sems.at[3 + component],
-        )
-        for component in range(3)
-    ]
-    for arrival in arrivals:
-        arrival.start()
+def unpack_kernel(group_ref, in_ref, jump_ref, out_ref, advect, sems):
     turn = group_ref[0] % 8
     sides_at = {}
     for side in range(4):
@@ -442,7 +436,6 @@
                 row = 8 * tile + lax.rem(k - turn + 8, 8)
                 advect[row] = block[16 * k : 16 * k + 16]
         first = component * QUAD
-        arrivals[component].wait()
         for point, sides in sides_at.items():
             value = advect[first + point]
             for side, step in sides:
@@ -558,9 +551,9 @@
         ],
     )
 
-    coefficients = call(
+    coefficients, jumps = call(
         main_kernel,
-        (GROUPS, BACK_TILES, NEAR, 128),
+        [(GROUPS, BACK_TILES, NEAR, 128), pltpu.VMEM((84, GROUPS, 128), jnp.float32)],
         arrived,
         own_metric,
         synth,
@@ -570,7 +563,7 @@
         scratch=[
             pltpu.VMEM((4 * QUAD, NEAR, 128), jnp.float32),
             pltpu.VMEM((3 * MODES, MODES), jnp.bfloat16),
-            pltpu.SemaphoreType.DMA((4,)),
+            pltpu.SemaphoreType.DMA((5,)),
             pltpu.VMEM((64 * FIELD_TILES, 2 * MODES), jnp.float32),
             pltpu.VMEM((8 * ROWS, MODES), jnp.float32),
             pltpu.VMEM((8 * ROWS, MODES), jnp.float32),
@@ -589,11 +582,10 @@
         group,
         returned,
         jumps,
-        places="svh",
+        places="svv",
         scratch=[
             pltpu.VMEM((8 * BACK_TILES, GROUPS, 128), jnp.float32),
-            pltpu.VMEM((84, GROUPS, 128), jnp.float32),
-            pltpu.SemaphoreType.DMA((6,)),
+            pltpu.SemaphoreType.DMA((3,)),
         ],
     )
     return jnp.transpose(out.reshape(3, QUAD, GROUPS, 128), (0, 2, 1, 3))

time: 76.4 us -> 75.7 us (level)
  no operation moved by 1% of the time
where the time goes in v5:
time: 75.7 us; the launch traced here: 75.3 us
  blocking collectives  21.9 us (29%)
  waiting for transfers between devices  20.9 us (28%)
  Pallas kernels  17.6 us (23%)
  starting transfers between devices  14.6 us (19%)
    all_to_all x1, blocking collectives, shards(): lax.all_to_all(coefficients, 'mode', split_axis=0, concat_axis=0, tiled=T...  21.9 us
    all_to_all x1, waiting for transfers between devices, shards(): lax.all_to_all(packed, 'mode', split_axis=0, concat_axis=0, tiled=True)  18.3 us
    pallas_call x6, Pallas kernels, call(): pl.pallas_call(kernel, out_shape=outs if many else outs[0], in_specs=[pl....  17.6 us
    ppermute x4, starting transfers between devices, passed_along(): lax.ppermute(block, axis, [((i - distance) % count, i) for i in range(cou...  7.58 us
    all_to_all x1, starting transfers between devices, shards(): lax.all_to_all(packed, 'mode', split_axis=0, concat_axis=0, tiled=True)  7.05 us
    ppermute x4, waiting for transfers between devices, passed_along(): lax.ppermute(block, axis, [((i - distance) % count, i) for i in range(cou...  2.59 us
  transfers between devices with their start and end apart: 5, of which 2 were waited for; matrix products, arithmetic and copies ran while one was open for 0% of the time, Pallas kernels for 10%

profile of v5, /device:TPU:480, one launch (start us, length us, event | category | flops | bytes accessed | tf_op | source)
XLA Modules:
  0.0 75.3 jit_solution(2213594566732764874)
XLA Ops:
  0.0 2.9 %shard_map.82 = f32[16,37,8,128]{3,2,1,0:T(8,128)} custom-call(s32[1]{0:T(128)} %bitcast.group_ref, f32[147,16,128]{2,1,0:T(8,128)} %bitcast.10, f32[147,16,128]{2,1,0:T(8,128)} %bitcast.13), custom_call_target="tpu_custom_call" | custom-call | bytes 4833284 | tf_op jit(solution)/shard_map/pallas_call | solution.py:470
  2.9 0.0 copy-start.3
  3.0 0.0 copy-start.2
  3.0 7.0 %all-to-all-start = ((f32[16,37,8,128]{3,2,1,0:T(8,128)}), f32[16,37,8,128]{3,2,1,0:T(8,128)S(1)}, u32[]{:S(2)}, u32[]{:S(2)}) async-start(f32[16,37,8,128]{3,2,1,0:T(8,128)} %shard_map.82), calls=%async_computation | async-start | bytes 4849664 | tf_op jit(solution)/shard_map/all_to_all | solution.py:509
  10.0 0.0 copy-done.3
  10.0 0.0 copy-start.1
  10.0 0.0 copy-start
  10.1 0.1 reshape.26.sides_ref
  10.1 2.5 %shard_map.84 = (f32[32,384]{1,0:T(8,128)}, f32[32,384]{1,0:T(8,128)}, f32[32,384]{1,0:T(8,128)}, f32[32,384]{1,0:T(8,128)}) custom-call(f32[147,16,128]{2,1,0:T(8,128)} %bitcast.11, s32[1,128]{1,0:T(1,128)S(1)} %reshape.26.sides_ref), custom_call_target="tpu_custom_call" | custom-call | bytes 1401344 | tf_op jit(solution)/shard_map/pallas_call | solution.py:470
  12.6 0.0 collective-permute-start
  12.6 1.7 %collective-permute-start.1 = (f32[32,384]{1,0:T(8,128)}, f32[32,384]{1,0:T(8,128)S(1)}, u32[]{:S(2)}, u32[]{:S(2)}) collective-permute-start(f32[32,384]{1,0:T(8,128)} %get-tuple-element.16), channel_id=1, source_target_pairs={{16,0},{32,16},{48,32},{64,48},{80,64},{96,80},{112,96},{128,112},... | collective-permute-start | bytes 147464 | tf_op jit(solution)/shard_map/ppermute | solution.py:483
  14.4 2.6 %collective-permute-start.2 = (f32[32,384]{1,0:T(8,128)}, f32[32,384]{1,0:T(8,128)S(1)}, u32[]{:S(2)}, u32[]{:S(2)}) collective-permute-start(f32[32,384]{1,0:T(8,128)} %get-tuple-element.17), channel_id=1, source_target_pairs={{480,0},{496,16},{0,32},{16,48},{32,64},{48,80},{64,96},{80,112},{... | collective-permute-start | bytes 147464 | tf_op jit(solution)/shard_map/ppermute | solution.py:483
  17.0 3.3 %collective-permute-start.3 = (f32[32,384]{1,0:T(8,128)}, f32[32,384]{1,0:T(8,128)S(1)}, u32[]{:S(2)}, u32[]{:S(2)}) collective-permute-start(f32[32,384]{1,0:T(8,128)} %get-tuple-element.18), channel_id=1, source_target_pairs={{32,0},{48,16},{64,32},{80,48},{96,64},{112,80},{128,96},{144,112}... | collective-permute-start | bytes 147464 | tf_op jit(solution)/shard_map/ppermute | solution.py:483
  20.3 1.4 %shard_map.83 = (f32[196,8,128]{2,1,0:T(8,128)}, bf16[768,512]{1,0:T(8,128)(2,1)S(1)}) custom-call(s32[1]{0:T(128)} %bitcast.group_ref, f32[196,128]{1,0:T(8,128)S(1)} %reshape.24.metric_ref, bf16[512,512]{1,0:T(8,128)(2,1)} %constant.8.clone.synth_ref), custom_call_target="tpu_custom_call" | custom-call | bytes 2213892 | tf_op jit(solution)/shard_map/pallas_call | solution.py:470
  21.7 0.0 collective-permute-done.refs_0_
  21.8 0.0 collective-permute-done.1.refs_1_
  21.8 0.0 collective-permute-done.2.refs_2_
  21.8 2.6 %collective-permute-done.3.refs_3_ = f32[32,384]{1,0:T(8,128)S(1)} collective-permute-done((f32[32,384]{1,0:T(8,128)}, f32[32,384]{1,0:T(8,128)S(1)}, u32[]{:S(2)}, u32[]{:S(2)}) %collective-permute-start.3) | collective-permute-done | bytes 49184 | tf_op jit(solution)/shard_map/ppermute | solution.py:483
  24.4 0.0 copy-done
  24.4 3.9 %shard_map.85.jump_hbm = f32[84,16,128]{2,1,0:T(8,128)} custom-call(f32[147,16,128]{2,1,0:T(8,128)} %bitcast.12, s32[4,128]{1,0:T(4,128)S(1)} %copy-done, f32[28,128]{1,0:T(8,128)S(1)} %reshape.25.penalty_ref, f32[32,384]{1,0:T(8,128)S(1)} %collective-permute-done.refs_0_, f32[32,384]{1,0:T(8,128)S(1)} %collective-permute-done.1.refs_1_, ...), custom_call_target="tpu_custom_call" | custom-call | bytes 2105344 | tf_op jit(solution)/shard_map/pallas_call | solution.py:470
  28.3 18.3 %all-to-all-done.in_ref = f32[16,37,8,128]{3,2,1,0:T(8,128)S(1)} async-done(((f32[16,37,8,128]{3,2,1,0:T(8,128)}), f32[16,37,8,128]{3,2,1,0:T(8,128)S(1)}, u32[]{:S(2)}, u32[]{:S(2)}) %all-to-all-start) | async-done | bytes 2424864 | tf_op jit(solution)/shard_map/all_to_all | solution.py:509
  46.6 5.6 %shard_map.86 = (f32[16,19,8,128]{3,2,1,0:T(8,128)S(1)}, f32[84,16,128]{2,1,0:T(8,128)S(1)}) custom-call(f32[16,37,8,128]{3,2,1,0:T(8,128)S(1)} %all-to-all-done.in_ref, f32[196,8,128]{2,1,0:T(8,128)} %get-tuple-element.13.metric_hbm, bf16[768,512]{1,0:T(8,128)(2,1)S(1)} %get-tuple-element.14.synth_ref, bf16[512,256]{1,0:T(8,128)(2,1)} %constant.9.clone.back_hbm, ...), custom_call_target="tpu_custom_call" | custom-call | bytes 6897664 | tf_op jit(solution)/shard_map/pallas_call | solution.py:470
  52.2 21.9 %all_to_all.10.in_ref = f32[16,19,8,128]{3,2,1,0:T(8,128)S(1)} all-to-all(f32[16,19,8,128]{3,2,1,0:T(8,128)S(1)} %get-tuple-element.19), channel_id=1, replica_groups=mesh['elem'=32,'mode'=16] {'mode'}, dimensions={0} | all-to-all | bytes 2490368 | tf_op jit(solution)/shard_map/all_to_all | solution.py:578
  74.1 1.3 %shard_map.87 = f32[147,16,128]{2,1,0:T(8,128)} custom-call(s32[1]{0:T(128)} %bitcast.group_ref, f32[16,19,8,128]{3,2,1,0:T(8,128)S(1)} %all_to_all.10.in_ref, f32[84,16,128]{2,1,0:T(8,128)S(1)} %get-tuple-element.20.jump_ref), custom_call_target="tpu_custom_call" | custom-call | bytes 3137540 | tf_op jit(solution)/shard_map/pallas_call | solution.py:470
  (6 shorter events, 0.0 us)
Async XLA Ops:
  2.9 7.1 %copy-start.3 = (s32[1,4,32]{2,1,0:T(4,128)S(1)}, s32[1,4,32]{2,1,0:T(4,128)}, u32[]{:S(2)}) copy-start(s32[1,4,32]{2,1,0:T(4,128)} %param.12) | copy-start | bytes 1540
  3.0 17.3 %copy-start.2 = (f32[4,7,128]{2,0,1:T(4,128)S(1)}, f32[4,7,128]{2,0,1:T(4,128)}, u32[]{:S(2)}) copy-start(f32[4,7,128]{2,0,1:T(4,128)} %param.11) | copy-start | bytes 43012
  3.0 43.6 %all-to-all-start = ((f32[16,37,8,128]{3,2,1,0:T(8,128)}), f32[16,37,8,128]{3,2,1,0:T(8,128)S(1)}, u32[]{:S(2)}, u32[]{:S(2)}) async-start(f32[16,37,8,128]{3,2,1,0:T(8,128)} %shard_map.82), calls=%async_computation | async-start | bytes 4849664 | tf_op jit(solution)/shard_map/all_to_all | solution.py:509
  10.0 10.2 %copy-start.1 = (f32[4,49,128]{2,0,1:T(4,128)S(1)}, f32[4,49,128]{2,0,1:T(4,128)}, u32[]{:S(2)}) copy-start(f32[4,49,128]{2,0,1:T(4,128)} %param.10) | copy-start | bytes 301060
  10.0 14.3 %copy-start = (s32[4,128]{1,0:T(4,128)S(1)}, s32[4,128]{1,0:T(4,128)}, u32[]{:S(2)}) copy-start(s32[4,128]{1,0:T(4,128)} %index_ref.1) | copy-start | bytes 6148
  12.6 9.1 %collective-permute-start = (f32[32,384]{1,0:T(8,128)}, f32[32,384]{1,0:T(8,128)S(1)}, u32[]{:S(2)}, u32[]{:S(2)}) collective-permute-start(f32[32,384]{1,0:T(8,128)} %get-tuple-element.15), channel_id=1, source_target_pairs={{496,0},{0,16},{16,32},{32,48},{48,64},{64,80},{80,96},{96,112},{1... | collective-permute-start | bytes 147464 | tf_op jit(solution)/shard_map/ppermute | solution.py:483
  12.6 9.1 %collective-permute-start.1 = (f32[32,384]{1,0:T(8,128)}, f32[32,384]{1,0:T(8,128)S(1)}, u32[]{:S(2)}, u32[]{:S(2)}) collective-permute-start(f32[32,384]{1,0:T(8,128)} %get-tuple-element.16), channel_id=1, source_target_pairs={{16,0},{32,16},{48,32},{64,48},{80,64},{96,80},{112,96},{128,112},... | collective-permute-start | bytes 147464 | tf_op jit(solution)/shard_map/ppermute | solution.py:483
  14.4 7.4 %collective-permute-start.2 = (f32[32,384]{1,0:T(8,128)}, f32[32,384]{1,0:T(8,128)S(1)}, u32[]{:S(2)}, u32[]{:S(2)}) collective-permute-start(f32[32,384]{1,0:T(8,128)} %get-tuple-element.17), channel_id=1, source_target_pairs={{480,0},{496,16},{0,32},{16,48},{32,64},{48,80},{64,96},{80,112},{... | collective-permute-start | bytes 147464 | tf_op jit(solution)/shard_map/ppermute | solution.py:483
  17.0 7.4 %collective-permute-start.3 = (f32[32,384]{1,0:T(8,128)}, f32[32,384]{1,0:T(8,128)S(1)}, u32[]{:S(2)}, u32[]{:S(2)}) collective-permute-start(f32[32,384]{1,0:T(8,128)} %get-tuple-element.18), channel_id=1, source_target_pairs={{32,0},{48,16},{64,32},{80,48},{96,64},{112,80},{128,96},{144,112}... | collective-permute-start | bytes 147464 | tf_op jit(solution)/shard_map/ppermute | solution.py:483

commit v6 on v5

--- a/solution.py
+++ b/solution.py
@@ -137,7 +137,25 @@
 PACK_GROUPS = (0, 6, 12, 18, 24, 30, 34, FIELD_TILES)
 
 
-def pack_kernel(group_ref, adjoint_ref, base_ref, out_ref, fields, packed, in_sems, out_sems):
+def pack_kernel(
+    group_ref,
+    adjoint_ref,
+    base_ref,
+    sides_ref,
+    metric_ref,
+    synth_hbm,
+    out_ref,
+    trace_out,
+    metric_out,
+    synth_out,
+    fields,
+    packed,
+    turned,
+    spread,
+    in_sems,
+    out_sems,
+    table_sems,
+):
     arrivals = []
     sources = ((adjoint_ref, 0, ADJOINT_CUTS), (base_ref, BACK_ROWS, BASE_CUTS))
     for source, offset, cuts in sources:
@@ -150,7 +168,11 @@
                 )
             )
             arrivals[-1].start()
+    tables = stack_table(synth_hbm, synth_out, table_sems)
     fields[ROWS:] = jnp.zeros((8 * FIELD_TILES - ROWS, GROUPS, 128), jnp.float32)
+    spread_metric(group_ref, metric_ref, turned, spread)
+    metric_copy = pltpu.make_async_copy(spread, metric_out, table_sems.at[3])
+    metric_copy.start()
     turn = group_ref[0] % 8
     order = [lax.rem(k - turn + 8, 8) for k in range(8)]
     departures = []
@@ -167,7 +189,9 @@
             )
         )
         departures[-1].start()
-    for departure in departures:
+        if number == 2:
+            outgoing_traces(fields, sides_ref, trace_out)
+    for departure in (*departures, *tables, metric_copy):
         departure.wait()
 
 
@@ -200,12 +224,17 @@
     metric_hbm,
     synth_ref,
     back_hbm,
-    jump_hbm,
-    out_ref,
-    jump_out,
+    trace_hbm,
+    out_hbm,
+    trace_out_0,
+    trace_out_1,
+    trace_out_2,
+    trace_out_3,
     metric_ref,
     back_ref,
+    out_ref,
     sems,
+    out_sems,
     plane,
     first,
     second,
@@ -215,8 +244,12 @@
     metric_copy = pltpu.make_async_copy(metric_hbm, metric_ref, sems.at[3])
     metric_copy.start()
     back_copies = stack_table(back_hbm, back_ref, sems)
-    jump_copy = pltpu.make_async_copy(jump_hbm, jump_out, sems.at[4])
-    jump_copy.start()
+    departures = [
+        pltpu.make_async_copy(trace_hbm.at[pl.ds(SLOTS * d, SLOTS)], target, out_sems.at[d])
+        for d, target in enumerate((trace_out_0, trace_out_1, trace_out_2, trace_out_3))
+    ]
+    for departure in departures:
+        departure.start()
     masks = block_masks()
     matrix = lobatto_matrix(POINTS - 1)
     mirrored = matrix[:, ::-1]
@@ -256,7 +289,7 @@
 
     def combine(half, point):
         east_first, north_first, east_second, north_second = (
-            metric_ref[k * QUAD + point] for k in range(4)
+            metric_ref[point * 4 + k] for k in range(4)
         )
         source = slice(MODES * half, MODES * half + 128)
         span = slice(MODES * half + 128, MODES * half + MODES)
@@ -328,7 +361,13 @@
         following = analyse(chunk + 1) if chunk < 3 else None
         scatter(chunk, held)
         held = following
-    jump_copy.wait()
+        tiles = pl.ds(BACK_CHUNKS[chunk], BACK_CHUNKS[chunk + 1] - BACK_CHUNKS[chunk])
+        departures.append(
+            pltpu.make_async_copy(out_ref.at[:, tiles], out_hbm.at[:, tiles], out_sems.at[4 + chunk])
+        )
+        departures[-1].start()
+    for departure in departures:
+        departure.wait()
 
 
 def traces_of(adjoint_ref):
@@ -350,17 +389,13 @@
     copy.wait()
 
 
-def send_kernel(adjoint_hbm, sides_ref, *refs):
-    out_refs, (adjoint_ref, sem) = refs[:4], refs[4:]
-    fetch(adjoint_hbm, adjoint_ref, sem)
-    traces = traces_of(adjoint_ref)
-    chosen = lax.broadcasted_iota(jnp.int32, (512, 4 * SLOTS), 0) == sides_ref[...]
+def outgoing_traces(adjoint_ref, sides_ref, out_ref):
+    sides = jnp.concatenate([sides_ref[d : d + 1] for d in range(4)], axis=1)
+    chosen = lax.broadcasted_iota(jnp.int32, (512, 4 * SLOTS), 0) == sides
     chosen = jnp.where(chosen, 1.0, 0.0).astype(jnp.bfloat16)
-    outgoing = sum(dot(part, chosen) for part in split_three(traces))
+    outgoing = sum(dot(part, chosen) for part in split_three(traces_of(adjoint_ref)))
     padding = jnp.zeros((TRACE_LANES - TRACE_ROWS, 128), jnp.float32)
-    outgoing = jnp.concatenate([outgoing, padding], axis=0).T
-    for direction, out_ref in enumerate(out_refs):
-        out_ref[...] = outgoing[direction * SLOTS : (direction + 1) * SLOTS]
+    out_ref[...] = jnp.concatenate([outgoing, padding], axis=0).T
 
 
 def stack_table(source, target, sems):
@@ -377,22 +412,18 @@
     return copies
 
 
-def ready_kernel(group_ref, metric_ref, synth_ref, out_ref, synth_out, turned, spread, sems):
-    copies = stack_table(synth_ref, synth_out, sems)
+def spread_metric(group_ref, metric_ref, turned, spread):
+    rows = [metric_ref[point] for point in range(QUAD)]
     turned[...] = jnp.concatenate(
-        [metric_ref[...], jnp.zeros((256 - 4 * QUAD, 128), jnp.float32)], axis=0
+        rows + [jnp.zeros((256 - 4 * QUAD, 128), jnp.float32)], axis=0
     ).T
     own = turned[pl.ds(pl.multiple_of(group_ref[0] * NEAR, NEAR), NEAR), :]
     for index in range(4 * QUAD):
         spread[index] = jnp.broadcast_to(own[:, index : index + 1], (NEAR, 128))
-    copies.append(pltpu.make_async_copy(spread, out_ref, sems.at[3]))
-    copies[-1].start()
-    for copy in copies:
-        copy.wait()
 
 
 def jump_kernel(adjoint_hbm, index_ref, penalty_ref, *refs):
-    received_refs, (out_ref, adjoint_ref, held, sem) = refs[:4], refs[4:]
+    received_refs, (out_ref, adjoint_ref, sem) = refs[:4], refs[4:]
     fetch(adjoint_hbm, adjoint_ref, sem)
     traces = traces_of(adjoint_ref)
     received = jnp.concatenate([ref[...] for ref in received_refs], axis=0).T[:TRACE_ROWS]
@@ -415,8 +446,7 @@
                 weight = penalty_ref[side * POINTS + step : side * POINTS + step + 1]
                 inner = adjoint_ref[component * QUAD + rim_point(side, step)]
                 jump = outer[far_row : far_row + GROUPS] - inner
-                held[(component * POINTS + step) * 4 + side] = weight * jump
-    fetch(held, out_ref, sem)
+                out_ref[(component * POINTS + step) * 4 + side] = weight * jump
 
 
 BACK_GROUPS = (0, 7, 13, BACK_TILES)
@@ -492,90 +522,73 @@
     base = jnp.transpose(base_flow, (0, 2, 1, 3)).reshape(BACK_ROWS, GROUPS, 128)
     group = lax.axis_index("mode").reshape(1)
 
-    packed = call(
+    f32, bf16 = jnp.float32, jnp.bfloat16
+    packed, traces, own_metric, synth = call(
         pack_kernel,
-        pltpu.HBM((GROUPS, FIELD_TILES, NEAR, 128), jnp.float32),
+        [
+            pltpu.HBM((GROUPS, FIELD_TILES, NEAR, 128), f32),
+            (4 * SLOTS, TRACE_LANES),
+            pltpu.HBM((4 * QUAD, NEAR, 128), f32),
+            pltpu.VMEM((3 * MODES, 2 * MODES), bf16),
+        ],
         group,
         natural,
         base,
-        places="shh",
+        send_sides.reshape(4, SLOTS),
+        jnp.transpose(metric, (1, 0, 2)),
+        jnp.asarray(synth),
+        places="shhvvh",
         scratch=[
-            pltpu.VMEM((8 * FIELD_TILES, GROUPS, 128), jnp.float32),
-            pltpu.VMEM((GROUPS, FIELD_TILES, NEAR, 128), jnp.float32),
+            pltpu.VMEM((8 * FIELD_TILES, GROUPS, 128), f32),
+            pltpu.VMEM((GROUPS, FIELD_TILES, NEAR, 128), f32),
+            pltpu.VMEM((128, 256), f32),
+            pltpu.VMEM((4 * QUAD, NEAR, 128), f32),
             pltpu.SemaphoreType.DMA((7,)),
             pltpu.SemaphoreType.DMA((7,)),
-        ],
-    )
-    arrived = lax.all_to_all(packed, "mode", split_axis=0, concat_axis=0, tiled=True)
-
-    outgoing = call(
-        send_kernel,
-        [(SLOTS, TRACE_LANES)] * 4,
-        natural,
-        send_sides.reshape(1, 4 * SLOTS),
-        places="hv",
-        scratch=[
-            pltpu.VMEM((BACK_ROWS, GROUPS, 128), jnp.float32),
-            pltpu.SemaphoreType.DMA(()),
-        ],
-    )
-    received = [passed_along(block, "elem", o) for block, o in zip(outgoing, OFFSETS)]
-    own_metric, synth = call(
-        ready_kernel,
-        [
-            pltpu.HBM((4 * QUAD, NEAR, 128), jnp.float32),
-            pltpu.VMEM((3 * MODES, 2 * MODES), jnp.bfloat16),
-        ],
-        group,
-        metric.reshape(4 * QUAD, 128),
-        jnp.asarray(synth),
-        places="svh",
-        scratch=[
-            pltpu.VMEM((128, 256), jnp.float32),
-            pltpu.VMEM((4 * QUAD, NEAR, 128), jnp.float32),
             pltpu.SemaphoreType.DMA((4,)),
         ],
-    )
+        grant=16,
+    )
+    arrived = lax.all_to_all(packed, "mode", split_axis=0, concat_axis=0, tiled=True)
+    coefficients, *outgoing = call(
+        main_kernel,
+        [pltpu.HBM((GROUPS, BACK_TILES, NEAR, 128), f32)]
+        + [pltpu.HBM((SLOTS, TRACE_LANES), f32)] * 4,
+        arrived,
+        own_metric,
+        synth,
+        jnp.asarray(back),
+        traces,
+        places="Vhvhh",
+        scratch=[
+            pltpu.VMEM((4 * QUAD, NEAR, 128), f32),
+            pltpu.VMEM((3 * MODES, MODES), bf16),
+            pltpu.VMEM((GROUPS, BACK_TILES, NEAR, 128), f32),
+            pltpu.SemaphoreType.DMA((4,)),
+            pltpu.SemaphoreType.DMA((8,)),
+            pltpu.VMEM((64 * FIELD_TILES, 2 * MODES), f32),
+            pltpu.VMEM((8 * ROWS, MODES), f32),
+            pltpu.VMEM((8 * ROWS, MODES), f32),
+            pltpu.VMEM((64 * BACK_TILES, MODES), f32),
+        ]
+        + [
+            pltpu.VMEM((64 * (end - first), 2 * MODES), bf16)
+            for first, end in zip(CHUNKS, CHUNKS[1:])
+        ],
+        grant=28,
+    )
+    returned = lax.all_to_all(coefficients, "mode", split_axis=0, concat_axis=0, tiled=True)
+    received = [passed_along(block, "elem", o) for block, o in zip(outgoing, OFFSETS)]
     jumps = call(
         jump_kernel,
-        pltpu.HBM((84, GROUPS, 128), jnp.float32),
+        (84, GROUPS, 128),
         natural,
         ext_index,
         penalty.reshape(4 * POINTS, 128),
         *received,
         places="hvvvvvv",
-        scratch=[
-            pltpu.VMEM((BACK_ROWS, GROUPS, 128), jnp.float32),
-            pltpu.VMEM((84, GROUPS, 128), jnp.float32),
-            pltpu.SemaphoreType.DMA(()),
-        ],
-    )
-
-    coefficients, jumps = call(
-        main_kernel,
-        [(GROUPS, BACK_TILES, NEAR, 128), pltpu.VMEM((84, GROUPS, 128), jnp.float32)],
-        arrived,
-        own_metric,
-        synth,
-        jnp.asarray(back),
-        jumps,
-        places="Vhvhh",
-        scratch=[
-            pltpu.VMEM((4 * QUAD, NEAR, 128), jnp.float32),
-            pltpu.VMEM((3 * MODES, MODES), jnp.bfloat16),
-            pltpu.SemaphoreType.DMA((5,)),
-            pltpu.VMEM((64 * FIELD_TILES, 2 * MODES), jnp.float32),
-            pltpu.VMEM((8 * ROWS, MODES), jnp.float32),
-            pltpu.VMEM((8 * ROWS, MODES), jnp.float32),
-            pltpu.VMEM((64 * BACK_TILES, MODES), jnp.float32),
-        ]
-        + [
-            pltpu.VMEM((64 * (end - first), 2 * MODES), jnp.bfloat16)
-            for first, end in zip(CHUNKS, CHUNKS[1:])
-        ],
-        grant=28,
-    )
-    returned = lax.all_to_all(coefficients, "mode", split_axis=0, concat_axis=0, tiled=True)
+        scratch=[pltpu.VMEM((BACK_ROWS, GROUPS, 128), f32), pltpu.SemaphoreType.DMA(())],
+    )
     out = call(
         unpack_kernel,
         pltpu.HBM((BACK_ROWS, GROUPS, 128), jnp.float32),
@@ -584,7 +597,7 @@
         jumps,
         places="svv",
         scratch=[
-            pltpu.VMEM((8 * BACK_TILES, GROUPS, 128), jnp.float32),
+            pltpu.VMEM((8 * BACK_TILES, GROUPS, 128), f32),
             pltpu.SemaphoreType.DMA((3,)),
         ],
     )

time: 75.7 us -> 77.2 us (1.020)
  the two profiles are of different devices: /device:TPU:480 before, /device:TPU:2 now
where the time goes in v6:
time: 77.2 us; the launch traced here: 76.8 us
  blocking collectives  38.2 us (49%)
  starting transfers between devices  20 us (26%)
  Pallas kernels  15.2 us (20%)
  waiting for transfers between devices  1.68 us (2%)
  local copies, waits for them, and re-layouts  1.61 us (2%)
    all_to_all x1, blocking collectives, shards(): lax.all_to_all(packed, 'mode', split_axis=0, concat_axis=0, tiled=True)  38.2 us
    pallas_call x4, Pallas kernels, call(): pl.pallas_call(kernel, out_shape=outs if many else outs[0], in_specs=[pl....  15.2 us
    ppermute x4, starting transfers between devices, passed_along(): lax.ppermute(block, axis, [((i - distance) % count, i) for i in range(cou...  14.9 us
    all_to_all x1, starting transfers between devices, shards(): lax.all_to_all(coefficients, 'mode', split_axis=0, concat_axis=0, tiled=T...  5.09 us
    ppermute x4, waiting for transfers between devices, passed_along(): lax.ppermute(block, axis, [((i - distance) % count, i) for i in range(cou...  1.68 us
    unnamed x19, local copies, waits for them, and re-layouts  1.61 us
  transfers between devices with their start and end apart: 5, of which 2 were waited for; matrix products, arithmetic and copies ran while one was open for 0% of the time, Pallas kernels for 4%

profile of v6, /device:TPU:2, one launch (start us, length us, event | category | flops | bytes accessed | tf_op | source)
XLA Modules:
  0.0 76.8 jit_solution(14370514865993429078)
XLA Ops:
  0.0 0.9 %copy-done.1 = f32[4,49,128]{2,0,1:T(4,128)S(1)} copy-done((f32[4,49,128]{2,0,1:T(4,128)S(1)}, f32[4,49,128]{2,0,1:T(4,128)}, u32[]{:S(2)}) %copy-start.1) | copy-done | bytes 100376
  0.9 0.7 copy-done.2
  1.6 3.6 %shard_map.82 = (f32[16,37,8,128]{3,2,1,0:T(8,128)}, f32[128,384]{1,0:T(8,128)S(1)}, f32[196,8,128]{2,1,0:T(8,128)}, bf16[768,512]{1,0:T(8,128)(2,1)S(1)}) custom-call(s32[1]{0:T(128)} %bitcast.group_ref, f32[147,16,128]{2,1,0:T(8,128)} %bitcast.14, f32[147,16,128]{2,1,0:T(8,128)} %bitcast.16, s32[4,32]{1,0:T(4,128)S(1)} %bitcast.13, ...), custom_call_target="tpu_custom_call" | custom-call | bytes 7244292 | tf_op jit(solution)/shard_map/pallas_call | solution.py:500
  5.2 0.0 copy-start
  5.2 38.2 %all_to_all.10.in_ref = f32[16,37,8,128]{3,2,1,0:T(8,128)S(1)} all-to-all(f32[16,37,8,128]{3,2,1,0:T(8,128)} %get-tuple-element.14), channel_id=1, replica_groups=mesh['elem'=32,'mode'=16] {'mode'}, dimensions={0} | all-to-all | bytes 4849664 | tf_op jit(solution)/shard_map/all_to_all | solution.py:552
  43.4 0.0 copy-done
  43.4 7.2 %shard_map.83 = (f32[16,19,8,128]{3,2,1,0:T(8,128)}, f32[32,384]{1,0:T(8,128)}, f32[32,384]{1,0:T(8,128)}, f32[32,384]{1,0:T(8,128)}, f32[32,384]{1,0:T(8,128)}) custom-call(f32[16,37,8,128]{3,2,1,0:T(8,128)S(1)} %all_to_all.10.in_ref, f32[196,8,128]{2,1,0:T(8,128)} %get-tuple-element.15.metric_hbm, bf16[768,512]{1,0:T(8,128)(2,1)S(1)} %get-tuple-element.16.synth_ref, ...), custom_call_target="tpu_custom_call" | custom-call | bytes 5914624 | tf_op jit(solution)/shard_map/pallas_call | solution.py:500
  50.6 0.0 copy-start.4
  50.6 0.0 copy-start.3
  50.7 5.1 %all-to-all-start.1 = ((f32[16,19,8,128]{3,2,1,0:T(8,128)}), f32[16,19,8,128]{3,2,1,0:T(8,128)S(1)}, u32[]{:S(2)}, u32[]{:S(2)}) async-start(f32[16,19,8,128]{3,2,1,0:T(8,128)} %get-tuple-element.18), calls=%async_computation.1 | async-start | bytes 2490368 | tf_op jit(solution)/shard_map/all_to_all | solution.py:580
  55.8 0.0 collective-permute-start
  55.8 7.3 %collective-permute-start.1 = (f32[32,384]{1,0:T(8,128)S(1)}, f32[32,384]{1,0:T(8,128)S(1)}, u32[]{:S(2)}, u32[]{:S(2)}) collective-permute-start(f32[32,384]{1,0:T(8,128)S(1)} %copy-done.7), channel_id=1, source_target_pairs={{16,0},{32,16},{48,32},{64,48},{80,64},{96,80},{112,96},{128,112},... | collective-permute-start | bytes 147464 | tf_op jit(solution)/shard_map/ppermute | solution.py:513
  63.1 0.0 copy-done.6
  63.1 1.9 %collective-permute-start.2 = (f32[32,384]{1,0:T(8,128)S(1)}, f32[32,384]{1,0:T(8,128)S(1)}, u32[]{:S(2)}, u32[]{:S(2)}) collective-permute-start(f32[32,384]{1,0:T(8,128)S(1)} %copy-done.6), channel_id=1, source_target_pairs={{480,0},{496,16},{0,32},{16,48},{32,64},{48,80},{64,96},{80,112},{... | collective-permute-start | bytes 147464 | tf_op jit(solution)/shard_map/ppermute | solution.py:513
  65.1 5.6 %collective-permute-start.3 = (f32[32,384]{1,0:T(8,128)S(1)}, f32[32,384]{1,0:T(8,128)S(1)}, u32[]{:S(2)}, u32[]{:S(2)}) collective-permute-start(f32[32,384]{1,0:T(8,128)S(1)} %copy-done.5), channel_id=1, source_target_pairs={{32,0},{48,16},{64,32},{80,48},{96,64},{112,80},{128,96},{144,112}... | collective-permute-start | bytes 147464 | tf_op jit(solution)/shard_map/ppermute | solution.py:513
  70.7 0.0 copy-done.4
  70.7 0.0 collective-permute-done.refs_0_
  70.7 0.0 collective-permute-done.1.refs_1_
  70.7 0.1 collective-permute-done.2.refs_2_
  70.8 1.6 %collective-permute-done.3.refs_3_ = f32[32,384]{1,0:T(8,128)S(1)} collective-permute-done((f32[32,384]{1,0:T(8,128)S(1)}, f32[32,384]{1,0:T(8,128)S(1)}, u32[]{:S(2)}, u32[]{:S(2)}) %collective-permute-start.3) | collective-permute-done | bytes 49184 | tf_op jit(solution)/shard_map/ppermute | solution.py:513
  72.4 0.0 copy-done.3
  72.4 3.1 %shard_map.84.jump_ref = f32[84,16,128]{2,1,0:T(8,128)S(1)} custom-call(f32[147,16,128]{2,1,0:T(8,128)} %bitcast.15, s32[4,128]{1,0:T(4,128)S(1)} %copy-done.3, f32[28,128]{1,0:T(8,128)S(1)} %reshape.22.penalty_ref, f32[32,384]{1,0:T(8,128)S(1)} %collective-permute-done.refs_0_, f32[32,384]{1,0:T(8,128)S(1)} %collective-permute-done.1.refs_1_, ...), custom_call_target="tpu_custom_call" | custom-call | bytes 2105344 | tf_op jit(solution)/shard_map/pallas_call | solution.py:500
  75.5 0.0 all-to-all-done.1.in_ref
  75.5 1.3 %shard_map.85 = f32[147,16,128]{2,1,0:T(8,128)} custom-call(s32[1]{0:T(128)} %bitcast.group_ref, f32[16,19,8,128]{3,2,1,0:T(8,128)S(1)} %all-to-all-done.1.in_ref, f32[84,16,128]{2,1,0:T(8,128)S(1)} %shard_map.84.jump_ref), custom_call_target="tpu_custom_call" | custom-call | bytes 3137540 | tf_op jit(solution)/shard_map/pallas_call | solution.py:500
  (11 shorter events, 0.0 us)
Async XLA Ops:
  0.0 0.9 %copy-start.1 = (f32[4,49,128]{2,0,1:T(4,128)S(1)}, f32[4,49,128]{2,0,1:T(4,128)}, u32[]{:S(2)}) copy-start(f32[4,49,128]{2,0,1:T(4,128)} %param.10) | copy-start | bytes 301060
  0.9 0.7 copy-start.2
  5.2 38.2 %copy-start = (f32[128,384]{1,0:T(8,128)}, f32[128,384]{1,0:T(8,128)S(1)}, u32[]{:S(2)}) copy-start(f32[128,384]{1,0:T(8,128)S(1)} %get-tuple-element.17.trace_hbm) | copy-start | bytes 589828
  50.6 5.2 %copy-start.8 = (f32[32,384]{1,0:T(8,128)S(1)}, f32[32,384]{1,0:T(8,128)}, u32[]{:S(2)}) copy-start(f32[32,384]{1,0:T(8,128)} %get-tuple-element.19) | copy-start | bytes 147460
  50.6 5.2 %copy-start.7 = (f32[32,384]{1,0:T(8,128)S(1)}, f32[32,384]{1,0:T(8,128)}, u32[]{:S(2)}) copy-start(f32[32,384]{1,0:T(8,128)} %get-tuple-element.20) | copy-start | bytes 147460
  50.6 12.5 %copy-start.6 = (f32[32,384]{1,0:T(8,128)S(1)}, f32[32,384]{1,0:T(8,128)}, u32[]{:S(2)}) copy-start(f32[32,384]{1,0:T(8,128)} %get-tuple-element.21) | copy-start | bytes 147460
  50.6 14.4 %copy-start.5 = (f32[32,384]{1,0:T(8,128)S(1)}, f32[32,384]{1,0:T(8,128)}, u32[]{:S(2)}) copy-start(f32[32,384]{1,0:T(8,128)} %get-tuple-element.22) | copy-start | bytes 147460
  50.6 20.1 %copy-start.4 = (f32[4,7,128]{2,0,1:T(4,128)S(1)}, f32[4,7,128]{2,0,1:T(4,128)}, u32[]{:S(2)}) copy-start(f32[4,7,128]{2,0,1:T(4,128)} %param.11) | copy-start | bytes 43012
  50.6 21.8 %copy-start.3 = (s32[4,128]{1,0:T(4,128)S(1)}, s32[4,128]{1,0:T(4,128)}, u32[]{:S(2)}) copy-start(s32[4,128]{1,0:T(4,128)} %index_ref.1) | copy-start | bytes 6148
  50.7 24.9 %all-to-all-start.1 = ((f32[16,19,8,128]{3,2,1,0:T(8,128)}), f32[16,19,8,128]{3,2,1,0:T(8,128)S(1)}, u32[]{:S(2)}, u32[]{:S(2)}) async-start(f32[16,19,8,128]{3,2,1,0:T(8,128)} %get-tuple-element.18), calls=%async_computation.1 | async-start | bytes 2490368 | tf_op jit(solution)/shard_map/all_to_all | solution.py:580
  55.8 15.0 %collective-permute-start = (f32[32,384]{1,0:T(8,128)S(1)}, f32[32,384]{1,0:T(8,128)S(1)}, u32[]{:S(2)}, u32[]{:S(2)}) collective-permute-start(f32[32,384]{1,0:T(8,128)S(1)} %copy-done.8), channel_id=1, source_target_pairs={{496,0},{0,16},{16,32},{32,48},{48,64},{64,80},{80,96},{96,112},{1... | collective-permute-start | bytes 147464 | tf_op jit(solution)/shard_map/ppermute | solution.py:513
  55.8 14.9 %collective-permute-start.1 = (f32[32,384]{1,0:T(8,128)S(1)}, f32[32,384]{1,0:T(8,128)S(1)}, u32[]{:S(2)}, u32[]{:S(2)}) collective-permute-start(f32[32,384]{1,0:T(8,128)S(1)} %copy-done.7), channel_id=1, source_target_pairs={{16,0},{32,16},{48,32},{64,48},{80,64},{96,80},{112,96},{128,112},... | collective-permute-start | bytes 147464 | tf_op jit(solution)/shard_map/ppermute | solution.py:513
  63.1 7.7 %collective-permute-start.2 = (f32[32,384]{1,0:T(8,128)S(1)}, f32[32,384]{1,0:T(8,128)S(1)}, u32[]{:S(2)}, u32[]{:S(2)}) collective-permute-start(f32[32,384]{1,0:T(8,128)S(1)} %copy-done.6), channel_id=1, source_target_pairs={{480,0},{496,16},{0,32},{16,48},{32,64},{48,80},{64,96},{80,112},{... | collective-permute-start | bytes 147464 | tf_op jit(solution)/shard_map/ppermute | solution.py:513
  65.1 7.3 %collective-permute-start.3 = (f32[32,384]{1,0:T(8,128)S(1)}, f32[32,384]{1,0:T(8,128)S(1)}, u32[]{:S(2)}, u32[]{:S(2)}) collective-permute-start(f32[32,384]{1,0:T(8,128)S(1)} %copy-done.5), channel_id=1, source_target_pairs={{32,0},{48,16},{64,32},{80,48},{96,64},{112,80},{128,96},{144,112}... | collective-permute-start | bytes 147464 | tf_op jit(solution)/shard_map/ppermute | solution.py:513

commit v7 on v6

--- a/solution.py
+++ b/solution.py
@@ -141,8 +141,8 @@
     group_ref,
     adjoint_ref,
     base_ref,
-    sides_ref,
-    metric_ref,
+    sides_hbm,
+    metric_hbm,
     synth_hbm,
     out_ref,
     trace_out,
@@ -152,10 +152,18 @@
     packed,
     turned,
     spread,
+    sides_ref,
+    metric_ref,
     in_sems,
     out_sems,
     table_sems,
 ):
+    small = (
+        pltpu.make_async_copy(metric_hbm, metric_ref, table_sems.at[4]),
+        pltpu.make_async_copy(sides_hbm, sides_ref, table_sems.at[5]),
+    )
+    for copy in small:
+        copy.start()
     arrivals = []
     sources = ((adjoint_ref, 0, ADJOINT_CUTS), (base_ref, BACK_ROWS, BASE_CUTS))
     for source, offset, cuts in sources:
@@ -170,6 +178,8 @@
             arrivals[-1].start()
     tables = stack_table(synth_hbm, synth_out, table_sems)
     fields[ROWS:] = jnp.zeros((8 * FIELD_TILES - ROWS, GROUPS, 128), jnp.float32)
+    for copy in small:
+        copy.wait()
     spread_metric(group_ref, metric_ref, turned, spread)
     metric_copy = pltpu.make_async_copy(spread, metric_out, table_sems.at[3])
     metric_copy.start()
@@ -361,11 +371,15 @@
         following = analyse(chunk + 1) if chunk < 3 else None
         scatter(chunk, held)
         held = following
-        tiles = pl.ds(BACK_CHUNKS[chunk], BACK_CHUNKS[chunk + 1] - BACK_CHUNKS[chunk])
-        departures.append(
-            pltpu.make_async_copy(out_ref.at[:, tiles], out_hbm.at[:, tiles], out_sems.at[4 + chunk])
-        )
-        departures[-1].start()
+        if chunk >= 2:
+            first_tile = 0 if chunk == 2 else BACK_CHUNKS[3]
+            tiles = pl.ds(first_tile, BACK_CHUNKS[chunk + 1] - first_tile)
+            departures.append(
+                pltpu.make_async_copy(
+                    out_ref.at[:, tiles], out_hbm.at[:, tiles], out_sems.at[2 + chunk]
+                )
+            )
+            departures[-1].start()
     for departure in departures:
         departure.wait()
 
@@ -383,12 +397,6 @@
     )
 
 
-def fetch(source, target, sem):
-    copy = pltpu.make_async_copy(source, target, sem)
-    copy.start()
-    copy.wait()
-
-
 def outgoing_traces(adjoint_ref, sides_ref, out_ref):
     sides = jnp.concatenate([sides_ref[d : d + 1] for d in range(4)], axis=1)
     chosen = lax.broadcasted_iota(jnp.int32, (512, 4 * SLOTS), 0) == sides
@@ -424,9 +432,11 @@
 
 def jump_kernel(adjoint_hbm, index_ref, penalty_ref, *refs):
     received_refs, (out_ref, adjoint_ref, sem) = refs[:4], refs[4:]
-    fetch(adjoint_hbm, adjoint_ref, sem)
+    copy = pltpu.make_async_copy(adjoint_hbm, adjoint_ref, sem)
+    copy.start()
+    received = jnp.concatenate([ref[...] for ref in received_refs], axis=0).T[:TRACE_ROWS]
+    copy.wait()
     traces = traces_of(adjoint_ref)
-    received = jnp.concatenate([ref[...] for ref in received_refs], axis=0).T[:TRACE_ROWS]
     index = index_ref[...]
     where_local = lax.broadcasted_iota(jnp.int32, (512, 128), 0)
     where_far = lax.broadcasted_iota(jnp.int32, (128, 128), 0) + 512
@@ -537,15 +547,17 @@
         send_sides.reshape(4, SLOTS),
         jnp.transpose(metric, (1, 0, 2)),
         jnp.asarray(synth),
-        places="shhvvh",
+        places="shhhhh",
         scratch=[
             pltpu.VMEM((8 * FIELD_TILES, GROUPS, 128), f32),
             pltpu.VMEM((GROUPS, FIELD_TILES, NEAR, 128), f32),
             pltpu.VMEM((128, 256), f32),
             pltpu.VMEM((4 * QUAD, NEAR, 128), f32),
+            pltpu.VMEM((4, SLOTS), jnp.int32),
+            pltpu.VMEM((QUAD, 4, 128), f32),
             pltpu.SemaphoreType.DMA((7,)),
             pltpu.SemaphoreType.DMA((7,)),
-            pltpu.SemaphoreType.DMA((4,)),
+            pltpu.SemaphoreType.DMA((6,)),
         ],
         grant=16,
     )
@@ -565,7 +577,7 @@
             pltpu.VMEM((3 * MODES, MODES), bf16),
             pltpu.VMEM((GROUPS, BACK_TILES, NEAR, 128), f32),
             pltpu.SemaphoreType.DMA((4,)),
-            pltpu.SemaphoreType.DMA((8,)),
+            pltpu.SemaphoreType.DMA((6,)),
             pltpu.VMEM((64 * FIELD_TILES, 2 * MODES), f32),
             pltpu.VMEM((8 * ROWS, MODES), f32),
             pltpu.VMEM((8 * ROWS, MODES), f32),

time: 77.2 us -> 76.1 us (0.986)
  local copies, waits for them, and re-layouts: 1.61 us -> 0.04 us
    unnamed x19 -> x15, local copies, waits for them, and re-layouts: 1.61 us -> 0.04 us
where the time goes in v7:
time: 76.1 us; the launch traced here: 75.7 us
  blocking collectives  38.2 us (50%)
  starting transfers between devices  20 us (26%)
  Pallas kernels  15.7 us (21%)
  waiting for transfers between devices  1.68 us (2%)
    all_to_all x1, blocking collectives, shards(): lax.all_to_all(packed, 'mode', split_axis=0, concat_axis=0, tiled=True)  38.2 us
    pallas_call x4, Pallas kernels, call(): pl.pallas_call(kernel, out_shape=outs if many else outs[0], in_specs=[pl....  15.7 us
    ppermute x4, starting transfers between devices, passed_along(): lax.ppermute(block, axis, [((i - distance) % count, i) for i in range(cou...  14.9 us
    all_to_all x1, starting transfers between devices, shards(): lax.all_to_all(coefficients, 'mode', split_axis=0, concat_axis=0, tiled=T...  5.09 us
    ppermute x4, waiting for transfers between devices, passed_along(): lax.ppermute(block, axis, [((i - distance) % count, i) for i in range(cou...  1.68 us
  transfers between devices with their start and end apart: 5, of which 2 were waited for; matrix products, arithmetic and copies ran while one was open for 0% of the time, Pallas kernels for 4%

profile of v7, /device:TPU:2, one launch (start us, length us, event | category | flops | bytes accessed | tf_op | source)
XLA Modules:
  0.0 75.7 jit_solution(11408931871300448216)
XLA Ops:
  0.0 4.2 %shard_map.82 = (f32[16,37,8,128]{3,2,1,0:T(8,128)}, f32[128,384]{1,0:T(8,128)S(1)}, f32[196,8,128]{2,1,0:T(8,128)}, bf16[768,512]{1,0:T(8,128)(2,1)S(1)}) custom-call(s32[1]{0:T(128)} %bitcast.group_ref, f32[147,16,128]{2,1,0:T(8,128)} %bitcast.12, f32[147,16,128]{2,1,0:T(8,128)} %bitcast.14, s32[4,32]{1,0:T(4,128)} %bitcast.16, f32[49,4,128]{2,1,0:T(4,128)} %bitcast.15, ...), custom_call_target="tpu_custom_call" | custom-call | bytes 7244292 | tf_op jit(solution)/shard_map/pallas_call | solution.py:510
  4.2 0.0 copy-start
  4.2 38.2 %all_to_all.10.in_ref = f32[16,37,8,128]{3,2,1,0:T(8,128)S(1)} all-to-all(f32[16,37,8,128]{3,2,1,0:T(8,128)} %get-tuple-element.14), channel_id=1, replica_groups=mesh['elem'=32,'mode'=16] {'mode'}, dimensions={0} | all-to-all | bytes 4849664 | tf_op jit(solution)/shard_map/all_to_all | solution.py:564
  42.4 0.0 copy-done
  42.4 7.2 %shard_map.83 = (f32[16,19,8,128]{3,2,1,0:T(8,128)}, f32[32,384]{1,0:T(8,128)}, f32[32,384]{1,0:T(8,128)}, f32[32,384]{1,0:T(8,128)}, f32[32,384]{1,0:T(8,128)}) custom-call(f32[16,37,8,128]{3,2,1,0:T(8,128)S(1)} %all_to_all.10.in_ref, f32[196,8,128]{2,1,0:T(8,128)} %get-tuple-element.15.metric_hbm, bf16[768,512]{1,0:T(8,128)(2,1)S(1)} %get-tuple-element.16.synth_ref, ...), custom_call_target="tpu_custom_call" | custom-call | bytes 5914624 | tf_op jit(solution)/shard_map/pallas_call | solution.py:510
  49.6 0.0 copy-start.6
  49.6 0.0 copy-start.5
  49.6 0.0 copy-start.4
  49.6 0.0 copy-start.2
  49.6 0.0 copy-start.1
  49.6 5.1 %all-to-all-start.1 = ((f32[16,19,8,128]{3,2,1,0:T(8,128)}), f32[16,19,8,128]{3,2,1,0:T(8,128)S(1)}, u32[]{:S(2)}, u32[]{:S(2)}) async-start(f32[16,19,8,128]{3,2,1,0:T(8,128)} %get-tuple-element.18), calls=%async_computation.1 | async-start | bytes 2490368 | tf_op jit(solution)/shard_map/all_to_all | solution.py:592
  54.7 0.0 collective-permute-start
  54.8 7.3 %collective-permute-start.1 = (f32[32,384]{1,0:T(8,128)S(1)}, f32[32,384]{1,0:T(8,128)S(1)}, u32[]{:S(2)}, u32[]{:S(2)}) collective-permute-start(f32[32,384]{1,0:T(8,128)S(1)} %copy-done.5), channel_id=1, source_target_pairs={{16,0},{32,16},{48,32},{64,48},{80,64},{96,80},{112,96},{128,112},... | collective-permute-start | bytes 147464 | tf_op jit(solution)/shard_map/ppermute | solution.py:523
  62.1 1.9 %collective-permute-start.2 = (f32[32,384]{1,0:T(8,128)S(1)}, f32[32,384]{1,0:T(8,128)S(1)}, u32[]{:S(2)}, u32[]{:S(2)}) collective-permute-start(f32[32,384]{1,0:T(8,128)S(1)} %copy-done.4), channel_id=1, source_target_pairs={{480,0},{496,16},{0,32},{16,48},{32,64},{48,80},{64,96},{80,112},{... | collective-permute-start | bytes 147464 | tf_op jit(solution)/shard_map/ppermute | solution.py:523
  64.0 5.6 %collective-permute-start.3 = (f32[32,384]{1,0:T(8,128)S(1)}, f32[32,384]{1,0:T(8,128)S(1)}, u32[]{:S(2)}, u32[]{:S(2)}) collective-permute-start(f32[32,384]{1,0:T(8,128)S(1)} %copy-done.3), channel_id=1, source_target_pairs={{32,0},{48,16},{64,32},{80,48},{96,64},{112,80},{128,96},{144,112}... | collective-permute-start | bytes 147464 | tf_op jit(solution)/shard_map/ppermute | solution.py:523
  69.7 0.0 copy-done.2
  69.7 0.0 collective-permute-done.refs_0_
  69.7 0.0 collective-permute-done.1.refs_1_
  69.7 0.1 collective-permute-done.2.refs_2_
  69.8 1.6 %collective-permute-done.3.refs_3_ = f32[32,384]{1,0:T(8,128)S(1)} collective-permute-done((f32[32,384]{1,0:T(8,128)S(1)}, f32[32,384]{1,0:T(8,128)S(1)}, u32[]{:S(2)}, u32[]{:S(2)}) %collective-permute-start.3) | collective-permute-done | bytes 49184 | tf_op jit(solution)/shard_map/ppermute | solution.py:523
  71.4 0.0 copy-done.1
  71.4 3.1 %shard_map.84.jump_ref = f32[84,16,128]{2,1,0:T(8,128)S(1)} custom-call(f32[147,16,128]{2,1,0:T(8,128)} %bitcast.13, s32[4,128]{1,0:T(4,128)S(1)} %copy-done.1, f32[28,128]{1,0:T(8,128)S(1)} %reshape.22.penalty_ref, f32[32,384]{1,0:T(8,128)S(1)} %collective-permute-done.refs_0_, f32[32,384]{1,0:T(8,128)S(1)} %collective-permute-done.1.refs_1_, ...), custom_call_target="tpu_custom_call" | custom-call | bytes 2105344 | tf_op jit(solution)/shard_map/pallas_call | solution.py:510
  74.5 0.0 all-to-all-done.1.in_ref
  74.5 1.3 %shard_map.85 = f32[147,16,128]{2,1,0:T(8,128)} custom-call(s32[1]{0:T(128)} %bitcast.group_ref, f32[16,19,8,128]{3,2,1,0:T(8,128)S(1)} %all-to-all-done.1.in_ref, f32[84,16,128]{2,1,0:T(8,128)S(1)} %shard_map.84.jump_ref), custom_call_target="tpu_custom_call" | custom-call | bytes 3137540 | tf_op jit(solution)/shard_map/pallas_call | solution.py:510
  (7 shorter events, 0.0 us)
Async XLA Ops:
  4.2 38.2 %copy-start = (f32[128,384]{1,0:T(8,128)}, f32[128,384]{1,0:T(8,128)S(1)}, u32[]{:S(2)}) copy-start(f32[128,384]{1,0:T(8,128)S(1)} %get-tuple-element.17.trace_hbm) | copy-start | bytes 589828
  49.6 5.2 %copy-start.6 = (f32[32,384]{1,0:T(8,128)S(1)}, f32[32,384]{1,0:T(8,128)}, u32[]{:S(2)}) copy-start(f32[32,384]{1,0:T(8,128)} %get-tuple-element.19) | copy-start | bytes 147460
  49.6 5.2 %copy-start.5 = (f32[32,384]{1,0:T(8,128)S(1)}, f32[32,384]{1,0:T(8,128)}, u32[]{:S(2)}) copy-start(f32[32,384]{1,0:T(8,128)} %get-tuple-element.20) | copy-start | bytes 147460
  49.6 12.5 %copy-start.4 = (f32[32,384]{1,0:T(8,128)S(1)}, f32[32,384]{1,0:T(8,128)}, u32[]{:S(2)}) copy-start(f32[32,384]{1,0:T(8,128)} %get-tuple-element.21) | copy-start | bytes 147460
  49.6 14.4 %copy-start.3 = (f32[32,384]{1,0:T(8,128)S(1)}, f32[32,384]{1,0:T(8,128)}, u32[]{:S(2)}) copy-start(f32[32,384]{1,0:T(8,128)} %get-tuple-element.22) | copy-start | bytes 147460
  49.6 20.1 %copy-start.2 = (f32[4,7,128]{2,0,1:T(4,128)S(1)}, f32[4,7,128]{2,0,1:T(4,128)}, u32[]{:S(2)}) copy-start(f32[4,7,128]{2,0,1:T(4,128)} %param.11) | copy-start | bytes 43012
  49.6 21.8 %copy-start.1 = (s32[4,128]{1,0:T(4,128)S(1)}, s32[4,128]{1,0:T(4,128)}, u32[]{:S(2)}) copy-start(s32[4,128]{1,0:T(4,128)} %index_ref.1) | copy-start | bytes 6148
  49.6 24.8 %all-to-all-start.1 = ((f32[16,19,8,128]{3,2,1,0:T(8,128)}), f32[16,19,8,128]{3,2,1,0:T(8,128)S(1)}, u32[]{:S(2)}, u32[]{:S(2)}) async-start(f32[16,19,8,128]{3,2,1,0:T(8,128)} %get-tuple-element.18), calls=%async_computation.1 | async-start | bytes 2490368 | tf_op jit(solution)/shard_map/all_to_all | solution.py:592
  54.7 15.0 %collective-permute-start = (f32[32,384]{1,0:T(8,128)S(1)}, f32[32,384]{1,0:T(8,128)S(1)}, u32[]{:S(2)}, u32[]{:S(2)}) collective-permute-start(f32[32,384]{1,0:T(8,128)S(1)} %copy-done.6), channel_id=1, source_target_pairs={{496,0},{0,16},{16,32},{32,48},{48,64},{64,80},{80,96},{96,112},{1... | collective-permute-start | bytes 147464 | tf_op jit(solution)/shard_map/ppermute | solution.py:523
  54.8 14.9 %collective-permute-start.1 = (f32[32,384]{1,0:T(8,128)S(1)}, f32[32,384]{1,0:T(8,128)S(1)}, u32[]{:S(2)}, u32[]{:S(2)}) collective-permute-start(f32[32,384]{1,0:T(8,128)S(1)} %copy-done.5), channel_id=1, source_target_pairs={{16,0},{32,16},{48,32},{64,48},{80,64},{96,80},{112,96},{128,112},... | collective-permute-start | bytes 147464 | tf_op jit(solution)/shard_map/ppermute | solution.py:523
  62.1 7.7 %collective-permute-start.2 = (f32[32,384]{1,0:T(8,128)S(1)}, f32[32,384]{1,0:T(8,128)S(1)}, u32[]{:S(2)}, u32[]{:S(2)}) collective-permute-start(f32[32,384]{1,0:T(8,128)S(1)} %copy-done.4), channel_id=1, source_target_pairs={{480,0},{496,16},{0,32},{16,48},{32,64},{48,80},{64,96},{80,112},{... | collective-permute-start | bytes 147464 | tf_op jit(solution)/shard_map/ppermute | solution.py:523
  64.0 7.3 %collective-permute-start.3 = (f32[32,384]{1,0:T(8,128)S(1)}, f32[32,384]{1,0:T(8,128)S(1)}, u32[]{:S(2)}, u32[]{:S(2)}) collective-permute-start(f32[32,384]{1,0:T(8,128)S(1)} %copy-done.3), channel_id=1, source_target_pairs={{32,0},{48,16},{64,32},{80,48},{96,64},{112,80},{128,96},{144,112}... | collective-permute-start | bytes 147464 | tf_op jit(solution)/shard_map/ppermute | solution.py:523
